TPU v7x, 128 devices: a whole 4x4x4 slice. The times are simulated.
128 devices in a mesh: section: 2 (over z_hi), mp: 8 (over y, core), dp: 8 (over x, z_lo).
Axes of the slice: x: 4, y: 4, z: 4 (z_hi: 2, z_lo: 2; z = z_hi * 2 + z_lo), core: 2. Of those that a mesh axis runs over, the one named last changes fastest.
Arguments:
- context: bfloat16 [2, 2048, 6144], P('section', 'dp', 'mp'), may hold values from -6 to 6
- residual: bfloat16 [2, 2048, 8192], P('section', ('dp', 'mp')), may hold values from -6 to 6
- out_weight: bfloat16 [2, 6144, 8192], P('section', 'mp', 'dp'), may hold values from -0.078125 to 0.078125
- ln_gain: float32 [2, 8192], P('section'), may hold values from 0.1 to 1.9
- ln_bias: float32 [2, 8192], P('section'), may hold values from -0.5 to 0.5
- out_grad: bfloat16 [2, 2048, 8192], P('section', ('dp', 'mp')), may hold values from -16 to 16
Outputs:
- normed: bfloat16 [2, 2048, 8192], P('section', ('dp', 'mp'))
- grad_residual: bfloat16 [2, 2048, 8192], P('section', ('dp', 'mp'))
- grad_context: bfloat16 [2, 2048, 6144], P('section', 'dp', 'mp')
- grad_weight: float32 [2, 6144, 8192], P('section', 'mp', 'dp')
- gain_grad: float32 [2, 8192], P('section')
- bias_grad: float32 [2, 8192], P('section')
All inputs are finite; a program needn't handle non-finite values.
Results may differ from a plain program's by a relative error of at most 0.017.
Values may be sent and summed in bfloat16 or wider, within the bound.
No kernel may reach another device: no remote copies, remote signals or barrier semaphores. Data moves between devices by JAX's collectives and lax.ppermute only.
A program may use at most 128 MiB of HBM per device.

v0:
```python
import jax
import jax.numpy as jnp
from jax import lax
from jax.experimental import pallas as pl
from jax.experimental.pallas import tpu as pltpu
from jax.sharding import PartitionSpec as P

EPSILON = 1e-05
WIDTH = 8192
BF = jnp.bfloat16
F32 = jnp.float32


def over_core(value):
    return lax.ppermute(value, "mp", [(i, i ^ 1) for i in range(8)])


def over_y(value, steps):
    return lax.ppermute(value, "mp", [(i, (i + 2 * steps) % 8) for i in range(8)])


def over_dp(value, steps, flip):
    return lax.ppermute(
        value, "dp", [(j, 2 * (((j >> 1) + steps) % 4) + ((j & 1) ^ flip)) for j in range(8)]
    )


def over_section(value, steps):
    return lax.ppermute(value, "section", [(s, (s + steps) % 2) for s in range(2)])


FIRST = ((0, 0), (0, 1), (1, 0), (3, 0))
SECOND = ((2, 0), (1, 1), (3, 1), (2, 1))
ORDER = FIRST + SECOND
NATURAL = tuple((k, f) for k in range(4) for f in range(2))


LANES = 128


def hidden_kernel(first, first_1, first_2, first_3, second, second_1, second_2, second_3, own, turned_1, turned_2, turned_3, gain, hidden, stats, stats_z):
    lane = lax.broadcasted_iota(jnp.int32, (32, LANES), 1)
    kind, place = lane // 32, lane % 8
    plain = jnp.zeros((32, LANES), F32)
    crossed = jnp.zeros((32, LANES), F32)
    turned = (own, turned_1, turned_2, turned_3)
    for index, (k, f) in enumerate(ORDER):
        group = (first, first_1, first_2, first_3) if index < 4 else (second, second_1, second_2, second_3)
        rows = pl.ds(index % 4 * 32, 32)
        attended = sum(part[rows, :].astype(F32) for part in group)
        value = (turned[k][f, 0].astype(F32) + attended).astype(BF)
        hidden[pl.ds(index * 32, 32), :] = value
        value = value.astype(F32)
        weighted = turned[k][f, 1].astype(F32) * gain[...]
        mean = jnp.sum(value, axis=-1, keepdims=True) * (1.0 / 1024)
        shifted = value - mean
        squares = jnp.sum(shifted * shifted, axis=-1, keepdims=True)
        total = jnp.sum(weighted, axis=-1, keepdims=True)
        cross = jnp.sum(weighted * shifted, axis=-1, keepdims=True)
        both = jnp.where(kind == 0, mean, jnp.where(kind == 1, squares, jnp.where(kind == 2, total, cross)))
        plain = jnp.where(place == 2 * k + f, both, plain)
        crossed = jnp.where(place == 2 * k + 1 - f, both, crossed)
    stats[...] = plain
    stats_z[...] = crossed


def norm_kernel(hidden, own, turned_1, turned_2, turned_3, gain, bias, stats, stats_1, stats_2, stats_3, returned, keep, send):
    sets = [stats[0], stats[1]]
    for k, other in ((1, stats_1), (2, stats_2), (3, stats_3)):
        sets += [pltpu.roll(other[f], 2 * k, 1) for f in (0, 1)]
    added = sum(sets)
    mean = added * 0.125
    squares = pltpu.roll(added, LANES - 32, 1)
    total = pltpu.roll(added, LANES - 64, 1) * (1.0 / WIDTH)
    cross = pltpu.roll(added, LANES - 96, 1)
    for part in sets:
        apart = part - mean
        squares = squares + 1024.0 * apart * apart
        cross = cross + apart * pltpu.roll(part, LANES - 64, 1)
    scaled = lax.rsqrt(squares * (1.0 / WIDTH) + EPSILON)
    cross = cross * scaled * (1.0 / WIDTH)
    turned = (own, turned_1, turned_2, turned_3)
    gain_sum = jnp.zeros((1, 1024), F32)
    bias_sum = jnp.zeros((1, 1024), F32)
    for index, (k, f) in enumerate(ORDER):
        at = 8 + 2 * k + f
        rows = pl.ds(index * 32, 32)
        standard = (hidden[rows, :].astype(F32) - mean[:, at : at + 1]) * scaled[:, at : at + 1]
        incoming = turned[k][f, 1].astype(F32)
        weighted = incoming * gain[...]
        result = scaled[:, at : at + 1] * (weighted - total[:, at : at + 1] - standard * cross[:, at : at + 1])
        result = result.astype(BF)
        target = send if f else keep
        returned[rows, :] = result
        target[k, 32:64, :] = result
        target[k, 0:32, :] = (standard * gain[...] + bias[...]).astype(BF)
        gain_sum = gain_sum + jnp.sum(incoming * standard, axis=0, keepdims=True)
        bias_sum = bias_sum + jnp.sum(incoming, axis=0, keepdims=True)
    row = lax.broadcasted_iota(jnp.int32, (16, 1024), 0)
    lines = jnp.zeros((16, 1024), F32)
    for first, rest in ((0, gain_sum), (3, bias_sum)):
        for place in range(3):
            part = rest.astype(BF).astype(F32)
            lines = jnp.where(row == first + place, part, lines)
            rest = rest - part
    lines = lines.astype(BF)
    for k in range(4):
        keep[k, 64:80, :] = lines
        send[k, 64:80, :] = lines


def called(kernel, results, *operands, flops=20_000_000):
    moved = sum(v.size * v.dtype.itemsize for v in (*operands, *results))
    return pl.pallas_call(
        kernel,
        out_shape=results,
        compiler_params=pltpu.CompilerParams(vmem_limit_bytes=32 * 2**20),
        cost_estimate=pl.CostEstimate(flops=flops, bytes_accessed=moved, transcendentals=4096),
    )(*operands)


def after(value, *others):
    return lax.optimization_barrier((value, *others))[0]


def shards(context, residual, out_weight, ln_gain, ln_bias, out_grad):
    mp, dp = lax.axis_index("mp"), lax.axis_index("dp")
    y, core = mp // 2, mp % 2
    x, z = dp // 2, dp % 2

    blocks = context[0].reshape(4, 2, 32, 768)
    by_y = [lax.dynamic_index_in_dim(blocks, (y - k) % 4, 0, False) for k in range(4)]
    theirs = jnp.stack([lax.dynamic_index_in_dim(b, 1 - core, 0, False) for b in by_y])
    mine = jnp.stack([lax.dynamic_index_in_dim(b, core, 0, False) for b in by_y])
    half = jnp.concatenate([mine, over_core(theirs)], axis=-1)

    got = {(0, 0): half}
    got[(1, 0)] = over_dp(half, 1, 0)
    got[(3, 0)] = over_dp(half, 3, 0)
    got[(0, 1)] = over_dp(half, 0, 1)
    got[(2, 0)] = over_dp(half, 2, 0)
    for k in (1, 3):
        got[(k, 1)] = over_dp(got[(0, 1)], k, 0)
    got[(2, 1)] = over_dp(got[(2, 0)], 0, 1)
    weight_own = out_weight[0]
    weight_other = over_core(after(weight_own, half))
    weights = jnp.concatenate([weight_own, weight_other], axis=0)

    columns = jnp.concatenate(
        [
            lax.dynamic_slice_in_dim(ln_gain, dp * 1024, 1024, 1),
            lax.dynamic_slice_in_dim(ln_bias, dp * 1024, 1024, 1),
        ],
        axis=0,
    )
    cotangent = over_section(after(out_grad[0], got[(0, 1)]), -1)
    columns = over_section(after(columns, got[(2, 0)]), -1)
    gain, bias = columns[:1], columns[1:]

    attended, tokens = [], []
    for group in (FIRST, SECOND):
        rows = jnp.stack([got[r] for r in group], axis=1)
        if attended:
            rows = after(rows, attended[0])
        tokens.append(rows)
        part = jnp.dot(rows.reshape(512, 1536), weights, preferred_element_type=F32).astype(BF)
        part = part.reshape(4, 128, 1024)
        attended += [part[0]] + [over_y(part[k], -k) for k in (1, 3, 2)]

    pair = after(jnp.stack([residual[0], cotangent]), attended[0])
    sides = [
        jnp.stack(
            [
                lax.dynamic_slice_in_dim(pair, (2 * ((x + k) % 4) + side) * 1024, 1024, 2)
                for k in range(4)
            ]
        )
        for side in (z, 1 - z)
    ]
    sides = jnp.stack([sides[0], over_dp(sides[1], 0, 1)], axis=1)
    turned = [sides[0]] + [over_dp(sides[k], k, 0) for k in (1, 2, 3)]

    line = jax.ShapeDtypeStruct((32, LANES), F32)
    rows_here = jax.ShapeDtypeStruct((256, 1024), BF)
    hidden, stats, stats_z = called(
        hidden_kernel, (rows_here, line, line), *attended, *turned, gain
    )
    stats = jnp.stack([stats, over_dp(stats_z, 0, 1)])
    stats = [stats] + [over_dp(stats, k, 0) for k in (1, 2, 3)]
    blocks_out = jax.ShapeDtypeStruct((4, 80, 1024), BF)
    returned, keep, send = called(
        norm_kernel, (rows_here, blocks_out, blocks_out), hidden, *turned, gain, bias, *stats
    )

    returned = returned.reshape(8, 32, 1024)
    flowing = [returned] + [over_y(returned, k) for k in (1, 3, 2)]
    flowing = [flowing[0], flowing[1], flowing[3], flowing[2]]

    by_source = jnp.stack([keep, over_dp(send, 0, 1)], axis=1)
    back = [by_source[0]] + [over_dp(by_source[k], -k, 0) for k in (1, 2, 3)]
    back = jnp.stack(back).reshape(8, 80, 1024)
    rows_back = jnp.concatenate(
        [
            lax.dynamic_index_in_dim(back, 2 * ((b // 2 - x) % 4) + ((b % 2) ^ z), 0, False)
            for b in range(8)
        ],
        axis=1,
    )
    upstream = rows_back[32:64]
    normed_rows = over_section(rows_back[:32], 1)
    sums = rows_back[64:70].astype(F32)
    whole = jnp.stack([sums[0] + sums[1] + sums[2], sums[3] + sums[4] + sums[5]])
    whole = whole + over_core(whole)
    whole = whole + sum(over_y(whole, k) for k in (1, 2, 3))
    whole = over_section(whole, 1)

    terms = [
        lax.dot_general(
            rows.reshape(256, 1024), weights, (((1,), (1,)), ((), ())), preferred_element_type=F32
        )
        .astype(BF)
        .reshape(8, 32, 1536)
        for rows in flowing
    ]
    term = {r: jnp.stack([t[place] for t in terms]) for place, r in enumerate(ORDER)}
    crossing = over_dp(term[(2, 1)], 0, 1).astype(F32)
    far = over_dp((term[(2, 0)].astype(F32) + crossing).astype(BF), -2, 0).astype(F32)
    other = term[(0, 1)].astype(F32)
    for k in (1, 3):
        other = other + over_dp(term[(k, 1)], -k, 0).astype(F32)
    context_sum = term[(0, 0)].astype(F32) + far
    for k in (1, 3):
        context_sum = context_sum + over_dp(term[(k, 0)], -k, 0).astype(F32)
    context_sum = context_sum + over_dp(other.astype(BF), 0, 1).astype(F32)
    context_sum = context_sum.astype(BF)
    kept, given = context_sum[..., :768], over_core(context_sum[..., 768:])
    both = jnp.stack([kept, given], axis=1)
    both = jnp.stack(
        [lax.dynamic_index_in_dim(both, (y - b) % 4, 0, False) for b in range(4)]
    )
    grad_context = jnp.where(core == 0, both, both[:, ::-1]).reshape(256, 768)

    spread = jnp.stack(flowing)
    weight_sum = sum(
        lax.dot_general(
            tokens[g], spread[:, 4 * g : 4 * g + 4], (((0, 1, 2), (0, 1, 2)), ((), ())), preferred_element_type=F32
        )
        for g in (0, 1)
    )
    grad_weight = weight_sum[:768] + over_core(weight_sum[768:].astype(BF)).astype(F32)
    return (
        normed_rows[None],
        upstream[None],
        grad_context[None],
        grad_weight[None],
        whole[0][None],
        whole[1][None],
    )


def solution(mesh):
    return jax.shard_map(
        shards,
        mesh=mesh,
        in_specs=(
            P("section", "dp", "mp"),
            P("section", ("dp", "mp"), None),
            P("section", "mp", "dp"),
            P("section", None),
            P("section", None),
            P("section", ("dp", "mp"), None),
        ),
        out_specs=(
            P("section", ("dp", "mp"), None),
            P("section", ("dp", "mp"), None),
            P("section", "dp", "mp"),
            P("section", "mp", "dp"),
            P("section", None),
            P("section", None),
        ),
        check_vma=False,
    )
```

profile of v0, /device:TPU:1, one launch (start us, length us, event | category | flops | bytes accessed | tf_op | source)
XLA Modules:
  0.0 192.9 jit_solution(15178805424906668773)
XLA Ops:
  4.5 1.8 collective-permute-start.1
  6.3 2.5 %collective-permute-start.3 = (bf16[4,32,1536]{2,1,0:T(8,128)(2,1)S(1)}, bf16[4,32,1536]{2,1,0:T(8,128)(2,1)S(1)}, u32[]{:S(2)}, u32[]{:S(2)}) collective-permute-start(bf16[4,32,1536]{2,1,0:T(8,128)(2,1)S(1)} %pad_maximum_fusion.7), channel_id=1, source_target_pairs={{0,6},{1,7},{2,0},{3,1},{4,2},{5,3},{6,4},{7,5},{8,14},{9,15},{10,... | collective-permute-start | bytes 1179656 | tf_op jit(solution)/shard_map/ppermute | solution.py:23
  12.2 3.3 %collective-permute-done.1 = bf16[4,32,1536]{2,1,0:T(8,128)(2,1)S(1)} collective-permute-done((bf16[4,32,1536]{2,1,0:T(8,128)(2,1)S(1)}, bf16[4,32,1536]{2,1,0:T(8,128)(2,1)S(1)}, u32[]{:S(2)}, u32[]{:S(2)}) %collective-permute-start.1) | collective-permute-done | bytes 393248 | tf_op jit(solution)/shard_map/ppermute | solution.py:23
  15.4 2.4 %collective-permute-start.10 = (bf16[4,32,1536]{2,1,0:T(8,128)(2,1)S(1)}, bf16[4,32,1536]{2,1,0:T(8,128)(2,1)S(1)}, u32[]{:S(2)}, u32[]{:S(2)}) collective-permute-start(bf16[4,32,1536]{2,1,0:T(8,128)(2,1)S(1)} %collective-permute-done.1), channel_id=1, source_target_pairs={{0,6},{1,7},{2,0},{3,1},{4,2},{5,3},{6,4},{7,5},{8,14},{9,15},{10,... | collective-permute-start | bytes 1179656 | tf_op jit(solution)/shard_map/ppermute | solution.py:23
  17.8 2.2 %collective-permute-done.8 = bf16[4,32,1536]{2,1,0:T(8,128)(2,1)S(1)} collective-permute-done((bf16[4,32,1536]{2,1,0:T(8,128)(2,1)S(1)}, bf16[4,32,1536]{2,1,0:T(8,128)(2,1)S(1)}, u32[]{:S(2)}, u32[]{:S(2)}) %collective-permute-start.8) | collective-permute-done | bytes 393248 | tf_op jit(solution)/shard_map/ppermute | solution.py:23
  20.0 4.5 %collective-permute-start.11 = (bf16[4,32,1536]{2,1,0:T(8,128)(2,1)S(1)}, bf16[4,32,1536]{2,1,0:T(8,128)(2,1)S(1)}, u32[]{:S(2)}, u32[]{:S(2)}) collective-permute-start(bf16[4,32,1536]{2,1,0:T(8,128)(2,1)S(1)} %collective-permute-done.8), channel_id=1, source_target_pairs={{0,1},{1,0},{2,3},{3,2},{4,5},{5,4},{6,7},{7,6},{8,9},{9,8},{10,11... | collective-permute-start | bytes 1179656 | tf_op jit(solution)/shard_map/ppermute | solution.py:23
  24.5 5.2 %collective-permute-done.2 = bf16[4,32,1536]{2,1,0:T(8,128)(2,1)S(1)} collective-permute-done((bf16[4,32,1536]{2,1,0:T(8,128)(2,1)S(1)}, bf16[4,32,1536]{2,1,0:T(8,128)(2,1)S(1)}, u32[]{:S(2)}, u32[]{:S(2)}) %collective-permute-start.2) | collective-permute-done | bytes 393248 | tf_op jit(solution)/shard_map/ppermute | solution.py:23
  29.7 3.3 %collective-permute-start.15 = (bf16[32,8192]{1,0:T(8,128)(2,1)S(1)}, bf16[32,8192]{1,0:T(8,128)(2,1)S(1)}, u32[]{:S(2)}, u32[]{:S(2)}) collective-permute-start(bf16[32,8192]{1,0:T(8,128)(2,1)S(1)} %bitcast.245), channel_id=1, source_target_pairs={{0,64},{64,0},{1,65},{65,1},{2,66},{66,2},{3,67},{67,3},{4,68},{68... | collective-permute-start | bytes 1572872 | tf_op jit(solution)/shard_map/ppermute | solution.py:29
  33.4 2.1 %collective-permute-done.9 = bf16[4,32,1536]{2,1,0:T(8,128)(2,1)S(1)} collective-permute-done((bf16[4,32,1536]{2,1,0:T(8,128)(2,1)S(1)}, bf16[4,32,1536]{2,1,0:T(8,128)(2,1)S(1)}, u32[]{:S(2)}, u32[]{:S(2)}) %collective-permute-start.9) | collective-permute-done | bytes 393248 | tf_op jit(solution)/shard_map/ppermute | solution.py:23
  35.7 9.8 %collective-permute-done.15 = bf16[32,8192]{1,0:T(8,128)(2,1)S(1)} collective-permute-done((bf16[32,8192]{1,0:T(8,128)(2,1)S(1)}, bf16[32,8192]{1,0:T(8,128)(2,1)S(1)}, u32[]{:S(2)}, u32[]{:S(2)}) %collective-permute-start.15) | collective-permute-done | bytes 524320 | tf_op jit(solution)/shard_map/ppermute | solution.py:29
  47.6 3.0 %collective-permute-start.7 = (bf16[128,1024]{1,0:T(8,128)(2,1)S(1)}, bf16[128,1024]{1,0:T(8,128)(2,1)S(1)}, u32[]{:S(2)}, u32[]{:S(2)}) collective-permute-start(bf16[128,1024]{1,0:T(8,128)(2,1)S(1)} %get-tuple-element.50), channel_id=1, source_target_pairs={{0,32},{8,40},{16,48},{24,56},{32,0},{40,8},{48,16},{56,24},{1,33}... | collective-permute-start | bytes 786440 | tf_op jit(solution)/shard_map/ppermute | solution.py:19
  51.0 2.3 %collective-permute-start.5 = (bf16[128,1024]{1,0:T(8,128)(2,1)S(1)}, bf16[128,1024]{1,0:T(8,128)(2,1)S(1)}, u32[]{:S(2)}, u32[]{:S(2)}) collective-permute-start(bf16[128,1024]{1,0:T(8,128)(2,1)S(1)} %get-tuple-element.52), channel_id=1, source_target_pairs={{0,48},{8,56},{16,0},{24,8},{32,16},{40,24},{48,32},{56,40},{1,49}... | collective-permute-start | bytes 786440 | tf_op jit(solution)/shard_map/ppermute | solution.py:19
  55.7 7.4 %collective-permute-done.16 = bf16[4,2,32,1024]{3,2,1,0:T(8,128)(2,1)S(1)} collective-permute-done((bf16[4,2,32,1024]{3,2,1,0:T(8,128)(2,1)S(1)}, bf16[4,2,32,1024]{3,2,1,0:T(8,128)(2,1)S(1)}, u32[]{:S(2)}, u32[]{:S(2)}) %collective-permute-start.16) | collective-permute-done | bytes 524320 | tf_op jit(solution)/shard_map/ppermute | solution.py:23
  63.1 3.4 %collective-permute-start.20 = (f32[2,1024]{1,0:T(2,128)S(1)}, f32[2,1024]{1,0:T(2,128)S(1)}, u32[]{:S(2)}, u32[]{:S(2)}) collective-permute-start(f32[2,1024]{1,0:T(2,128)S(1)} %pad_maximum_fusion.19), channel_id=1, source_target_pairs={{0,64},{64,0},{1,65},{65,1},{2,66},{66,2},{3,67},{67,3},{4,68},{68... | collective-permute-start | bytes 24584 | tf_op jit(solution)/shard_map/ppermute | solution.py:29
  68.0 2.7 %collective-permute-start.12 = (bf16[128,1024]{1,0:T(8,128)(2,1)S(1)}, bf16[128,1024]{1,0:T(8,128)(2,1)S(1)}, u32[]{:S(2)}, u32[]{:S(2)}) collective-permute-start(bf16[128,1024]{1,0:T(8,128)(2,1)S(1)} %get-tuple-element.48), channel_id=1, source_target_pairs={{0,48},{8,56},{16,0},{24,8},{32,16},{40,24},{48,32},{56,40},{1,49}... | collective-permute-start | bytes 786440 | tf_op jit(solution)/shard_map/ppermute | solution.py:19
  77.5 3.0 %collective-permute-done.18.turned_2 = bf16[2,2,32,1024]{3,2,1,0:T(8,128)(2,1)S(1)} collective-permute-done((bf16[2,2,32,1024]{3,2,1,0:T(8,128)(2,1)S(1)}, bf16[2,2,32,1024]{3,2,1,0:T(8,128)(2,1)S(1)}, u32[]{:S(2)}, u32[]{:S(2)}) %collective-permute-start.18) | collective-permute-done | bytes 262176 | tf_op jit(solution)/shard_map/ppermute | solution.py:23
  82.2 2.3 %collective-permute-done.21 = f32[32,128]{1,0:T(8,128)S(1)} collective-permute-done((f32[32,128]{1,0:T(8,128)S(1)}, f32[32,128]{1,0:T(8,128)S(1)}, u32[]{:S(2)}, u32[]{:S(2)}) %collective-permute-start.21) | collective-permute-done | bytes 16416 | tf_op jit(solution)/shard_map/ppermute | solution.py:23
  87.5 1.8 collective-permute-done.23.stats_2
  93.4 2.4 %convolution_convert_fusion.3 = bf16[256,1536]{1,0:T(8,128)(2,1)S(1)} fusion(bf16[256,1024]{1,0:T(8,128)(2,1)S(1)} %get-tuple-element.27, bf16[768,1024]{1,0:T(8,128)(2,1)} %copy-done.11, bf16[768,1024]{1,0:T(8,128)(2,1)S(1)} %bitcast.241), kind=kOutput, calls=%fused_computation.8 | convolution fusion | flops 811991040 | bytes 4456448 | tf_op jit(solution)/shard_map/dot_general | solution.py:218
  95.9 10.7 %collective-permute-done.30 = bf16[8,32,1024]{2,1,0:T(8,128)(2,1)S(1)} collective-permute-done((bf16[8,32,1024]{2,1,0:T(8,128)(2,1)S(1)}, bf16[8,32,1024]{2,1,0:T(8,128)(2,1)S(1)}, u32[]{:S(2)}, u32[]{:S(2)}) %collective-permute-start.30) | collective-permute-done | bytes 524320 | tf_op jit(solution)/shard_map/ppermute | solution.py:19
  114.7 1.8 fusion.2
  116.6 1.8 bitcast_add_fusion
  121.6 3.1 %collective-permute-start.27 = (bf16[2,80,1024]{2,1,0:T(8,128)(2,1)S(1)}, bf16[2,80,1024]{2,1,0:T(8,128)(2,1)S(1)}, u32[]{:S(2)}, u32[]{:S(2)}) collective-permute-start(bf16[2,80,1024]{2,1,0:T(8,128)(2,1)S(1)} %get-tuple-element.33), channel_id=1, source_target_pairs={{0,4},{1,5},{2,6},{3,7},{4,0},{5,1},{6,2},{7,3},{8,12},{9,13},{10,... | collective-permute-start | bytes 983048 | tf_op jit(solution)/shard_map/ppermute | solution.py:23
  125.9 2.8 %collective-permute-done.28 = bf16[2,80,1024]{2,1,0:T(8,128)(2,1)S(1)} collective-permute-done((bf16[2,80,1024]{2,1,0:T(8,128)(2,1)S(1)}, bf16[2,80,1024]{2,1,0:T(8,128)(2,1)S(1)}, u32[]{:S(2)}, u32[]{:S(2)}) %collective-permute-start.28) | collective-permute-done | bytes 327712 | tf_op jit(solution)/shard_map/ppermute | solution.py:23
  128.7 7.6 %collective-permute-done.27 = bf16[2,80,1024]{2,1,0:T(8,128)(2,1)S(1)} collective-permute-done((bf16[2,80,1024]{2,1,0:T(8,128)(2,1)S(1)}, bf16[2,80,1024]{2,1,0:T(8,128)(2,1)S(1)}, u32[]{:S(2)}, u32[]{:S(2)}) %collective-permute-start.27) | collective-permute-done | bytes 327712 | tf_op jit(solution)/shard_map/ppermute | solution.py:23
  136.9 15.1 %collective-permute-start.42 = (f32[2,8192]{1,0:T(2,128)S(1)}, f32[2,8192]{1,0:T(2,128)S(1)}, u32[]{:S(2)}, u32[]{:S(2)}) collective-permute-start(f32[2,8192]{1,0:T(2,128)S(1)} %pad_maximum_fusion.17), channel_id=1, source_target_pairs={{0,8},{8,0},{16,24},{24,16},{32,40},{40,32},{48,56},{56,48},{1,9},... | collective-permute-start | bytes 196616 | tf_op jit(solution)/shard_map/ppermute | solution.py:15
  156.2 2.1 %collective-permute-start.41 = (bf16[768,1024]{1,0:T(8,128)(2,1)S(1)}, bf16[768,1024]{1,0:T(8,128)(2,1)S(1)}, u32[]{:S(2)}, u32[]{:S(2)}) collective-permute-start(bf16[768,1024]{1,0:T(8,128)(2,1)S(1)} %slice.577), channel_id=1, source_target_pairs={{0,8},{8,0},{16,24},{24,16},{32,40},{40,32},{48,56},{56,48},{1,9},... | collective-permute-start | bytes 4718600 | tf_op jit(solution)/shard_map/ppermute | solution.py:15
  158.3 1.9 collective-permute-done.43
  161.1 6.3 %collective-permute-start.29 = (bf16[32,8192]{1,0:T(8,128)(2,1)S(1)}, bf16[32,8192]{1,0:T(8,128)(2,1)S(1)}, u32[]{:S(2)}, u32[]{:S(2)}) collective-permute-start(bf16[32,8192]{1,0:T(8,128)(2,1)S(1)} %get-tuple-element.29), channel_id=1, source_target_pairs={{0,64},{64,0},{1,65},{65,1},{2,66},{66,2},{3,67},{67,3},{4,68},{68... | collective-permute-start | bytes 1572872 | tf_op jit(solution)/shard_map/ppermute | solution.py:29
  170.3 3.2 %collective-permute-start.40 = (bf16[4,32,768]{2,1,0:T(8,128)(2,1)S(1)}, bf16[4,32,768]{2,1,0:T(8,128)(2,1)S(1)}, u32[]{:S(2)}, u32[]{:S(2)}) collective-permute-start(bf16[4,32,768]{2,1,0:T(8,128)(2,1)S(1)} %get-tuple-element.90), channel_id=1, source_target_pairs={{0,8},{8,0},{16,24},{24,16},{32,40},{40,32},{48,56},{56,48},{1,9},... | collective-permute-start | bytes 589832 | tf_op jit(solution)/shard_map/ppermute | solution.py:15
  173.4 14.7 %collective-permute-done.46 = f32[2,8192]{1,0:T(2,128)S(1)} collective-permute-done((f32[2,8192]{1,0:T(2,128)S(1)}, f32[2,8192]{1,0:T(2,128)S(1)}, u32[]{:S(2)}, u32[]{:S(2)}) %collective-permute-start.46) | collective-permute-done | bytes 65568 | tf_op jit(solution)/shard_map/ppermute | solution.py:29
  189.7 2.4 %fusion = f32[1,768,1024]{2,1,0:T(8,128)} fusion(f32[1536,1024]{1,0:T(8,128)S(1)} %bitcast_add_fusion, bf16[768,1024]{1,0:T(8,128)(2,1)S(1)} %collective-permute-done.41), kind=kLoop, calls=%fused_computation.3 | loop fusion | flops 1572864 | bytes 7864320 | tf_op jit(solution)/shard_map/broadcast_in_dim | solution.py:255
  (156 shorter events, 52.9 us)
Async XLA Ops:
  4.5 11.0 %collective-permute-start.1 = (bf16[4,32,1536]{2,1,0:T(8,128)(2,1)S(1)}, bf16[4,32,1536]{2,1,0:T(8,128)(2,1)S(1)}, u32[]{:S(2)}, u32[]{:S(2)}) collective-permute-start(bf16[4,32,1536]{2,1,0:T(8,128)(2,1)S(1)} %pad_maximum_fusion.7), channel_id=1, source_target_pairs={{0,1},{1,0},{2,3},{3,2},{4,5},{5,4},{6,7},{7,6},{8,9},{9,8},{10,11... | collective-permute-start | bytes 1179656 | tf_op jit(solution)/shard_map/ppermute | solution.py:23
  6.3 11.6 %collective-permute-start.3 = (bf16[4,32,1536]{2,1,0:T(8,128)(2,1)S(1)}, bf16[4,32,1536]{2,1,0:T(8,128)(2,1)S(1)}, u32[]{:S(2)}, u32[]{:S(2)}) collective-permute-start(bf16[4,32,1536]{2,1,0:T(8,128)(2,1)S(1)} %pad_maximum_fusion.7), channel_id=1, source_target_pairs={{0,6},{1,7},{2,0},{3,1},{4,2},{5,3},{6,4},{7,5},{8,14},{9,15},{10,... | collective-permute-start | bytes 1179656 | tf_op jit(solution)/shard_map/ppermute | solution.py:23
  8.7 11.2 %collective-permute-start.8 = (bf16[4,32,1536]{2,1,0:T(8,128)(2,1)S(1)}, bf16[4,32,1536]{2,1,0:T(8,128)(2,1)S(1)}, u32[]{:S(2)}, u32[]{:S(2)}) collective-permute-start(bf16[4,32,1536]{2,1,0:T(8,128)(2,1)S(1)} %pad_maximum_fusion.7), channel_id=1, source_target_pairs={{0,4},{1,5},{2,6},{3,7},{4,0},{5,1},{6,2},{7,3},{8,12},{9,13},{10,... | collective-permute-start | bytes 1179656 | tf_op jit(solution)/shard_map/ppermute | solution.py:23
  9.3 20.4 %collective-permute-start.2 = (bf16[4,32,1536]{2,1,0:T(8,128)(2,1)S(1)}, bf16[4,32,1536]{2,1,0:T(8,128)(2,1)S(1)}, u32[]{:S(2)}, u32[]{:S(2)}) collective-permute-start(bf16[4,32,1536]{2,1,0:T(8,128)(2,1)S(1)} %pad_maximum_fusion.7), channel_id=1, source_target_pairs={{0,2},{1,3},{2,4},{3,5},{4,6},{5,7},{6,0},{7,1},{8,10},{9,11},{10,... | collective-permute-start | bytes 1179656 | tf_op jit(solution)/shard_map/ppermute | solution.py:23
  10.6 35.1 %collective-permute-start.4 = (bf16[768,1024]{1,0:T(8,128)(2,1)}, bf16[768,1024]{1,0:T(8,128)(2,1)S(1)}, u32[]{:S(2)}, u32[]{:S(2)}) collective-permute-start(bf16[768,1024]{1,0:T(8,128)(2,1)} %bitcast.238), channel_id=1, source_target_pairs={{0,8},{8,0},{16,24},{24,16},{32,40},{40,32},{48,56},{56,48},{1,9},... | collective-permute-start | bytes 4718600 | tf_op jit(solution)/shard_map/ppermute | solution.py:15
  15.4 18.0 %collective-permute-start.10 = (bf16[4,32,1536]{2,1,0:T(8,128)(2,1)S(1)}, bf16[4,32,1536]{2,1,0:T(8,128)(2,1)S(1)}, u32[]{:S(2)}, u32[]{:S(2)}) collective-permute-start(bf16[4,32,1536]{2,1,0:T(8,128)(2,1)S(1)} %collective-permute-done.1), channel_id=1, source_target_pairs={{0,6},{1,7},{2,0},{3,1},{4,2},{5,3},{6,4},{7,5},{8,14},{9,15},{10,... | collective-permute-start | bytes 1179656 | tf_op jit(solution)/shard_map/ppermute | solution.py:23
  17.8 17.7 %collective-permute-start.9 = (bf16[4,32,1536]{2,1,0:T(8,128)(2,1)S(1)}, bf16[4,32,1536]{2,1,0:T(8,128)(2,1)S(1)}, u32[]{:S(2)}, u32[]{:S(2)}) collective-permute-start(bf16[4,32,1536]{2,1,0:T(8,128)(2,1)S(1)} %collective-permute-done.1), channel_id=1, source_target_pairs={{0,2},{1,3},{2,4},{3,5},{4,6},{5,7},{6,0},{7,1},{8,10},{9,11},{10,... | collective-permute-start | bytes 1179656 | tf_op jit(solution)/shard_map/ppermute | solution.py:23
  20.0 15.5 %collective-permute-start.11 = (bf16[4,32,1536]{2,1,0:T(8,128)(2,1)S(1)}, bf16[4,32,1536]{2,1,0:T(8,128)(2,1)S(1)}, u32[]{:S(2)}, u32[]{:S(2)}) collective-permute-start(bf16[4,32,1536]{2,1,0:T(8,128)(2,1)S(1)} %collective-permute-done.8), channel_id=1, source_target_pairs={{0,1},{1,0},{2,3},{3,2},{4,5},{5,4},{6,7},{7,6},{8,9},{9,8},{10,11... | collective-permute-start | bytes 1179656 | tf_op jit(solution)/shard_map/ppermute | solution.py:23
  29.7 15.8 %collective-permute-start.15 = (bf16[32,8192]{1,0:T(8,128)(2,1)S(1)}, bf16[32,8192]{1,0:T(8,128)(2,1)S(1)}, u32[]{:S(2)}, u32[]{:S(2)}) collective-permute-start(bf16[32,8192]{1,0:T(8,128)(2,1)S(1)} %bitcast.245), channel_id=1, source_target_pairs={{0,64},{64,0},{1,65},{65,1},{2,66},{66,2},{3,67},{67,3},{4,68},{68... | collective-permute-start | bytes 1572872 | tf_op jit(solution)/shard_map/ppermute | solution.py:29
  47.6 20.4 %collective-permute-start.7 = (bf16[128,1024]{1,0:T(8,128)(2,1)S(1)}, bf16[128,1024]{1,0:T(8,128)(2,1)S(1)}, u32[]{:S(2)}, u32[]{:S(2)}) collective-permute-start(bf16[128,1024]{1,0:T(8,128)(2,1)S(1)} %get-tuple-element.50), channel_id=1, source_target_pairs={{0,32},{8,40},{16,48},{24,56},{32,0},{40,8},{48,16},{56,24},{1,33}... | collective-permute-start | bytes 786440 | tf_op jit(solution)/shard_map/ppermute | solution.py:19
  50.6 20.1 %collective-permute-start.6 = (bf16[128,1024]{1,0:T(8,128)(2,1)S(1)}, bf16[128,1024]{1,0:T(8,128)(2,1)S(1)}, u32[]{:S(2)}, u32[]{:S(2)}) collective-permute-start(bf16[128,1024]{1,0:T(8,128)(2,1)S(1)} %get-tuple-element.51), channel_id=1, source_target_pairs={{0,16},{8,24},{16,32},{24,40},{32,48},{40,56},{48,0},{56,8},{1,17}... | collective-permute-start | bytes 786440 | tf_op jit(solution)/shard_map/ppermute | solution.py:19
  51.0 19.8 %collective-permute-start.5 = (bf16[128,1024]{1,0:T(8,128)(2,1)S(1)}, bf16[128,1024]{1,0:T(8,128)(2,1)S(1)}, u32[]{:S(2)}, u32[]{:S(2)}) collective-permute-start(bf16[128,1024]{1,0:T(8,128)(2,1)S(1)} %get-tuple-element.52), channel_id=1, source_target_pairs={{0,48},{8,56},{16,0},{24,8},{32,16},{40,24},{48,32},{56,40},{1,49}... | collective-permute-start | bytes 786440 | tf_op jit(solution)/shard_map/ppermute | solution.py:19
  53.4 9.7 %collective-permute-start.16 = (bf16[4,2,32,1024]{3,2,1,0:T(8,128)(2,1)S(1)}, bf16[4,2,32,1024]{3,2,1,0:T(8,128)(2,1)S(1)}, u32[]{:S(2)}, u32[]{:S(2)}) collective-permute-start(bf16[4,2,32,1024]{3,2,1,0:T(8,128)(2,1)S(1)} %pad_maximum_fusion.6), channel_id=1, source_target_pairs={{0,1},{1,0},{2,3},{3,2},{4,5},{5,4},{6,7},{7,6},{8,9},{9,8},{10,11... | collective-permute-start | bytes 1572872 | tf_op jit(solution)/shard_map/ppermute | solution.py:23
  55.5 16.7 %collective-permute-start.14 = (bf16[128,1024]{1,0:T(8,128)(2,1)S(1)}, bf16[128,1024]{1,0:T(8,128)(2,1)S(1)}, u32[]{:S(2)}, u32[]{:S(2)}) collective-permute-start(bf16[128,1024]{1,0:T(8,128)(2,1)S(1)} %get-tuple-element.46), channel_id=1, source_target_pairs={{0,32},{8,40},{16,48},{24,56},{32,0},{40,8},{48,16},{56,24},{1,33}... | collective-permute-start | bytes 786440 | tf_op jit(solution)/shard_map/ppermute | solution.py:19
  72.2 8.3 %collective-permute-start.18 = (bf16[2,2,32,1024]{3,2,1,0:T(8,128)(2,1)S(1)}, bf16[2,2,32,1024]{3,2,1,0:T(8,128)(2,1)S(1)}, u32[]{:S(2)}, u32[]{:S(2)}) collective-permute-start(bf16[2,2,32,1024]{3,2,1,0:T(8,128)(2,1)S(1)} %get-tuple-element.37), channel_id=1, source_target_pairs={{0,4},{1,5},{2,6},{3,7},{4,0},{5,1},{6,2},{7,3},{8,12},{9,13},{10,... | collective-permute-start | bytes 786440 | tf_op jit(solution)/shard_map/ppermute | solution.py:23
  91.3 17.5 %collective-permute-start.32 = (bf16[8,32,1024]{2,1,0:T(8,128)(2,1)S(1)}, bf16[8,32,1024]{2,1,0:T(8,128)(2,1)S(1)}, u32[]{:S(2)}, u32[]{:S(2)}) collective-permute-start(bf16[8,32,1024]{2,1,0:T(8,128)(2,1)S(1)} %bitcast.196), channel_id=1, source_target_pairs={{0,48},{8,56},{16,0},{24,8},{32,16},{40,24},{48,32},{56,40},{1,49}... | collective-permute-start | bytes 1572872 | tf_op jit(solution)/shard_map/ppermute | solution.py:19
  91.4 16.3 %collective-permute-start.31 = (bf16[8,32,1024]{2,1,0:T(8,128)(2,1)S(1)}, bf16[8,32,1024]{2,1,0:T(8,128)(2,1)S(1)}, u32[]{:S(2)}, u32[]{:S(2)}) collective-permute-start(bf16[8,32,1024]{2,1,0:T(8,128)(2,1)S(1)} %bitcast.197), channel_id=1, source_target_pairs={{0,32},{8,40},{16,48},{24,56},{32,0},{40,8},{48,16},{56,24},{1,33}... | collective-permute-start | bytes 1572872 | tf_op jit(solution)/shard_map/ppermute | solution.py:19
  91.8 14.8 %collective-permute-start.30 = (bf16[8,32,1024]{2,1,0:T(8,128)(2,1)S(1)}, bf16[8,32,1024]{2,1,0:T(8,128)(2,1)S(1)}, u32[]{:S(2)}, u32[]{:S(2)}) collective-permute-start(bf16[8,32,1024]{2,1,0:T(8,128)(2,1)S(1)} %bitcast.198), channel_id=1, source_target_pairs={{0,16},{8,24},{16,32},{24,40},{32,48},{40,56},{48,0},{56,8},{1,17}... | collective-permute-start | bytes 1572872 | tf_op jit(solution)/shard_map/ppermute | solution.py:19
  92.8 25.9 %collective-permute-start.25 = (bf16[4,80,1024]{2,1,0:T(8,128)(2,1)S(1)}, bf16[4,80,1024]{2,1,0:T(8,128)(2,1)S(1)}, u32[]{:S(2)}, u32[]{:S(2)}) collective-permute-start(bf16[4,80,1024]{2,1,0:T(8,128)(2,1)S(1)} %get-tuple-element.26), channel_id=1, source_target_pairs={{0,1},{1,0},{2,3},{3,2},{4,5},{5,4},{6,7},{7,6},{8,9},{9,8},{10,11... | collective-permute-start | bytes 1966088 | tf_op jit(solution)/shard_map/ppermute | solution.py:23
  109.9 42.1 %collective-permute-start.33 = (bf16[4,32,1536]{2,1,0:T(8,128)(2,1)S(1)}, bf16[4,32,1536]{2,1,0:T(8,128)(2,1)S(1)}, u32[]{:S(2)}, u32[]{:S(2)}) collective-permute-start(bf16[4,32,1536]{2,1,0:T(8,128)(2,1)S(1)} %pad_maximum_fusion.8), channel_id=1, source_target_pairs={{0,1},{1,0},{2,3},{3,2},{4,5},{5,4},{6,7},{7,6},{8,9},{9,8},{10,11... | collective-permute-start | bytes 1179656 | tf_op jit(solution)/shard_map/ppermute | solution.py:23
  110.7 50.4 %collective-permute-start.35 = (bf16[4,32,1536]{2,1,0:T(8,128)(2,1)S(1)}, bf16[4,32,1536]{2,1,0:T(8,128)(2,1)S(1)}, u32[]{:S(2)}, u32[]{:S(2)}) collective-permute-start(bf16[4,32,1536]{2,1,0:T(8,128)(2,1)S(1)} %pad_maximum_fusion.9), channel_id=1, source_target_pairs={{0,6},{1,7},{2,0},{3,1},{4,2},{5,3},{6,4},{7,5},{8,14},{9,15},{10,... | collective-permute-start | bytes 1179656 | tf_op jit(solution)/shard_map/ppermute | solution.py:23
  111.5 10.1 %collective-permute-start.37 = (bf16[4,32,1536]{2,1,0:T(8,128)(2,1)S(1)}, bf16[4,32,1536]{2,1,0:T(8,128)(2,1)S(1)}, u32[]{:S(2)}, u32[]{:S(2)}) collective-permute-start(bf16[4,32,1536]{2,1,0:T(8,128)(2,1)S(1)} %pad_maximum_fusion.11), channel_id=1, source_target_pairs={{0,6},{1,7},{2,0},{3,1},{4,2},{5,3},{6,4},{7,5},{8,14},{9,15},{10,... | collective-permute-start | bytes 1179656 | tf_op jit(solution)/shard_map/ppermute | solution.py:23
  111.8 9.7 %collective-permute-start.38 = (bf16[4,32,1536]{2,1,0:T(8,128)(2,1)S(1)}, bf16[4,32,1536]{2,1,0:T(8,128)(2,1)S(1)}, u32[]{:S(2)}, u32[]{:S(2)}) collective-permute-start(bf16[4,32,1536]{2,1,0:T(8,128)(2,1)S(1)} %pad_maximum_fusion.12), channel_id=1, source_target_pairs={{0,2},{1,3},{2,4},{3,5},{4,6},{5,7},{6,0},{7,1},{8,10},{9,11},{10,... | collective-permute-start | bytes 1179656 | tf_op jit(solution)/shard_map/ppermute | solution.py:23
  121.6 14.7 %collective-permute-start.27 = (bf16[2,80,1024]{2,1,0:T(8,128)(2,1)S(1)}, bf16[2,80,1024]{2,1,0:T(8,128)(2,1)S(1)}, u32[]{:S(2)}, u32[]{:S(2)}) collective-permute-start(bf16[2,80,1024]{2,1,0:T(8,128)(2,1)S(1)} %get-tuple-element.33), channel_id=1, source_target_pairs={{0,4},{1,5},{2,6},{3,7},{4,0},{5,1},{6,2},{7,3},{8,12},{9,13},{10,... | collective-permute-start | bytes 983048 | tf_op jit(solution)/shard_map/ppermute | solution.py:23
  125.4 41.9 %collective-permute-start.36 = (bf16[4,32,1536]{2,1,0:T(8,128)(2,1)S(1)}, bf16[4,32,1536]{2,1,0:T(8,128)(2,1)S(1)}, u32[]{:S(2)}, u32[]{:S(2)}) collective-permute-start(bf16[4,32,1536]{2,1,0:T(8,128)(2,1)S(1)} %pad_maximum_fusion.10), channel_id=1, source_target_pairs={{0,2},{1,3},{2,4},{3,5},{4,6},{5,7},{6,0},{7,1},{8,10},{9,11},{10,... | collective-permute-start | bytes 1179656 | tf_op jit(solution)/shard_map/ppermute | solution.py:23
  136.9 16.0 %collective-permute-start.42 = (f32[2,8192]{1,0:T(2,128)S(1)}, f32[2,8192]{1,0:T(2,128)S(1)}, u32[]{:S(2)}, u32[]{:S(2)}) collective-permute-start(f32[2,8192]{1,0:T(2,128)S(1)} %pad_maximum_fusion.17), channel_id=1, source_target_pairs={{0,8},{8,0},{16,24},{24,16},{32,40},{40,32},{48,56},{56,48},{1,9},... | collective-permute-start | bytes 196616 | tf_op jit(solution)/shard_map/ppermute | solution.py:15
  156.2 33.5 %collective-permute-start.41 = (bf16[768,1024]{1,0:T(8,128)(2,1)S(1)}, bf16[768,1024]{1,0:T(8,128)(2,1)S(1)}, u32[]{:S(2)}, u32[]{:S(2)}) collective-permute-start(bf16[768,1024]{1,0:T(8,128)(2,1)S(1)} %slice.577), channel_id=1, source_target_pairs={{0,8},{8,0},{16,24},{24,16},{32,40},{40,32},{48,56},{56,48},{1,9},... | collective-permute-start | bytes 4718600 | tf_op jit(solution)/shard_map/ppermute | solution.py:15
  158.3 10.0 %collective-permute-start.34 = (bf16[4,32,1536]{2,1,0:T(8,128)(2,1)S(1)}, bf16[4,32,1536]{2,1,0:T(8,128)(2,1)S(1)}, u32[]{:S(2)}, u32[]{:S(2)}) collective-permute-start(bf16[4,32,1536]{2,1,0:T(8,128)(2,1)S(1)} %add_convert_fusion.2), channel_id=1, source_target_pairs={{0,4},{1,5},{2,6},{3,7},{4,0},{5,1},{6,2},{7,3},{8,12},{9,13},{10,... | collective-permute-start | bytes 1179656 | tf_op jit(solution)/shard_map/ppermute | solution.py:23
  160.2 9.8 %collective-permute-start.39 = (bf16[4,32,1536]{2,1,0:T(8,128)(2,1)S(1)}, bf16[4,32,1536]{2,1,0:T(8,128)(2,1)S(1)}, u32[]{:S(2)}, u32[]{:S(2)}) collective-permute-start(bf16[4,32,1536]{2,1,0:T(8,128)(2,1)S(1)} %add_convert_fusion.1), channel_id=1, source_target_pairs={{0,1},{1,0},{2,3},{3,2},{4,5},{5,4},{6,7},{7,6},{8,9},{9,8},{10,11... | collective-permute-start | bytes 1179656 | tf_op jit(solution)/shard_map/ppermute | solution.py:23
  161.1 27.7 %collective-permute-start.29 = (bf16[32,8192]{1,0:T(8,128)(2,1)S(1)}, bf16[32,8192]{1,0:T(8,128)(2,1)S(1)}, u32[]{:S(2)}, u32[]{:S(2)}) collective-permute-start(bf16[32,8192]{1,0:T(8,128)(2,1)S(1)} %get-tuple-element.29), channel_id=1, source_target_pairs={{0,64},{64,0},{1,65},{65,1},{2,66},{66,2},{3,67},{67,3},{4,68},{68... | collective-permute-start | bytes 1572872 | tf_op jit(solution)/shard_map/ppermute | solution.py:29
  167.3 20.7 %collective-permute-start.46 = (f32[2,8192]{1,0:T(2,128)S(1)}, f32[2,8192]{1,0:T(2,128)S(1)}, u32[]{:S(2)}, u32[]{:S(2)}) collective-permute-start(f32[2,8192]{1,0:T(2,128)S(1)} %add_add_fusion), channel_id=1, source_target_pairs={{0,64},{64,0},{1,65},{65,1},{2,66},{66,2},{3,67},{67,3},{4,68},{68... | collective-permute-start | bytes 196616 | tf_op jit(solution)/shard_map/ppermute | solution.py:29
  170.3 18.5 %collective-permute-start.40 = (bf16[4,32,768]{2,1,0:T(8,128)(2,1)S(1)}, bf16[4,32,768]{2,1,0:T(8,128)(2,1)S(1)}, u32[]{:S(2)}, u32[]{:S(2)}) collective-permute-start(bf16[4,32,768]{2,1,0:T(8,128)(2,1)S(1)} %get-tuple-element.90), channel_id=1, source_target_pairs={{0,8},{8,0},{16,24},{24,16},{32,40},{40,32},{48,56},{56,48},{1,9},... | collective-permute-start | bytes 589832 | tf_op jit(solution)/shard_map/ppermute | solution.py:15
  (29 other events, 198.9 us)
where the time goes:
time: 193 us
  waiting for transfers between devices  88.1 us (46%)
  starting transfers between devices  77 us (40%)
  matrix products  12.7 us (7%)
  local copies, waits for them, and re-layouts  6.99 us (4%)
  other arithmetic  5.09 us (3%)
    ppermute x26, waiting for transfers between devices, over_dp(): lax.ppermute(value, 'dp', [(j, 2 * (((j >> 1) + steps) % 4) + (j & 1 ^ fl...  46.7 us
    ppermute x26, starting transfers between devices, over_dp(): lax.ppermute(value, 'dp', [(j, 2 * (((j >> 1) + steps) % 4) + (j & 1 ^ fl...  29 us
    ppermute x4, waiting for transfers between devices, over_section(): lax.ppermute(value, 'section', [(s, (s + steps) % 2) for s in range(2)])  25.9 us
    ppermute x5, starting transfers between devices, over_core(): return lax.ppermute(value, 'mp', [(i, i ^ 1) for i in range(8)])  23.4 us
    ppermute x12, waiting for transfers between devices, over_y(): lax.ppermute(value, 'mp', [(i, (i + 2 * steps) % 8) for i in range(8)])  13.6 us
    ppermute x4, starting transfers between devices, over_section(): lax.ppermute(value, 'section', [(s, (s + steps) % 2) for s in range(2)])  13 us
    ppermute x12, starting transfers between devices, over_y(): lax.ppermute(value, 'mp', [(i, (i + 2 * steps) % 8) for i in range(8)])  11.6 us
    dot_general x4, matrix products, shards(): lax.dot_general(rows.reshape(256, 1024), weights, (((1,), (1,)), ((), ())...  5.46 us
  transfers between devices with their start and end apart: 47, of which 28 were waited for; matrix products, arithmetic and copies ran while one was open for 9% of the time, Pallas kernels for 0%

commit v1 on v0

--- a/solution.py
+++ b/solution.py
@@ -27,6 +27,11 @@
 
 def over_section(value, steps):
     return lax.ppermute(value, "section", [(s, (s + steps) % 2) for s in range(2)])
+
+
+def over_both(value, steps, flip):
+    pairs = [(i, (i + 8 * steps) % 16 ^ flip) for i in range(16)]
+    return lax.ppermute(value, ("section", "dp"), pairs)
 
 
 FIRST = ((0, 0), (0, 1), (1, 0), (3, 0))
@@ -64,7 +69,7 @@
     stats_z[...] = crossed
 
 
-def norm_kernel(hidden, own, turned_1, turned_2, turned_3, gain, bias, stats, stats_1, stats_2, stats_3, returned, keep, send):
+def norm_kernel(hidden, own, turned_1, turned_2, turned_3, gain, bias, stats, stats_1, stats_2, stats_3, returned, out, out_1, out_2, out_3):
     sets = [stats[0], stats[1]]
     for k, other in ((1, stats_1), (2, stats_2), (3, stats_3)):
         sets += [pltpu.roll(other[f], 2 * k, 1) for f in (0, 1)]
@@ -80,6 +85,7 @@
     scaled = lax.rsqrt(squares * (1.0 / WIDTH) + EPSILON)
     cross = cross * scaled * (1.0 / WIDTH)
     turned = (own, turned_1, turned_2, turned_3)
+    outs = (out, out_1, out_2, out_3)
     gain_sum = jnp.zeros((1, 1024), F32)
     bias_sum = jnp.zeros((1, 1024), F32)
     for index, (k, f) in enumerate(ORDER):
@@ -90,10 +96,10 @@
         weighted = incoming * gain[...]
         result = scaled[:, at : at + 1] * (weighted - total[:, at : at + 1] - standard * cross[:, at : at + 1])
         result = result.astype(BF)
-        target = send if f else keep
+        target = outs[k]
         returned[rows, :] = result
-        target[k, 32:64, :] = result
-        target[k, 0:32, :] = (standard * gain[...] + bias[...]).astype(BF)
+        target[f, 48:80, :] = result
+        target[f, 0:32, :] = (standard * gain[...] + bias[...]).astype(BF)
         gain_sum = gain_sum + jnp.sum(incoming * standard, axis=0, keepdims=True)
         bias_sum = bias_sum + jnp.sum(incoming, axis=0, keepdims=True)
     row = lax.broadcasted_iota(jnp.int32, (16, 1024), 0)
@@ -104,9 +110,9 @@
             lines = jnp.where(row == first + place, part, lines)
             rest = rest - part
     lines = lines.astype(BF)
-    for k in range(4):
-        keep[k, 64:80, :] = lines
-        send[k, 64:80, :] = lines
+    for target in outs:
+        target[0, 32:48, :] = lines
+        target[1, 32:48, :] = lines
 
 
 def called(kernel, results, *operands, flops=20_000_000):
@@ -134,18 +140,33 @@
     mine = jnp.stack([lax.dynamic_index_in_dim(b, core, 0, False) for b in by_y])
     half = jnp.concatenate([mine, over_core(theirs)], axis=-1)
 
+    sides = [
+        [
+            jnp.stack(
+                [
+                    lax.dynamic_slice_in_dim(rows[0], (2 * ((x + k) % 4) + side) * 1024, 1024, 1)
+                    for k in range(4)
+                ]
+            )
+            for side in (z, 1 - z)
+        ]
+        for rows in (residual, out_grad)
+    ]
+    stream = [sides[0][0], over_both(sides[0][1], 0, 1)]
+    cotangent = [over_both(sides[1][f], -1, f) for f in (0, 1)]
+
     got = {(0, 0): half}
-    got[(1, 0)] = over_dp(half, 1, 0)
+    got[(0, 1)] = over_dp(half, 0, 1)
     got[(3, 0)] = over_dp(half, 3, 0)
-    got[(0, 1)] = over_dp(half, 0, 1)
-    got[(2, 0)] = over_dp(half, 2, 0)
+    got[(1, 0)] = over_dp(after(half, cotangent[1]), 1, 0)
+    got[(2, 0)] = over_dp(after(half, cotangent[0], stream[1]), 2, 0)
     for k in (1, 3):
         got[(k, 1)] = over_dp(got[(0, 1)], k, 0)
-    got[(2, 1)] = over_dp(got[(2, 0)], 0, 1)
+
     weight_own = out_weight[0]
-    weight_other = over_core(after(weight_own, half))
+    weight_other = over_core(after(weight_own, cotangent[1]))
     weights = jnp.concatenate([weight_own, weight_other], axis=0)
-
+    got[(2, 1)] = over_dp(after(got[(2, 0)], weight_other), 0, 1)
     columns = jnp.concatenate(
         [
             lax.dynamic_slice_in_dim(ln_gain, dp * 1024, 1024, 1),
@@ -153,8 +174,7 @@
         ],
         axis=0,
     )
-    cotangent = over_section(after(out_grad[0], got[(0, 1)]), -1)
-    columns = over_section(after(columns, got[(2, 0)]), -1)
+    columns = over_section(after(columns, got[(3, 0)]), -1)
     gain, bias = columns[:1], columns[1:]
 
     attended, tokens = [], []
@@ -167,18 +187,8 @@
         part = part.reshape(4, 128, 1024)
         attended += [part[0]] + [over_y(part[k], -k) for k in (1, 3, 2)]
 
-    pair = after(jnp.stack([residual[0], cotangent]), attended[0])
-    sides = [
-        jnp.stack(
-            [
-                lax.dynamic_slice_in_dim(pair, (2 * ((x + k) % 4) + side) * 1024, 1024, 2)
-                for k in range(4)
-            ]
-        )
-        for side in (z, 1 - z)
-    ]
-    sides = jnp.stack([sides[0], over_dp(sides[1], 0, 1)], axis=1)
-    turned = [sides[0]] + [over_dp(sides[k], k, 0) for k in (1, 2, 3)]
+    mixed = [jnp.stack([jnp.stack([stream[f][k], cotangent[f][k]]) for f in (0, 1)]) for k in range(4)]
+    turned = [mixed[0]] + [over_dp(after(mixed[k], attended[0]), k, 0) for k in (1, 2, 3)]
 
     line = jax.ShapeDtypeStruct((32, LANES), F32)
     rows_here = jax.ShapeDtypeStruct((256, 1024), BF)
@@ -187,33 +197,35 @@
     )
     stats = jnp.stack([stats, over_dp(stats_z, 0, 1)])
     stats = [stats] + [over_dp(stats, k, 0) for k in (1, 2, 3)]
-    blocks_out = jax.ShapeDtypeStruct((4, 80, 1024), BF)
-    returned, keep, send = called(
-        norm_kernel, (rows_here, blocks_out, blocks_out), hidden, *turned, gain, bias, *stats
+    block_out = jax.ShapeDtypeStruct((2, 80, 1024), BF)
+    returned, *outs = called(
+        norm_kernel, (rows_here, *[block_out] * 4), hidden, *turned, gain, bias, *stats
     )
 
     returned = returned.reshape(8, 32, 1024)
-    flowing = [returned] + [over_y(returned, k) for k in (1, 3, 2)]
-    flowing = [flowing[0], flowing[1], flowing[3], flowing[2]]
-
-    by_source = jnp.stack([keep, over_dp(send, 0, 1)], axis=1)
-    back = [by_source[0]] + [over_dp(by_source[k], -k, 0) for k in (1, 2, 3)]
-    back = jnp.stack(back).reshape(8, 80, 1024)
-    rows_back = jnp.concatenate(
+    flowing = [returned] + [over_y(returned, k) for k in (1, 2, 3)]
+
+    crossed = [outs[0], over_dp(outs[1], -1, 0), None, over_dp(outs[3], -3, 0)]
+    crossed[2] = over_dp(after(outs[2], crossed[1], crossed[3]), -2, 0)
+    to_rows = lambda near, beside: jnp.concatenate(
         [
-            lax.dynamic_index_in_dim(back, 2 * ((b // 2 - x) % 4) + ((b % 2) ^ z), 0, False)
+            jnp.where(b % 2 == z, *(lax.dynamic_index_in_dim(v, (b // 2 - x) % 4, 0, False) for v in (near, beside)))
             for b in range(8)
         ],
         axis=1,
     )
-    upstream = rows_back[32:64]
-    normed_rows = over_section(rows_back[:32], 1)
-    sums = rows_back[64:70].astype(F32)
+    gradient = [jnp.stack([c[f, 48:] for c in crossed]) for f in (0, 1)]
+    ahead = [over_both(jnp.stack([c[f, :40] for c in crossed]), 1, f) for f in (0, 1)]
+    upstream = to_rows(gradient[0], over_both(gradient[1], 0, 1))
+    arrived = to_rows(*ahead)
+    normed_rows = arrived[:32]
+    sums = arrived[32:].astype(F32)
     whole = jnp.stack([sums[0] + sums[1] + sums[2], sums[3] + sums[4] + sums[5]])
     whole = whole + over_core(whole)
     whole = whole + sum(over_y(whole, k) for k in (1, 2, 3))
-    whole = over_section(whole, 1)
-
+
+    flowing[1] = after(flowing[1], crossed[1], crossed[3])
+    flowing[2] = after(flowing[2], crossed[2])
     terms = [
         lax.dot_general(
             rows.reshape(256, 1024), weights, (((1,), (1,)), ((), ())), preferred_element_type=F32
@@ -224,15 +236,13 @@
     ]
     term = {r: jnp.stack([t[place] for t in terms]) for place, r in enumerate(ORDER)}
     crossing = over_dp(term[(2, 1)], 0, 1).astype(F32)
-    far = over_dp((term[(2, 0)].astype(F32) + crossing).astype(BF), -2, 0).astype(F32)
-    other = term[(0, 1)].astype(F32)
-    for k in (1, 3):
-        other = other + over_dp(term[(k, 1)], -k, 0).astype(F32)
-    context_sum = term[(0, 0)].astype(F32) + far
-    for k in (1, 3):
-        context_sum = context_sum + over_dp(term[(k, 0)], -k, 0).astype(F32)
-    context_sum = context_sum + over_dp(other.astype(BF), 0, 1).astype(F32)
-    context_sum = context_sum.astype(BF)
+    near = [over_dp(jnp.stack([term[(k, 0)], term[(k, 1)]]), -k, 0).astype(F32) for k in (1, 3)]
+    far = (term[(2, 0)].astype(F32) + crossing).astype(BF)
+    far = over_dp(far, -2, 0).astype(F32)
+    other = term[(0, 1)].astype(F32) + near[0][1] + near[1][1]
+    other = over_dp(other.astype(BF), 0, 1).astype(F32)
+    context_sum = (term[(0, 0)].astype(F32) + near[0][0] + near[1][0] + far + other).astype(BF)
+    context_sum = after(context_sum, whole)
     kept, given = context_sum[..., :768], over_core(context_sum[..., 768:])
     both = jnp.stack([kept, given], axis=1)
     both = jnp.stack(

time: 193 us -> 173 us (0.90)
  starting transfers between devices: 77 us -> 55.5 us
    ppermute x4 -> x1, waiting for transfers between devices: 25.9 us -> 0.01 us  [over_section(): lax.ppermute(value, 'section', [(s, (s + steps) % 2) for s in range(2)])]
    ppermute x12, waiting for transfers between devices: 13.6 us -> 29 us  [over_y(): lax.ppermute(value, 'mp', [(i, (i + 2 * steps) % 8) for i in range(8)])]
    ppermute x4 -> x1, starting transfers between devices: 13 us -> 1.34 us  [over_section(): lax.ppermute(value, 'section', [(s, (s + steps) % 2) for s in range(2)])]
    ppermute x26 -> x22, starting transfers between devices: 29 us -> 17.9 us  [over_dp(): lax.ppermute(value, 'dp', [(j, 2 * (((j >> 1) + steps) % 4) + (j & 1 ^ fl...]
    ppermute x5, starting transfers between devices: 23.4 us -> 13.3 us  [over_core(): return lax.ppermute(value, 'mp', [(i, i ^ 1) for i in range(8)])]
    ppermute x0 -> x6, starting transfers between devices: none -> 8.76 us  [over_both(): return lax.ppermute(value, ('section', 'dp'), pairs)]
    ppermute x0 -> x6, waiting for transfers between devices: none -> 8.31 us  [over_both(): return lax.ppermute(value, ('section', 'dp'), pairs)]
    ppermute x12, starting transfers between devices: 11.6 us -> 14.2 us  [over_y(): lax.ppermute(value, 'mp', [(i, (i + 2 * steps) % 8) for i in range(8)])]
  transfers between devices with their start and end apart: 47 -> 46, of which waited for: 28 -> 21; matrix products, arithmetic and copies ran while one was open for 9% -> 12% of each run, Pallas kernels for 0% -> 0%
where the time goes in v1:
time: 173 us
  waiting for transfers between devices  87.6 us (51%)
  starting transfers between devices  55.5 us (32%)
  matrix products  12.7 us (7%)
  local copies, waits for them, and re-layouts  6.79 us (4%)
  other arithmetic  6.64 us (4%)
    ppermute x22, waiting for transfers between devices, over_dp(): lax.ppermute(value, 'dp', [(j, 2 * (((j >> 1) + steps) % 4) + (j & 1 ^ fl...  48.2 us
    ppermute x12, waiting for transfers between devices, over_y(): lax.ppermute(value, 'mp', [(i, (i + 2 * steps) % 8) for i in range(8)])  29 us
    ppermute x22, starting transfers between devices, over_dp(): lax.ppermute(value, 'dp', [(j, 2 * (((j >> 1) + steps) % 4) + (j & 1 ^ fl...  17.9 us
    ppermute x12, starting transfers between devices, over_y(): lax.ppermute(value, 'mp', [(i, (i + 2 * steps) % 8) for i in range(8)])  14.2 us
    ppermute x5, starting transfers between devices, over_core(): return lax.ppermute(value, 'mp', [(i, i ^ 1) for i in range(8)])  13.3 us
    ppermute x6, starting transfers between devices, over_both(): return lax.ppermute(value, ('section', 'dp'), pairs)  8.76 us
    ppermute x6, waiting for transfers between devices, over_both(): return lax.ppermute(value, ('section', 'dp'), pairs)  8.31 us
    dot_general x4, matrix products, shards(): lax.dot_general(rows.reshape(256, 1024), weights, (((1,), (1,)), ((), ())...  5.46 us
  transfers between devices with their start and end apart: 46, of which 21 were waited for; matrix products, arithmetic and copies ran while one was open for 12% of the time, Pallas kernels for 0%

profile of v1, /device:TPU:1, one launch (start us, length us, event | category | flops | bytes accessed | tf_op | source)
XLA Modules:
  0.0 172.7 jit_solution(2687036962138360168)
XLA Ops:
  4.1 1.8 %collective-permute-start.10 = (bf16[4,32,1024]{2,1,0:T(8,128)(2,1)S(1)}, bf16[4,32,1024]{2,1,0:T(8,128)(2,1)S(1)}, u32[]{:S(2)}, u32[]{:S(2)}) collective-permute-start(bf16[4,32,1024]{2,1,0:T(8,128)(2,1)S(1)} %pad_maximum_fusion.13), channel_id=1, source_target_pairs={{0,1},{1,0},{2,3},{3,2},{4,5},{5,4},{6,7},{7,6},{64,65},{65,64},{6... | collective-permute-start | bytes 786440 | tf_op jit(solution)/shard_map/ppermute | solution.py:34
  6.0 2.3 %collective-permute-start.2 = (bf16[4,32,1024]{2,1,0:T(8,128)(2,1)S(1)}, bf16[4,32,1024]{2,1,0:T(8,128)(2,1)S(1)}, u32[]{:S(2)}, u32[]{:S(2)}) collective-permute-start(bf16[4,32,1024]{2,1,0:T(8,128)(2,1)S(1)} %pad_maximum_fusion.11), channel_id=1, source_target_pairs={{0,65},{1,64},{2,67},{3,66},{4,69},{5,68},{6,71},{7,70},{64,1},{65... | collective-permute-start | bytes 786440 | tf_op jit(solution)/shard_map/ppermute | solution.py:34
  10.4 2.5 %collective-permute-start.4 = (bf16[4,32,1536]{2,1,0:T(8,128)(2,1)S(1)}, bf16[4,32,1536]{2,1,0:T(8,128)(2,1)S(1)}, u32[]{:S(2)}, u32[]{:S(2)}) collective-permute-start(bf16[4,32,1536]{2,1,0:T(8,128)(2,1)S(1)} %pad_maximum_fusion.6), channel_id=1, source_target_pairs={{0,6},{1,7},{2,0},{3,1},{4,2},{5,3},{6,4},{7,5},{8,14},{9,15},{10,... | collective-permute-start | bytes 1179656 | tf_op jit(solution)/shard_map/ppermute | solution.py:23
  13.0 6.4 %collective-permute-done.2 = bf16[4,32,1024]{2,1,0:T(8,128)(2,1)S(1)} collective-permute-done((bf16[4,32,1024]{2,1,0:T(8,128)(2,1)S(1)}, bf16[4,32,1024]{2,1,0:T(8,128)(2,1)S(1)}, u32[]{:S(2)}, u32[]{:S(2)}) %collective-permute-start.2) | collective-permute-done | bytes 262176 | tf_op jit(solution)/shard_map/ppermute | solution.py:34
  19.3 1.9 %collective-permute-done.9 = bf16[4,32,1024]{2,1,0:T(8,128)(2,1)S(1)} collective-permute-done((bf16[4,32,1024]{2,1,0:T(8,128)(2,1)S(1)}, bf16[4,32,1024]{2,1,0:T(8,128)(2,1)S(1)}, u32[]{:S(2)}, u32[]{:S(2)}) %collective-permute-start.9) | collective-permute-done | bytes 262176 | tf_op jit(solution)/shard_map/ppermute | solution.py:34
  21.3 2.7 %collective-permute-start.11 = (bf16[4,32,1536]{2,1,0:T(8,128)(2,1)S(1)}, bf16[4,32,1536]{2,1,0:T(8,128)(2,1)S(1)}, u32[]{:S(2)}, u32[]{:S(2)}) collective-permute-start(bf16[4,32,1536]{2,1,0:T(8,128)(2,1)S(1)} %pad_maximum_fusion.6), channel_id=1, source_target_pairs={{0,4},{1,5},{2,6},{3,7},{4,0},{5,1},{6,2},{7,3},{8,12},{9,13},{10,... | collective-permute-start | bytes 1179656 | tf_op jit(solution)/shard_map/ppermute | solution.py:23
  27.8 2.4 %collective-permute-start.13 = (bf16[4,32,1536]{2,1,0:T(8,128)(2,1)S(1)}, bf16[4,32,1536]{2,1,0:T(8,128)(2,1)S(1)}, u32[]{:S(2)}, u32[]{:S(2)}) collective-permute-start(bf16[4,32,1536]{2,1,0:T(8,128)(2,1)S(1)} %collective-permute-done.1), channel_id=1, source_target_pairs={{0,6},{1,7},{2,0},{3,1},{4,2},{5,3},{6,4},{7,5},{8,14},{9,15},{10,... | collective-permute-start | bytes 1179656 | tf_op jit(solution)/shard_map/ppermute | solution.py:23
  30.1 12.1 %collective-permute-done.3 = bf16[4,32,1536]{2,1,0:T(8,128)(2,1)S(1)} collective-permute-done((bf16[4,32,1536]{2,1,0:T(8,128)(2,1)S(1)}, bf16[4,32,1536]{2,1,0:T(8,128)(2,1)S(1)}, u32[]{:S(2)}, u32[]{:S(2)}) %collective-permute-start.3) | collective-permute-done | bytes 393248 | tf_op jit(solution)/shard_map/ppermute | solution.py:23
  43.1 1.8 %convolution_convert_fusion.5 = bf16[512,1024]{1,0:T(8,128)(2,1)S(1)} fusion(bf16[512,1536]{1,0:T(8,128)(2,1)S(1)} %bitcast.221, bf16[768,1024]{1,0:T(8,128)(2,1)S(1)} %collective-permute-done.5, bf16[768,1024]{1,0:T(8,128)(2,1)S(1)} %bitcast.245), kind=kOutput, calls=%fused_computation.13 | convolution fusion | flops 1617428480 | bytes 5767168 | tf_op jit(solution)/shard_map/dot_general | solution.py:186
  45.2 3.2 %collective-permute-start.19 = (bf16[2,2,32,1024]{3,2,1,0:T(8,128)(2,1)S(1)}, bf16[2,2,32,1024]{3,2,1,0:T(8,128)(2,1)S(1)}, u32[]{:S(2)}, u32[]{:S(2)}) collective-permute-start(bf16[2,2,32,1024]{3,2,1,0:T(8,128)(2,1)S(1)} %pad_maximum_fusion.16), channel_id=1, source_target_pairs={{0,4},{1,5},{2,6},{3,7},{4,0},{5,1},{6,2},{7,3},{8,12},{9,13},{10,... | collective-permute-start | bytes 786440 | tf_op jit(solution)/shard_map/ppermute | solution.py:23
  48.4 5.2 %collective-permute-done.12 = bf16[4,32,1536]{2,1,0:T(8,128)(2,1)S(1)} collective-permute-done((bf16[4,32,1536]{2,1,0:T(8,128)(2,1)S(1)}, bf16[4,32,1536]{2,1,0:T(8,128)(2,1)S(1)}, u32[]{:S(2)}, u32[]{:S(2)}) %collective-permute-start.12) | collective-permute-done | bytes 393248 | tf_op jit(solution)/shard_map/ppermute | solution.py:23
  53.7 2.9 %collective-permute-start.8 = (bf16[128,1024]{1,0:T(8,128)(2,1)S(1)}, bf16[128,1024]{1,0:T(8,128)(2,1)S(1)}, u32[]{:S(2)}, u32[]{:S(2)}) collective-permute-start(bf16[128,1024]{1,0:T(8,128)(2,1)S(1)} %get-tuple-element.52), channel_id=1, source_target_pairs={{0,32},{8,40},{16,48},{24,56},{32,0},{40,8},{48,16},{56,24},{1,33}... | collective-permute-start | bytes 786440 | tf_op jit(solution)/shard_map/ppermute | solution.py:19
  56.9 1.8 %convolution_convert_fusion.4 = bf16[512,1024]{1,0:T(8,128)(2,1)S(1)} fusion(bf16[512,1536]{1,0:T(8,128)(2,1)S(1)} %bitcast.222, bf16[768,1024]{1,0:T(8,128)(2,1)S(1)} %collective-permute-done.5, bf16[768,1024]{1,0:T(8,128)(2,1)S(1)} %bitcast.246), kind=kOutput, calls=%fused_computation.12 | convolution fusion | flops 1617428480 | bytes 5767168 | tf_op jit(solution)/shard_map/dot_general | solution.py:186
  59.3 5.6 %collective-permute-done.18.turned_1 = bf16[2,2,32,1024]{3,2,1,0:T(8,128)(2,1)S(1)} collective-permute-done((bf16[2,2,32,1024]{3,2,1,0:T(8,128)(2,1)S(1)}, bf16[2,2,32,1024]{3,2,1,0:T(8,128)(2,1)S(1)}, u32[]{:S(2)}, u32[]{:S(2)}) %collective-permute-start.18) | collective-permute-done | bytes 262176 | tf_op jit(solution)/shard_map/ppermute | solution.py:23
  64.9 2.7 %collective-permute-start.6 = (bf16[128,1024]{1,0:T(8,128)(2,1)S(1)}, bf16[128,1024]{1,0:T(8,128)(2,1)S(1)}, u32[]{:S(2)}, u32[]{:S(2)}) collective-permute-start(bf16[128,1024]{1,0:T(8,128)(2,1)S(1)} %get-tuple-element.54), channel_id=1, source_target_pairs={{0,48},{8,56},{16,0},{24,8},{32,16},{40,24},{48,32},{56,40},{1,49}... | collective-permute-start | bytes 786440 | tf_op jit(solution)/shard_map/ppermute | solution.py:19
  68.7 2.0 %collective-permute-start.15 = (bf16[128,1024]{1,0:T(8,128)(2,1)S(1)}, bf16[128,1024]{1,0:T(8,128)(2,1)S(1)}, u32[]{:S(2)}, u32[]{:S(2)}) collective-permute-start(bf16[128,1024]{1,0:T(8,128)(2,1)S(1)} %get-tuple-element.50), channel_id=1, source_target_pairs={{0,48},{8,56},{16,0},{24,8},{32,16},{40,24},{48,32},{56,40},{1,49}... | collective-permute-start | bytes 786440 | tf_op jit(solution)/shard_map/ppermute | solution.py:19
  70.7 2.2 %collective-permute-done.6.first_1 = bf16[128,1024]{1,0:T(8,128)(2,1)S(1)} collective-permute-done((bf16[128,1024]{1,0:T(8,128)(2,1)S(1)}, bf16[128,1024]{1,0:T(8,128)(2,1)S(1)}, u32[]{:S(2)}, u32[]{:S(2)}) %collective-permute-start.6) | collective-permute-done | bytes 262176 | tf_op jit(solution)/shard_map/ppermute | solution.py:19
  72.9 2.5 %collective-permute-done.17.second_3 = bf16[128,1024]{1,0:T(8,128)(2,1)S(1)} collective-permute-done((bf16[128,1024]{1,0:T(8,128)(2,1)S(1)}, bf16[128,1024]{1,0:T(8,128)(2,1)S(1)}, u32[]{:S(2)}, u32[]{:S(2)}) %collective-permute-start.17) | collective-permute-done | bytes 262176 | tf_op jit(solution)/shard_map/ppermute | solution.py:19
  75.4 7.6 %collective-permute-done.16.second_2 = bf16[128,1024]{1,0:T(8,128)(2,1)S(1)} collective-permute-done((bf16[128,1024]{1,0:T(8,128)(2,1)S(1)}, bf16[128,1024]{1,0:T(8,128)(2,1)S(1)}, u32[]{:S(2)}, u32[]{:S(2)}) %collective-permute-start.16) | collective-permute-done | bytes 262176 | tf_op jit(solution)/shard_map/ppermute | solution.py:19
  84.0 2.6 %collective-permute-done.22 = f32[32,128]{1,0:T(8,128)S(1)} collective-permute-done((f32[32,128]{1,0:T(8,128)S(1)}, f32[32,128]{1,0:T(8,128)S(1)}, u32[]{:S(2)}, u32[]{:S(2)}) %collective-permute-start.22) | collective-permute-done | bytes 16416 | tf_op jit(solution)/shard_map/ppermute | solution.py:23
  92.7 3.5 %collective-permute-start.34 = (bf16[8,32,1024]{2,1,0:T(8,128)(2,1)S(1)}, bf16[8,32,1024]{2,1,0:T(8,128)(2,1)S(1)}, u32[]{:S(2)}, u32[]{:S(2)}) collective-permute-start(bf16[8,32,1024]{2,1,0:T(8,128)(2,1)S(1)} %bitcast.216), channel_id=1, source_target_pairs={{0,48},{8,56},{16,0},{24,8},{32,16},{40,24},{48,32},{56,40},{1,49}... | collective-permute-start | bytes 1572872 | tf_op jit(solution)/shard_map/ppermute | solution.py:19
  98.3 2.4 %convolution_convert_fusion.3 = bf16[256,1536]{1,0:T(8,128)(2,1)S(1)} fusion(bf16[256,1024]{1,0:T(8,128)(2,1)S(1)} %get-tuple-element.44, bf16[768,1024]{1,0:T(8,128)(2,1)} %copy-done.13, bf16[768,1024]{1,0:T(8,128)(2,1)S(1)} %bitcast.247), kind=kOutput, calls=%fused_computation.8 | convolution fusion | flops 811991040 | bytes 4456448 | tf_op jit(solution)/shard_map/dot_general | solution.py:230
  100.8 2.2 %collective-permute-done.26 = bf16[2,80,1024]{2,1,0:T(8,128)(2,1)S(1)} collective-permute-done((bf16[2,80,1024]{2,1,0:T(8,128)(2,1)S(1)}, bf16[2,80,1024]{2,1,0:T(8,128)(2,1)S(1)}, u32[]{:S(2)}, u32[]{:S(2)}) %collective-permute-start.26) | collective-permute-done | bytes 327712 | tf_op jit(solution)/shard_map/ppermute | solution.py:23
  103.1 2.4 %collective-permute-done.27 = bf16[2,80,1024]{2,1,0:T(8,128)(2,1)S(1)} collective-permute-done((bf16[2,80,1024]{2,1,0:T(8,128)(2,1)S(1)}, bf16[2,80,1024]{2,1,0:T(8,128)(2,1)S(1)}, u32[]{:S(2)}, u32[]{:S(2)}) %collective-permute-start.27) | collective-permute-done | bytes 327712 | tf_op jit(solution)/shard_map/ppermute | solution.py:23
  105.5 16.6 %collective-permute-done.32 = bf16[8,32,1024]{2,1,0:T(8,128)(2,1)S(1)} collective-permute-done((bf16[8,32,1024]{2,1,0:T(8,128)(2,1)S(1)}, bf16[8,32,1024]{2,1,0:T(8,128)(2,1)S(1)}, u32[]{:S(2)}, u32[]{:S(2)}) %collective-permute-start.32) | collective-permute-done | bytes 524320 | tf_op jit(solution)/shard_map/ppermute | solution.py:19
  132.5 1.8 %fusion.2 = f32[1536,1024,1,1]{1,0,3,2:T(8,128)S(1)} fusion(bf16[4,8,32,1024]{3,2,1,0:T(8,128)(2,1)S(1)} %pad_maximum_fusion.1, bf16[4,1,32,1536]{3,2,1,0:T(8,128)(2,1)S(1)} %bitcast.230, bf16[4,1,32,1536]{3,2,1,0:T(8,128)(2,1)S(1)} %bitcast.234, bf16[4,1,32,1536]{3,2,1,0:T(8,128)(2,1)S(1)} %bitcast.232, bf16[4,1,32,1536]{3,2,1,0:T(8,128)(2,1)S(1)} %copy-done.1), kind=kOutput, calls=%fused_computation.15 | convolution fusion | flops 1612972032 | bytes 8912896 | tf_op jit(solution)/shard_map/dot_general | solution.py:255
  134.4 1.8 %bitcast_add_fusion = f32[1536,1024]{1,0:T(8,128)S(1)} fusion(f32[1536,1024,1,1]{1,0,3,2:T(8,128)S(1)} %fusion.2, bf16[4,8,32,1024]{3,2,1,0:T(8,128)(2,1)S(1)} %pad_maximum_fusion.1, bf16[4,4,32,1536]{3,2,0,1:T(8,128)(2,1)S(1)} %pad_maximum_fusion.3), kind=kOutput, calls=%fused_computation | convolution fusion | flops 1612185600 | bytes 15204352 | tf_op jit(solution)/shard_map/dot_general | solution.py:255
  137.1 5.9 %collective-permute-start.45 = (bf16[768,1024]{1,0:T(8,128)(2,1)S(1)}, bf16[768,1024]{1,0:T(8,128)(2,1)S(1)}, u32[]{:S(2)}, u32[]{:S(2)}) collective-permute-start(bf16[768,1024]{1,0:T(8,128)(2,1)S(1)} %slice.658), channel_id=1, source_target_pairs={{0,8},{8,0},{16,24},{24,16},{32,40},{40,32},{48,56},{56,48},{1,9},... | collective-permute-start | bytes 4718600 | tf_op jit(solution)/shard_map/ppermute | solution.py:15
  148.1 6.7 %collective-permute-done.36 = bf16[2,4,32,1536]{3,2,1,0:T(8,128)(2,1)S(1)} collective-permute-done((bf16[2,4,32,1536]{3,2,1,0:T(8,128)(2,1)S(1)}, bf16[2,4,32,1536]{3,2,1,0:T(8,128)(2,1)S(1)}, u32[]{:S(2)}, u32[]{:S(2)}) %collective-permute-start.36) | collective-permute-done | bytes 786464 | tf_op jit(solution)/shard_map/ppermute | solution.py:23
  156.8 7.0 %collective-permute-done.38 = bf16[4,32,1536]{2,1,0:T(8,128)(2,1)S(1)} collective-permute-done((bf16[4,32,1536]{2,1,0:T(8,128)(2,1)S(1)}, bf16[4,32,1536]{2,1,0:T(8,128)(2,1)S(1)}, u32[]{:S(2)}, u32[]{:S(2)}) %collective-permute-start.38) | collective-permute-done | bytes 393248 | tf_op jit(solution)/shard_map/ppermute | solution.py:23
  164.1 4.2 %collective-permute-start.44 = (bf16[4,32,768]{2,1,0:T(8,128)(2,1)S(1)}, bf16[4,32,768]{2,1,0:T(8,128)(2,1)S(1)}, u32[]{:S(2)}, u32[]{:S(2)}) collective-permute-start(bf16[4,32,768]{2,1,0:T(8,128)(2,1)S(1)} %get-tuple-element.108), channel_id=1, source_target_pairs={{0,8},{8,0},{16,24},{24,16},{32,40},{40,32},{48,56},{56,48},{1,9},... | collective-permute-start | bytes 589832 | tf_op jit(solution)/shard_map/ppermute | solution.py:15
  170.2 2.4 %fusion = f32[1,768,1024]{2,1,0:T(8,128)} fusion(f32[1536,1024]{1,0:T(8,128)S(1)} %bitcast_add_fusion, bf16[768,1024]{1,0:T(8,128)(2,1)S(1)} %collective-permute-done.45), kind=kLoop, calls=%fused_computation.3 | loop fusion | flops 1572864 | bytes 7864320 | tf_op jit(solution)/shard_map/broadcast_in_dim | solution.py:265
  (190 shorter events, 41.8 us)
Async XLA Ops:
  4.1 15.2 %collective-permute-start.10 = (bf16[4,32,1024]{2,1,0:T(8,128)(2,1)S(1)}, bf16[4,32,1024]{2,1,0:T(8,128)(2,1)S(1)}, u32[]{:S(2)}, u32[]{:S(2)}) collective-permute-start(bf16[4,32,1024]{2,1,0:T(8,128)(2,1)S(1)} %pad_maximum_fusion.13), channel_id=1, source_target_pairs={{0,1},{1,0},{2,3},{3,2},{4,5},{5,4},{6,7},{7,6},{64,65},{65,64},{6... | collective-permute-start | bytes 786440 | tf_op jit(solution)/shard_map/ppermute | solution.py:34
  6.0 13.4 %collective-permute-start.2 = (bf16[4,32,1024]{2,1,0:T(8,128)(2,1)S(1)}, bf16[4,32,1024]{2,1,0:T(8,128)(2,1)S(1)}, u32[]{:S(2)}, u32[]{:S(2)}) collective-permute-start(bf16[4,32,1024]{2,1,0:T(8,128)(2,1)S(1)} %pad_maximum_fusion.11), channel_id=1, source_target_pairs={{0,65},{1,64},{2,67},{3,66},{4,69},{5,68},{6,71},{7,70},{64,1},{65... | collective-permute-start | bytes 786440 | tf_op jit(solution)/shard_map/ppermute | solution.py:34
  8.3 12.9 %collective-permute-start.9 = (bf16[4,32,1024]{2,1,0:T(8,128)(2,1)S(1)}, bf16[4,32,1024]{2,1,0:T(8,128)(2,1)S(1)}, u32[]{:S(2)}, u32[]{:S(2)}) collective-permute-start(bf16[4,32,1024]{2,1,0:T(8,128)(2,1)S(1)} %pad_maximum_fusion.12), channel_id=1, source_target_pairs={{0,64},{1,65},{2,66},{3,67},{4,68},{5,69},{6,70},{7,71},{64,0},{65... | collective-permute-start | bytes 786440 | tf_op jit(solution)/shard_map/ppermute | solution.py:34
  10.4 16.0 %collective-permute-start.4 = (bf16[4,32,1536]{2,1,0:T(8,128)(2,1)S(1)}, bf16[4,32,1536]{2,1,0:T(8,128)(2,1)S(1)}, u32[]{:S(2)}, u32[]{:S(2)}) collective-permute-start(bf16[4,32,1536]{2,1,0:T(8,128)(2,1)S(1)} %pad_maximum_fusion.6), channel_id=1, source_target_pairs={{0,6},{1,7},{2,0},{3,1},{4,2},{5,3},{6,4},{7,5},{8,14},{9,15},{10,... | collective-permute-start | bytes 1179656 | tf_op jit(solution)/shard_map/ppermute | solution.py:23
  12.9 14.8 %collective-permute-start.1 = (bf16[4,32,1536]{2,1,0:T(8,128)(2,1)S(1)}, bf16[4,32,1536]{2,1,0:T(8,128)(2,1)S(1)}, u32[]{:S(2)}, u32[]{:S(2)}) collective-permute-start(bf16[4,32,1536]{2,1,0:T(8,128)(2,1)S(1)} %pad_maximum_fusion.6), channel_id=1, source_target_pairs={{0,1},{1,0},{2,3},{3,2},{4,5},{5,4},{6,7},{7,6},{8,9},{9,8},{10,11... | collective-permute-start | bytes 1179656 | tf_op jit(solution)/shard_map/ppermute | solution.py:23
  21.3 21.7 %collective-permute-start.11 = (bf16[4,32,1536]{2,1,0:T(8,128)(2,1)S(1)}, bf16[4,32,1536]{2,1,0:T(8,128)(2,1)S(1)}, u32[]{:S(2)}, u32[]{:S(2)}) collective-permute-start(bf16[4,32,1536]{2,1,0:T(8,128)(2,1)S(1)} %pad_maximum_fusion.6), channel_id=1, source_target_pairs={{0,4},{1,5},{2,6},{3,7},{4,0},{5,1},{6,2},{7,3},{8,12},{9,13},{10,... | collective-permute-start | bytes 1179656 | tf_op jit(solution)/shard_map/ppermute | solution.py:23
  24.0 18.2 %collective-permute-start.3 = (bf16[4,32,1536]{2,1,0:T(8,128)(2,1)S(1)}, bf16[4,32,1536]{2,1,0:T(8,128)(2,1)S(1)}, u32[]{:S(2)}, u32[]{:S(2)}) collective-permute-start(bf16[4,32,1536]{2,1,0:T(8,128)(2,1)S(1)} %pad_maximum_fusion.6), channel_id=1, source_target_pairs={{0,2},{1,3},{2,4},{3,5},{4,6},{5,7},{6,0},{7,1},{8,10},{9,11},{10,... | collective-permute-start | bytes 1179656 | tf_op jit(solution)/shard_map/ppermute | solution.py:23
  24.3 18.7 %collective-permute-start.5 = (bf16[768,1024]{1,0:T(8,128)(2,1)S(1)}, bf16[768,1024]{1,0:T(8,128)(2,1)S(1)}, u32[]{:S(2)}, u32[]{:S(2)}) collective-permute-start(bf16[768,1024]{1,0:T(8,128)(2,1)S(1)} %bitcast.244), channel_id=1, source_target_pairs={{0,8},{8,0},{16,24},{24,16},{32,40},{40,32},{48,56},{56,48},{1,9},... | collective-permute-start | bytes 4718600 | tf_op jit(solution)/shard_map/ppermute | solution.py:15
  26.4 32.3 %collective-permute-start.21 = (f32[2,1024]{1,0:T(2,128)S(1)}, f32[2,1024]{1,0:T(2,128)S(1)}, u32[]{:S(2)}, u32[]{:S(2)}) collective-permute-start(f32[2,1024]{1,0:T(2,128)S(1)} %pad_maximum_fusion.23), channel_id=1, source_target_pairs={{0,64},{64,0},{1,65},{65,1},{2,66},{66,2},{3,67},{67,3},{4,68},{68... | collective-permute-start | bytes 24584 | tf_op jit(solution)/shard_map/ppermute | solution.py:29
  27.8 17.4 %collective-permute-start.13 = (bf16[4,32,1536]{2,1,0:T(8,128)(2,1)S(1)}, bf16[4,32,1536]{2,1,0:T(8,128)(2,1)S(1)}, u32[]{:S(2)}, u32[]{:S(2)}) collective-permute-start(bf16[4,32,1536]{2,1,0:T(8,128)(2,1)S(1)} %collective-permute-done.1), channel_id=1, source_target_pairs={{0,6},{1,7},{2,0},{3,1},{4,2},{5,3},{6,4},{7,5},{8,14},{9,15},{10,... | collective-permute-start | bytes 1179656 | tf_op jit(solution)/shard_map/ppermute | solution.py:23
  42.3 11.4 %collective-permute-start.12 = (bf16[4,32,1536]{2,1,0:T(8,128)(2,1)S(1)}, bf16[4,32,1536]{2,1,0:T(8,128)(2,1)S(1)}, u32[]{:S(2)}, u32[]{:S(2)}) collective-permute-start(bf16[4,32,1536]{2,1,0:T(8,128)(2,1)S(1)} %collective-permute-done.1), channel_id=1, source_target_pairs={{0,2},{1,3},{2,4},{3,5},{4,6},{5,7},{6,0},{7,1},{8,10},{9,11},{10,... | collective-permute-start | bytes 1179656 | tf_op jit(solution)/shard_map/ppermute | solution.py:23
  43.0 10.7 %collective-permute-start.14 = (bf16[4,32,1536]{2,1,0:T(8,128)(2,1)S(1)}, bf16[4,32,1536]{2,1,0:T(8,128)(2,1)S(1)}, u32[]{:S(2)}, u32[]{:S(2)}) collective-permute-start(bf16[4,32,1536]{2,1,0:T(8,128)(2,1)S(1)} %collective-permute-done.11), channel_id=1, source_target_pairs={{0,1},{1,0},{2,3},{3,2},{4,5},{5,4},{6,7},{7,6},{8,9},{9,8},{10,11... | collective-permute-start | bytes 1179656 | tf_op jit(solution)/shard_map/ppermute | solution.py:23
  45.0 19.9 %collective-permute-start.18 = (bf16[2,2,32,1024]{3,2,1,0:T(8,128)(2,1)S(1)}, bf16[2,2,32,1024]{3,2,1,0:T(8,128)(2,1)S(1)}, u32[]{:S(2)}, u32[]{:S(2)}) collective-permute-start(bf16[2,2,32,1024]{3,2,1,0:T(8,128)(2,1)S(1)} %pad_maximum_fusion.15), channel_id=1, source_target_pairs={{0,2},{1,3},{2,4},{3,5},{4,6},{5,7},{6,0},{7,1},{8,10},{9,11},{10,... | collective-permute-start | bytes 786440 | tf_op jit(solution)/shard_map/ppermute | solution.py:23
  45.2 22.4 %collective-permute-start.19 = (bf16[2,2,32,1024]{3,2,1,0:T(8,128)(2,1)S(1)}, bf16[2,2,32,1024]{3,2,1,0:T(8,128)(2,1)S(1)}, u32[]{:S(2)}, u32[]{:S(2)}) collective-permute-start(bf16[2,2,32,1024]{3,2,1,0:T(8,128)(2,1)S(1)} %pad_maximum_fusion.16), channel_id=1, source_target_pairs={{0,4},{1,5},{2,6},{3,7},{4,0},{5,1},{6,2},{7,3},{8,12},{9,13},{10,... | collective-permute-start | bytes 786440 | tf_op jit(solution)/shard_map/ppermute | solution.py:23
  53.7 14.3 %collective-permute-start.20 = (bf16[2,2,32,1024]{3,2,1,0:T(8,128)(2,1)S(1)}, bf16[2,2,32,1024]{3,2,1,0:T(8,128)(2,1)S(1)}, u32[]{:S(2)}, u32[]{:S(2)}) collective-permute-start(bf16[2,2,32,1024]{3,2,1,0:T(8,128)(2,1)S(1)} %pad_maximum_fusion.17), channel_id=1, source_target_pairs={{0,6},{1,7},{2,0},{3,1},{4,2},{5,3},{6,4},{7,5},{8,14},{9,15},{10,... | collective-permute-start | bytes 786440 | tf_op jit(solution)/shard_map/ppermute | solution.py:23
  53.7 15.0 %collective-permute-start.8 = (bf16[128,1024]{1,0:T(8,128)(2,1)S(1)}, bf16[128,1024]{1,0:T(8,128)(2,1)S(1)}, u32[]{:S(2)}, u32[]{:S(2)}) collective-permute-start(bf16[128,1024]{1,0:T(8,128)(2,1)S(1)} %get-tuple-element.52), channel_id=1, source_target_pairs={{0,32},{8,40},{16,48},{24,56},{32,0},{40,8},{48,16},{56,24},{1,33}... | collective-permute-start | bytes 786440 | tf_op jit(solution)/shard_map/ppermute | solution.py:19
  58.8 11.9 %collective-permute-start.7 = (bf16[128,1024]{1,0:T(8,128)(2,1)S(1)}, bf16[128,1024]{1,0:T(8,128)(2,1)S(1)}, u32[]{:S(2)}, u32[]{:S(2)}) collective-permute-start(bf16[128,1024]{1,0:T(8,128)(2,1)S(1)} %get-tuple-element.53), channel_id=1, source_target_pairs={{0,16},{8,24},{16,32},{24,40},{32,48},{40,56},{48,0},{56,8},{1,17}... | collective-permute-start | bytes 786440 | tf_op jit(solution)/shard_map/ppermute | solution.py:19
  68.0 15.0 %collective-permute-start.16 = (bf16[128,1024]{1,0:T(8,128)(2,1)S(1)}, bf16[128,1024]{1,0:T(8,128)(2,1)S(1)}, u32[]{:S(2)}, u32[]{:S(2)}) collective-permute-start(bf16[128,1024]{1,0:T(8,128)(2,1)S(1)} %get-tuple-element.49), channel_id=1, source_target_pairs={{0,16},{8,24},{16,32},{24,40},{32,48},{40,56},{48,0},{56,8},{1,17}... | collective-permute-start | bytes 786440 | tf_op jit(solution)/shard_map/ppermute | solution.py:19
  68.7 14.4 %collective-permute-start.15 = (bf16[128,1024]{1,0:T(8,128)(2,1)S(1)}, bf16[128,1024]{1,0:T(8,128)(2,1)S(1)}, u32[]{:S(2)}, u32[]{:S(2)}) collective-permute-start(bf16[128,1024]{1,0:T(8,128)(2,1)S(1)} %get-tuple-element.50), channel_id=1, source_target_pairs={{0,48},{8,56},{16,0},{24,8},{32,16},{40,24},{48,32},{56,40},{1,49}... | collective-permute-start | bytes 786440 | tf_op jit(solution)/shard_map/ppermute | solution.py:19
  92.7 30.5 %collective-permute-start.34 = (bf16[8,32,1024]{2,1,0:T(8,128)(2,1)S(1)}, bf16[8,32,1024]{2,1,0:T(8,128)(2,1)S(1)}, u32[]{:S(2)}, u32[]{:S(2)}) collective-permute-start(bf16[8,32,1024]{2,1,0:T(8,128)(2,1)S(1)} %bitcast.216), channel_id=1, source_target_pairs={{0,48},{8,56},{16,0},{24,8},{32,16},{40,24},{48,32},{56,40},{1,49}... | collective-permute-start | bytes 1572872 | tf_op jit(solution)/shard_map/ppermute | solution.py:19
  96.2 31.8 %collective-permute-start.33 = (bf16[8,32,1024]{2,1,0:T(8,128)(2,1)S(1)}, bf16[8,32,1024]{2,1,0:T(8,128)(2,1)S(1)}, u32[]{:S(2)}, u32[]{:S(2)}) collective-permute-start(bf16[8,32,1024]{2,1,0:T(8,128)(2,1)S(1)} %bitcast.217), channel_id=1, source_target_pairs={{0,32},{8,40},{16,48},{24,56},{32,0},{40,8},{48,16},{56,24},{1,33}... | collective-permute-start | bytes 1572872 | tf_op jit(solution)/shard_map/ppermute | solution.py:19
  96.2 25.9 %collective-permute-start.32 = (bf16[8,32,1024]{2,1,0:T(8,128)(2,1)S(1)}, bf16[8,32,1024]{2,1,0:T(8,128)(2,1)S(1)}, u32[]{:S(2)}, u32[]{:S(2)}) collective-permute-start(bf16[8,32,1024]{2,1,0:T(8,128)(2,1)S(1)} %bitcast.218), channel_id=1, source_target_pairs={{0,16},{8,24},{16,32},{24,40},{32,48},{40,56},{48,0},{56,8},{1,17}... | collective-permute-start | bytes 1572872 | tf_op jit(solution)/shard_map/ppermute | solution.py:19
  105.4 18.9 %collective-permute-start.28 = (bf16[2,80,1024]{2,1,0:T(8,128)(2,1)S(1)}, bf16[2,80,1024]{2,1,0:T(8,128)(2,1)S(1)}, u32[]{:S(2)}, u32[]{:S(2)}) collective-permute-start(bf16[2,80,1024]{2,1,0:T(8,128)(2,1)S(1)} %get-tuple-element.43), channel_id=1, source_target_pairs={{0,4},{1,5},{2,6},{3,7},{4,0},{5,1},{6,2},{7,3},{8,12},{9,13},{10,... | collective-permute-start | bytes 983048 | tf_op jit(solution)/shard_map/ppermute | solution.py:23
  124.4 12.3 %collective-permute-start.31 = (bf16[4,32,1024]{2,1,0:T(8,128)(2,1)S(1)}, bf16[4,32,1024]{2,1,0:T(8,128)(2,1)S(1)}, u32[]{:S(2)}, u32[]{:S(2)}) collective-permute-start(bf16[4,32,1024]{2,1,0:T(8,128)(2,1)S(1)} %pad_maximum_fusion.19), channel_id=1, source_target_pairs={{0,1},{1,0},{2,3},{3,2},{4,5},{5,4},{6,7},{7,6},{64,65},{65,64},{6... | collective-permute-start | bytes 786440 | tf_op jit(solution)/shard_map/ppermute | solution.py:34
  124.5 12.6 %collective-permute-start.30 = (bf16[4,40,1024]{2,1,0:T(8,128)(2,1)S(1)}, bf16[4,40,1024]{2,1,0:T(8,128)(2,1)S(1)}, u32[]{:S(2)}, u32[]{:S(2)}) collective-permute-start(bf16[4,40,1024]{2,1,0:T(8,128)(2,1)S(1)} %pad_maximum_fusion.10), channel_id=1, source_target_pairs={{0,65},{1,64},{2,67},{3,66},{4,69},{5,68},{6,71},{7,70},{64,1},{65... | collective-permute-start | bytes 983048 | tf_op jit(solution)/shard_map/ppermute | solution.py:34
  126.2 16.7 %collective-permute-start.29 = (bf16[4,40,1024]{2,1,0:T(8,128)(2,1)S(1)}, bf16[4,40,1024]{2,1,0:T(8,128)(2,1)S(1)}, u32[]{:S(2)}, u32[]{:S(2)}) collective-permute-start(bf16[4,40,1024]{2,1,0:T(8,128)(2,1)S(1)} %pad_maximum_fusion.9), channel_id=1, source_target_pairs={{0,64},{1,65},{2,66},{3,67},{4,68},{5,69},{6,70},{7,71},{64,0},{65... | collective-permute-start | bytes 983048 | tf_op jit(solution)/shard_map/ppermute | solution.py:34
  129.1 17.8 %collective-permute-start.37 = (bf16[4,32,1536]{2,1,0:T(8,128)(2,1)S(1)}, bf16[4,32,1536]{2,1,0:T(8,128)(2,1)S(1)}, u32[]{:S(2)}, u32[]{:S(2)}) collective-permute-start(bf16[4,32,1536]{2,1,0:T(8,128)(2,1)S(1)} %pad_maximum_fusion.7), channel_id=1, source_target_pairs={{0,1},{1,0},{2,3},{3,2},{4,5},{5,4},{6,7},{7,6},{8,9},{9,8},{10,11... | collective-permute-start | bytes 1179656 | tf_op jit(solution)/shard_map/ppermute | solution.py:23
  129.4 17.6 %collective-permute-start.35 = (bf16[2,4,32,1536]{3,2,1,0:T(8,128)(2,1)S(1)}, bf16[2,4,32,1536]{3,2,1,0:T(8,128)(2,1)S(1)}, u32[]{:S(2)}, u32[]{:S(2)}) collective-permute-start(bf16[2,4,32,1536]{3,2,1,0:T(8,128)(2,1)S(1)} %pad_maximum_fusion.4), channel_id=1, source_target_pairs={{0,6},{1,7},{2,0},{3,1},{4,2},{5,3},{6,4},{7,5},{8,14},{9,15},{10,... | collective-permute-start | bytes 2359304 | tf_op jit(solution)/shard_map/ppermute | solution.py:23
  136.7 18.1 %collective-permute-start.36 = (bf16[2,4,32,1536]{3,2,1,0:T(8,128)(2,1)S(1)}, bf16[2,4,32,1536]{3,2,1,0:T(8,128)(2,1)S(1)}, u32[]{:S(2)}, u32[]{:S(2)}) collective-permute-start(bf16[2,4,32,1536]{3,2,1,0:T(8,128)(2,1)S(1)} %pad_maximum_fusion.5), channel_id=1, source_target_pairs={{0,2},{1,3},{2,4},{3,5},{4,6},{5,7},{6,0},{7,1},{8,10},{9,11},{10,... | collective-permute-start | bytes 2359304 | tf_op jit(solution)/shard_map/ppermute | solution.py:23
  137.1 33.2 %collective-permute-start.45 = (bf16[768,1024]{1,0:T(8,128)(2,1)S(1)}, bf16[768,1024]{1,0:T(8,128)(2,1)S(1)}, u32[]{:S(2)}, u32[]{:S(2)}) collective-permute-start(bf16[768,1024]{1,0:T(8,128)(2,1)S(1)} %slice.658), channel_id=1, source_target_pairs={{0,8},{8,0},{16,24},{24,16},{32,40},{40,32},{48,56},{56,48},{1,9},... | collective-permute-start | bytes 4718600 | tf_op jit(solution)/shard_map/ppermute | solution.py:15
  146.9 9.7 %collective-permute-start.42 = (f32[2,8192]{1,0:T(2,128)S(1)}, f32[2,8192]{1,0:T(2,128)S(1)}, u32[]{:S(2)}, u32[]{:S(2)}) collective-permute-start(f32[2,8192]{1,0:T(2,128)S(1)} %fusion.16), channel_id=1, source_target_pairs={{0,32},{8,40},{16,48},{24,56},{32,0},{40,8},{48,16},{56,24},{1,33}... | collective-permute-start | bytes 196616 | tf_op jit(solution)/shard_map/ppermute | solution.py:19
  147.0 9.6 %collective-permute-start.41 = (f32[2,8192]{1,0:T(2,128)S(1)}, f32[2,8192]{1,0:T(2,128)S(1)}, u32[]{:S(2)}, u32[]{:S(2)}) collective-permute-start(f32[2,8192]{1,0:T(2,128)S(1)} %fusion.16), channel_id=1, source_target_pairs={{0,16},{8,24},{16,32},{24,40},{32,48},{40,56},{48,0},{56,8},{1,17}... | collective-permute-start | bytes 196616 | tf_op jit(solution)/shard_map/ppermute | solution.py:19
  (29 other events, 228.1 us)

commit v2 on v1

--- a/solution.py
+++ b/solution.py
@@ -152,14 +152,14 @@
         ]
         for rows in (residual, out_grad)
     ]
-    stream = [sides[0][0], over_both(sides[0][1], 0, 1)]
-    cotangent = [over_both(sides[1][f], -1, f) for f in (0, 1)]
+    stream = [sides[0][0], over_both(after(sides[0][1], half), 0, 1)]
+    cotangent = [over_both(after(sides[1][f], half), -1, f) for f in (0, 1)]
 
     got = {(0, 0): half}
     got[(0, 1)] = over_dp(half, 0, 1)
     got[(3, 0)] = over_dp(half, 3, 0)
-    got[(1, 0)] = over_dp(after(half, cotangent[1]), 1, 0)
-    got[(2, 0)] = over_dp(after(half, cotangent[0], stream[1]), 2, 0)
+    got[(1, 0)] = over_dp(half, 1, 0)
+    got[(2, 0)] = over_dp(after(half, *cotangent, stream[1]), 2, 0)
     for k in (1, 3):
         got[(k, 1)] = over_dp(got[(0, 1)], k, 0)
 
@@ -216,7 +216,6 @@
     )
     gradient = [jnp.stack([c[f, 48:] for c in crossed]) for f in (0, 1)]
     ahead = [over_both(jnp.stack([c[f, :40] for c in crossed]), 1, f) for f in (0, 1)]
-    upstream = to_rows(gradient[0], over_both(gradient[1], 0, 1))
     arrived = to_rows(*ahead)
     normed_rows = arrived[:32]
     sums = arrived[32:].astype(F32)
@@ -235,21 +234,14 @@
         for rows in flowing
     ]
     term = {r: jnp.stack([t[place] for t in terms]) for place, r in enumerate(ORDER)}
-    crossing = over_dp(term[(2, 1)], 0, 1).astype(F32)
+    passing = over_dp(term[(2, 1)], 0, 1)
+    crossing = passing.astype(F32)
     near = [over_dp(jnp.stack([term[(k, 0)], term[(k, 1)]]), -k, 0).astype(F32) for k in (1, 3)]
     far = (term[(2, 0)].astype(F32) + crossing).astype(BF)
     far = over_dp(far, -2, 0).astype(F32)
+    upstream = to_rows(gradient[0], over_both(after(gradient[1], passing), 0, 1))
     other = term[(0, 1)].astype(F32) + near[0][1] + near[1][1]
     other = over_dp(other.astype(BF), 0, 1).astype(F32)
-    context_sum = (term[(0, 0)].astype(F32) + near[0][0] + near[1][0] + far + other).astype(BF)
-    context_sum = after(context_sum, whole)
-    kept, given = context_sum[..., :768], over_core(context_sum[..., 768:])
-    both = jnp.stack([kept, given], axis=1)
-    both = jnp.stack(
-        [lax.dynamic_index_in_dim(both, (y - b) % 4, 0, False) for b in range(4)]
-    )
-    grad_context = jnp.where(core == 0, both, both[:, ::-1]).reshape(256, 768)
-
     spread = jnp.stack(flowing)
     weight_sum = sum(
         lax.dot_general(
@@ -257,7 +249,16 @@
         )
         for g in (0, 1)
     )
-    grad_weight = weight_sum[:768] + over_core(weight_sum[768:].astype(BF)).astype(F32)
+    grad_weight = weight_sum[:768] + over_core(after(weight_sum[768:].astype(BF), passing)).astype(F32)
+    here = after(term[(0, 0)].astype(F32) + near[0][0] + near[1][0], grad_weight)
+    context_sum = (here + far + other).astype(BF)
+    kept, given = context_sum[..., :768], over_core(context_sum[..., 768:])
+    both = jnp.stack([kept, given], axis=1)
+    both = jnp.stack(
+        [lax.dynamic_index_in_dim(both, (y - b) % 4, 0, False) for b in range(4)]
+    )
+    grad_context = jnp.where(core == 0, both, both[:, ::-1]).reshape(256, 768)
+
     return (
         normed_rows[None],
         upstream[None],

time: 173 us -> 160 us (0.925)
  waiting for transfers between devices: 87.6 us -> 79 us
  starting transfers between devices: 55.5 us -> 52.7 us
    ppermute x22, waiting for transfers between devices: 48.2 us -> 28.9 us  [over_dp(): lax.ppermute(value, 'dp', [(j, 2 * (((j >> 1) + steps) % 4) + (j & 1 ^ fl...]
    ppermute x6, waiting for transfers between devices: 8.31 us -> 16 us  [over_both(): return lax.ppermute(value, ('section', 'dp'), pairs)]
    ppermute x22, starting transfers between devices: 17.9 us -> 22.3 us  [over_dp(): lax.ppermute(value, 'dp', [(j, 2 * (((j >> 1) + steps) % 4) + (j & 1 ^ fl...]
    ppermute x12, waiting for transfers between devices: 29 us -> 33 us  [over_y(): lax.ppermute(value, 'mp', [(i, (i + 2 * steps) % 8) for i in range(8)])]
    ppermute x5, starting transfers between devices: 13.3 us -> 9.31 us  [over_core(): return lax.ppermute(value, 'mp', [(i, i ^ 1) for i in range(8)])]
    add x0 -> x2, other arithmetic: none -> 2.8 us  [the longest x1 2.41 us: shards(): weight_sum[:768]]
    broadcast_in_dim x1 -> x0, other arithmetic: 2.41 us -> none  [shards(): grad_weight[None]]
  transfers between devices with their start and end apart: 46 -> 46, of which waited for: 21 -> 25; matrix products, arithmetic and copies ran while one was open for 12% -> 14% of each run, Pallas kernels for 0% -> 0%
where the time goes in v2:
time: 160 us
  waiting for transfers between devices  79 us (49%)
  starting transfers between devices  52.7 us (33%)
  matrix products  12.7 us (8%)
  local copies, waits for them, and re-layouts  6.31 us (4%)
  other arithmetic  6.06 us (4%)
  Pallas kernels  1.71 us (1%)
  between operations  1.64 us (1%)
    ppermute x12, waiting for transfers between devices, over_y(): lax.ppermute(value, 'mp', [(i, (i + 2 * steps) % 8) for i in range(8)])  33 us
    ppermute x22, waiting for transfers between devices, over_dp(): lax.ppermute(value, 'dp', [(j, 2 * (((j >> 1) + steps) % 4) + (j & 1 ^ fl...  28.9 us
    ppermute x22, starting transfers between devices, over_dp(): lax.ppermute(value, 'dp', [(j, 2 * (((j >> 1) + steps) % 4) + (j & 1 ^ fl...  22.3 us
    ppermute x6, waiting for transfers between devices, over_both(): return lax.ppermute(value, ('section', 'dp'), pairs)  16 us
    ppermute x12, starting transfers between devices, over_y(): lax.ppermute(value, 'mp', [(i, (i + 2 * steps) % 8) for i in range(8)])  13.9 us
    ppermute x5, starting transfers between devices, over_core(): return lax.ppermute(value, 'mp', [(i, i ^ 1) for i in range(8)])  9.31 us
    ppermute x6, starting transfers between devices, over_both(): return lax.ppermute(value, ('section', 'dp'), pairs)  7.06 us
    dot_general x4, matrix products, shards(): lax.dot_general(rows.reshape(256, 1024), weights, (((1,), (1,)), ((), ())...  5.47 us
  transfers between devices with their start and end apart: 46, of which 25 were waited for; matrix products, arithmetic and copies ran while one was open for 14% of the time, Pallas kernels for 0%

profile of v2, /device:TPU:1, one launch (start us, length us, event | category | flops | bytes accessed | tf_op | source)
XLA Modules:
  0.0 160.1 jit_solution(2645642602653660412)
XLA Ops:
  4.5 1.8 %collective-permute-start.10 = (bf16[4,32,1024]{2,1,0:T(8,128)(2,1)S(1)}, bf16[4,32,1024]{2,1,0:T(8,128)(2,1)S(1)}, u32[]{:S(2)}, u32[]{:S(2)}) collective-permute-start(bf16[4,32,1024]{2,1,0:T(8,128)(2,1)S(1)} %pad_maximum_fusion.13), channel_id=1, source_target_pairs={{0,1},{1,0},{2,3},{3,2},{4,5},{5,4},{6,7},{7,6},{64,65},{65,64},{6... | collective-permute-start | bytes 786440 | tf_op jit(solution)/shard_map/ppermute | solution.py:34
  6.3 3.3 %collective-permute-start.9 = (bf16[4,32,1024]{2,1,0:T(8,128)(2,1)S(1)}, bf16[4,32,1024]{2,1,0:T(8,128)(2,1)S(1)}, u32[]{:S(2)}, u32[]{:S(2)}) collective-permute-start(bf16[4,32,1024]{2,1,0:T(8,128)(2,1)S(1)} %get-tuple-element.33), channel_id=1, source_target_pairs={{0,64},{1,65},{2,66},{3,67},{4,68},{5,69},{6,70},{7,71},{64,0},{65... | collective-permute-start | bytes 786440 | tf_op jit(solution)/shard_map/ppermute | solution.py:34
  9.6 2.5 %collective-permute-start.3 = (bf16[4,32,1536]{2,1,0:T(8,128)(2,1)S(1)}, bf16[4,32,1536]{2,1,0:T(8,128)(2,1)S(1)}, u32[]{:S(2)}, u32[]{:S(2)}) collective-permute-start(bf16[4,32,1536]{2,1,0:T(8,128)(2,1)S(1)} %pad_maximum_fusion.6), channel_id=1, source_target_pairs={{0,6},{1,7},{2,0},{3,1},{4,2},{5,3},{6,4},{7,5},{8,14},{9,15},{10,... | collective-permute-start | bytes 1179656 | tf_op jit(solution)/shard_map/ppermute | solution.py:23
  13.9 7.5 %collective-permute-done.9 = bf16[4,32,1024]{2,1,0:T(8,128)(2,1)S(1)} collective-permute-done((bf16[4,32,1024]{2,1,0:T(8,128)(2,1)S(1)}, bf16[4,32,1024]{2,1,0:T(8,128)(2,1)S(1)}, u32[]{:S(2)}, u32[]{:S(2)}) %collective-permute-start.9) | collective-permute-done | bytes 262176 | tf_op jit(solution)/shard_map/ppermute | solution.py:34
  21.4 2.0 %collective-permute-done.4 = bf16[4,32,1024]{2,1,0:T(8,128)(2,1)S(1)} collective-permute-done((bf16[4,32,1024]{2,1,0:T(8,128)(2,1)S(1)}, bf16[4,32,1024]{2,1,0:T(8,128)(2,1)S(1)}, u32[]{:S(2)}, u32[]{:S(2)}) %collective-permute-start.4) | collective-permute-done | bytes 262176 | tf_op jit(solution)/shard_map/ppermute | solution.py:34
  23.3 2.7 %collective-permute-start.11 = (bf16[4,32,1536]{2,1,0:T(8,128)(2,1)S(1)}, bf16[4,32,1536]{2,1,0:T(8,128)(2,1)S(1)}, u32[]{:S(2)}, u32[]{:S(2)}) collective-permute-start(bf16[4,32,1536]{2,1,0:T(8,128)(2,1)S(1)} %pad_maximum_fusion.6), channel_id=1, source_target_pairs={{0,4},{1,5},{2,6},{3,7},{4,0},{5,1},{6,2},{7,3},{8,12},{9,13},{10,... | collective-permute-start | bytes 1179656 | tf_op jit(solution)/shard_map/ppermute | solution.py:23
  26.1 2.1 %collective-permute-start.5 = (bf16[768,1024]{1,0:T(8,128)(2,1)S(1)}, bf16[768,1024]{1,0:T(8,128)(2,1)S(1)}, u32[]{:S(2)}, u32[]{:S(2)}) collective-permute-start(bf16[768,1024]{1,0:T(8,128)(2,1)S(1)} %bitcast.238), channel_id=1, source_target_pairs={{0,8},{8,0},{16,24},{24,16},{32,40},{40,32},{48,56},{56,48},{1,9},... | collective-permute-start | bytes 4718600 | tf_op jit(solution)/shard_map/ppermute | solution.py:15
  30.5 3.2 %collective-permute-done.11 = bf16[4,32,1536]{2,1,0:T(8,128)(2,1)S(1)} collective-permute-done((bf16[4,32,1536]{2,1,0:T(8,128)(2,1)S(1)}, bf16[4,32,1536]{2,1,0:T(8,128)(2,1)S(1)}, u32[]{:S(2)}, u32[]{:S(2)}) %collective-permute-start.11) | collective-permute-done | bytes 393248 | tf_op jit(solution)/shard_map/ppermute | solution.py:23
  33.6 1.8 %convolution_convert_fusion.5 = bf16[512,1024]{1,0:T(8,128)(2,1)S(1)} fusion(bf16[512,1536]{1,0:T(8,128)(2,1)S(1)} %bitcast.215, bf16[768,1024]{1,0:T(8,128)(2,1)S(1)} %collective-permute-done.5, bf16[768,1024]{1,0:T(8,128)(2,1)S(1)} %bitcast.239), kind=kOutput, calls=%fused_computation.12 | convolution fusion | flops 1617428480 | bytes 5767168 | tf_op jit(solution)/shard_map/dot_general | solution.py:186
  36.9 6.5 %collective-permute-done.13 = bf16[4,32,1536]{2,1,0:T(8,128)(2,1)S(1)} collective-permute-done((bf16[4,32,1536]{2,1,0:T(8,128)(2,1)S(1)}, bf16[4,32,1536]{2,1,0:T(8,128)(2,1)S(1)}, u32[]{:S(2)}, u32[]{:S(2)}) %collective-permute-start.13) | collective-permute-done | bytes 393248 | tf_op jit(solution)/shard_map/ppermute | solution.py:23
  45.2 2.8 %collective-permute-start.20 = (bf16[2,2,32,1024]{3,2,1,0:T(8,128)(2,1)S(1)}, bf16[2,2,32,1024]{3,2,1,0:T(8,128)(2,1)S(1)}, u32[]{:S(2)}, u32[]{:S(2)}) collective-permute-start(bf16[2,2,32,1024]{3,2,1,0:T(8,128)(2,1)S(1)} %pad_maximum_fusion.17), channel_id=1, source_target_pairs={{0,6},{1,7},{2,0},{3,1},{4,2},{5,3},{6,4},{7,5},{8,14},{9,15},{10,... | collective-permute-start | bytes 786440 | tf_op jit(solution)/shard_map/ppermute | solution.py:23
  48.0 2.9 %collective-permute-start.8 = (bf16[128,1024]{1,0:T(8,128)(2,1)S(1)}, bf16[128,1024]{1,0:T(8,128)(2,1)S(1)}, u32[]{:S(2)}, u32[]{:S(2)}) collective-permute-start(bf16[128,1024]{1,0:T(8,128)(2,1)S(1)} %get-tuple-element.62), channel_id=1, source_target_pairs={{0,32},{8,40},{16,48},{24,56},{32,0},{40,8},{48,16},{56,24},{1,33}... | collective-permute-start | bytes 786440 | tf_op jit(solution)/shard_map/ppermute | solution.py:19
  53.6 2.3 %collective-permute-start.6 = (bf16[128,1024]{1,0:T(8,128)(2,1)S(1)}, bf16[128,1024]{1,0:T(8,128)(2,1)S(1)}, u32[]{:S(2)}, u32[]{:S(2)}) collective-permute-start(bf16[128,1024]{1,0:T(8,128)(2,1)S(1)} %get-tuple-element.64), channel_id=1, source_target_pairs={{0,48},{8,56},{16,0},{24,8},{32,16},{40,24},{48,32},{56,40},{1,49}... | collective-permute-start | bytes 786440 | tf_op jit(solution)/shard_map/ppermute | solution.py:19
  56.2 2.7 %collective-permute-done.20.turned_3 = bf16[2,2,32,1024]{3,2,1,0:T(8,128)(2,1)S(1)} collective-permute-done((bf16[2,2,32,1024]{3,2,1,0:T(8,128)(2,1)S(1)}, bf16[2,2,32,1024]{3,2,1,0:T(8,128)(2,1)S(1)}, u32[]{:S(2)}, u32[]{:S(2)}) %collective-permute-start.20) | collective-permute-done | bytes 262176 | tf_op jit(solution)/shard_map/ppermute | solution.py:23
  61.8 1.8 %collective-permute-done.7.first_2 = bf16[128,1024]{1,0:T(8,128)(2,1)S(1)} collective-permute-done((bf16[128,1024]{1,0:T(8,128)(2,1)S(1)}, bf16[128,1024]{1,0:T(8,128)(2,1)S(1)}, u32[]{:S(2)}, u32[]{:S(2)}) %collective-permute-start.7) | collective-permute-done | bytes 262176 | tf_op jit(solution)/shard_map/ppermute | solution.py:19
  63.6 4.1 %collective-permute-done.17.second_3 = bf16[128,1024]{1,0:T(8,128)(2,1)S(1)} collective-permute-done((bf16[128,1024]{1,0:T(8,128)(2,1)S(1)}, bf16[128,1024]{1,0:T(8,128)(2,1)S(1)}, u32[]{:S(2)}, u32[]{:S(2)}) %collective-permute-start.17) | collective-permute-done | bytes 262176 | tf_op jit(solution)/shard_map/ppermute | solution.py:19
  67.7 6.3 %collective-permute-done.16.second_2 = bf16[128,1024]{1,0:T(8,128)(2,1)S(1)} collective-permute-done((bf16[128,1024]{1,0:T(8,128)(2,1)S(1)}, bf16[128,1024]{1,0:T(8,128)(2,1)S(1)}, u32[]{:S(2)}, u32[]{:S(2)}) %collective-permute-start.16) | collective-permute-done | bytes 262176 | tf_op jit(solution)/shard_map/ppermute | solution.py:19
  75.0 2.6 %collective-permute-done.22 = f32[32,128]{1,0:T(8,128)S(1)} collective-permute-done((f32[32,128]{1,0:T(8,128)S(1)}, f32[32,128]{1,0:T(8,128)S(1)}, u32[]{:S(2)}, u32[]{:S(2)}) %collective-permute-start.22) | collective-permute-done | bytes 16416 | tf_op jit(solution)/shard_map/ppermute | solution.py:23
  80.3 2.4 %collective-permute-done.24.stats_2 = f32[2,32,128]{2,1,0:T(8,128)S(1)} collective-permute-done((f32[2,32,128]{2,1,0:T(8,128)S(1)}, f32[2,32,128]{2,1,0:T(8,128)S(1)}, u32[]{:S(2)}, u32[]{:S(2)}) %collective-permute-start.24) | collective-permute-done | bytes 32800 | tf_op jit(solution)/shard_map/ppermute | solution.py:23
  84.5 2.8 %collective-permute-start.33 = (bf16[8,32,1024]{2,1,0:T(8,128)(2,1)S(1)}, bf16[8,32,1024]{2,1,0:T(8,128)(2,1)S(1)}, u32[]{:S(2)}, u32[]{:S(2)}) collective-permute-start(bf16[8,32,1024]{2,1,0:T(8,128)(2,1)S(1)} %bitcast.209), channel_id=1, source_target_pairs={{0,48},{8,56},{16,0},{24,8},{32,16},{40,24},{48,32},{56,40},{1,49}... | collective-permute-start | bytes 1572872 | tf_op jit(solution)/shard_map/ppermute | solution.py:19
  89.5 2.4 %convolution_convert_fusion.3 = bf16[256,1536]{1,0:T(8,128)(2,1)S(1)} fusion(bf16[256,1024]{1,0:T(8,128)(2,1)S(1)} %get-tuple-element.50, bf16[768,1024]{1,0:T(8,128)(2,1)} %copy-done.13, bf16[768,1024]{1,0:T(8,128)(2,1)S(1)} %bitcast.241), kind=kOutput, calls=%fused_computation.7 | convolution fusion | flops 811991040 | bytes 4456448 | tf_op jit(solution)/shard_map/dot_general | solution.py:229
  92.1 2.2 %collective-permute-done.26 = bf16[2,80,1024]{2,1,0:T(8,128)(2,1)S(1)} collective-permute-done((bf16[2,80,1024]{2,1,0:T(8,128)(2,1)S(1)}, bf16[2,80,1024]{2,1,0:T(8,128)(2,1)S(1)}, u32[]{:S(2)}, u32[]{:S(2)}) %collective-permute-start.26) | collective-permute-done | bytes 327712 | tf_op jit(solution)/shard_map/ppermute | solution.py:23
  94.3 2.6 %collective-permute-done.27 = bf16[2,80,1024]{2,1,0:T(8,128)(2,1)S(1)} collective-permute-done((bf16[2,80,1024]{2,1,0:T(8,128)(2,1)S(1)}, bf16[2,80,1024]{2,1,0:T(8,128)(2,1)S(1)}, u32[]{:S(2)}, u32[]{:S(2)}) %collective-permute-start.27) | collective-permute-done | bytes 327712 | tf_op jit(solution)/shard_map/ppermute | solution.py:23
  97.0 16.5 %collective-permute-done.31 = bf16[8,32,1024]{2,1,0:T(8,128)(2,1)S(1)} collective-permute-done((bf16[8,32,1024]{2,1,0:T(8,128)(2,1)S(1)}, bf16[8,32,1024]{2,1,0:T(8,128)(2,1)S(1)}, u32[]{:S(2)}, u32[]{:S(2)}) %collective-permute-start.31) | collective-permute-done | bytes 524320 | tf_op jit(solution)/shard_map/ppermute | solution.py:19
  124.0 1.8 %fusion.1 = f32[1536,1024,1,1]{1,0,3,2:T(8,128)S(1)} fusion(bf16[4,8,32,1024]{3,2,1,0:T(8,128)(2,1)S(1)} %pad_maximum_fusion.1, bf16[4,1,32,1536]{3,2,1,0:T(8,128)(2,1)S(1)} %bitcast.224, bf16[4,1,32,1536]{3,2,1,0:T(8,128)(2,1)S(1)} %bitcast.226, bf16[4,1,32,1536]{3,2,1,0:T(8,128)(2,1)S(1)} %bitcast.228, bf16[4,1,32,1536]{3,2,1,0:T(8,128)(2,1)S(1)} %copy-done.1), kind=kOutput, calls=%fused_computation.14 | convolution fusion | flops 1612972032 | bytes 8912896 | tf_op jit(solution)/shard_map/dot_general | solution.py:247
  125.8 1.8 %bitcast_add_fusion = f32[1536,1024]{1,0:T(8,128)S(1)} fusion(f32[1536,1024,1,1]{1,0,3,2:T(8,128)S(1)} %fusion.1, bf16[4,8,32,1024]{3,2,1,0:T(8,128)(2,1)S(1)} %pad_maximum_fusion.1, bf16[4,4,32,1536]{3,2,0,1:T(8,128)(2,1)S(1)} %pad_maximum_fusion.3), kind=kOutput, calls=%fused_computation | convolution fusion | flops 1612185600 | bytes 15204352 | tf_op jit(solution)/shard_map/dot_general | solution.py:247
  128.0 5.1 %collective-permute-done.30 = bf16[4,40,1024]{2,1,0:T(8,128)(2,1)S(1)} collective-permute-done((bf16[4,40,1024]{2,1,0:T(8,128)(2,1)S(1)}, bf16[4,40,1024]{2,1,0:T(8,128)(2,1)S(1)}, u32[]{:S(2)}, u32[]{:S(2)}) %collective-permute-start.30) | collective-permute-done | bytes 327712 | tf_op jit(solution)/shard_map/ppermute | solution.py:34
  137.4 1.8 %collective-permute-done.45 = f32[2,8192]{1,0:T(2,128)S(1)} collective-permute-done((f32[2,8192]{1,0:T(2,128)S(1)}, f32[2,8192]{1,0:T(2,128)S(1)}, u32[]{:S(2)}, u32[]{:S(2)}) %collective-permute-start.45) | collective-permute-done | bytes 65568 | tf_op jit(solution)/shard_map/ppermute | solution.py:19
  146.6 2.4 %slice_add_fusion = f32[768,1024]{1,0:T(8,128)} fusion(f32[1536,1024]{1,0:T(8,128)S(1)} %bitcast_add_fusion, bf16[768,1024]{1,0:T(8,128)(2,1)S(1)} %collective-permute-done.38), kind=kLoop, calls=%fused_computation.2 | loop fusion | flops 1572864 | bytes 7864320 | tf_op jit(solution)/shard_map/add | solution.py:252
  149.0 2.1 %collective-permute-done.39 = bf16[4,32,1536]{2,1,0:T(8,128)(2,1)S(1)} collective-permute-done((bf16[4,32,1536]{2,1,0:T(8,128)(2,1)S(1)}, bf16[4,32,1536]{2,1,0:T(8,128)(2,1)S(1)}, u32[]{:S(2)}, u32[]{:S(2)}) %collective-permute-start.39) | collective-permute-done | bytes 393248 | tf_op jit(solution)/shard_map/ppermute | solution.py:23
  151.1 3.1 %collective-permute-done.40 = bf16[4,32,1536]{2,1,0:T(8,128)(2,1)S(1)} collective-permute-done((bf16[4,32,1536]{2,1,0:T(8,128)(2,1)S(1)}, bf16[4,32,1536]{2,1,0:T(8,128)(2,1)S(1)}, u32[]{:S(2)}, u32[]{:S(2)}) %collective-permute-start.40) | collective-permute-done | bytes 393248 | tf_op jit(solution)/shard_map/ppermute | solution.py:23
  154.4 3.7 %collective-permute-start.41 = (bf16[4,32,768]{2,1,0:T(8,128)(2,1)S(1)}, bf16[4,32,768]{2,1,0:T(8,128)(2,1)S(1)}, u32[]{:S(2)}, u32[]{:S(2)}) collective-permute-start(bf16[4,32,768]{2,1,0:T(8,128)(2,1)S(1)} %get-tuple-element.118), channel_id=1, source_target_pairs={{0,8},{8,0},{16,24},{24,16},{32,40},{40,32},{48,56},{56,48},{1,9},... | collective-permute-start | bytes 589832 | tf_op jit(solution)/shard_map/ppermute | solution.py:15
  (191 shorter events, 48.6 us)
Async XLA Ops:
  4.5 8.2 %collective-permute-start.10 = (bf16[4,32,1024]{2,1,0:T(8,128)(2,1)S(1)}, bf16[4,32,1024]{2,1,0:T(8,128)(2,1)S(1)}, u32[]{:S(2)}, u32[]{:S(2)}) collective-permute-start(bf16[4,32,1024]{2,1,0:T(8,128)(2,1)S(1)} %pad_maximum_fusion.13), channel_id=1, source_target_pairs={{0,1},{1,0},{2,3},{3,2},{4,5},{5,4},{6,7},{7,6},{64,65},{65,64},{6... | collective-permute-start | bytes 786440 | tf_op jit(solution)/shard_map/ppermute | solution.py:34
  6.3 15.0 %collective-permute-start.9 = (bf16[4,32,1024]{2,1,0:T(8,128)(2,1)S(1)}, bf16[4,32,1024]{2,1,0:T(8,128)(2,1)S(1)}, u32[]{:S(2)}, u32[]{:S(2)}) collective-permute-start(bf16[4,32,1024]{2,1,0:T(8,128)(2,1)S(1)} %get-tuple-element.33), channel_id=1, source_target_pairs={{0,64},{1,65},{2,66},{3,67},{4,68},{5,69},{6,70},{7,71},{64,0},{65... | collective-permute-start | bytes 786440 | tf_op jit(solution)/shard_map/ppermute | solution.py:34
  9.6 13.7 %collective-permute-start.4 = (bf16[4,32,1024]{2,1,0:T(8,128)(2,1)S(1)}, bf16[4,32,1024]{2,1,0:T(8,128)(2,1)S(1)}, u32[]{:S(2)}, u32[]{:S(2)}) collective-permute-start(bf16[4,32,1024]{2,1,0:T(8,128)(2,1)S(1)} %get-tuple-element.31), channel_id=1, source_target_pairs={{0,65},{1,64},{2,67},{3,66},{4,69},{5,68},{6,71},{7,70},{64,1},{65... | collective-permute-start | bytes 786440 | tf_op jit(solution)/shard_map/ppermute | solution.py:34
  9.6 18.9 %collective-permute-start.3 = (bf16[4,32,1536]{2,1,0:T(8,128)(2,1)S(1)}, bf16[4,32,1536]{2,1,0:T(8,128)(2,1)S(1)}, u32[]{:S(2)}, u32[]{:S(2)}) collective-permute-start(bf16[4,32,1536]{2,1,0:T(8,128)(2,1)S(1)} %pad_maximum_fusion.6), channel_id=1, source_target_pairs={{0,6},{1,7},{2,0},{3,1},{4,2},{5,3},{6,4},{7,5},{8,14},{9,15},{10,... | collective-permute-start | bytes 1179656 | tf_op jit(solution)/shard_map/ppermute | solution.py:23
  12.2 17.5 %collective-permute-start.2 = (bf16[4,32,1536]{2,1,0:T(8,128)(2,1)S(1)}, bf16[4,32,1536]{2,1,0:T(8,128)(2,1)S(1)}, u32[]{:S(2)}, u32[]{:S(2)}) collective-permute-start(bf16[4,32,1536]{2,1,0:T(8,128)(2,1)S(1)} %pad_maximum_fusion.6), channel_id=1, source_target_pairs={{0,2},{1,3},{2,4},{3,5},{4,6},{5,7},{6,0},{7,1},{8,10},{9,11},{10,... | collective-permute-start | bytes 1179656 | tf_op jit(solution)/shard_map/ppermute | solution.py:23
  12.7 16.0 %collective-permute-start.1 = (bf16[4,32,1536]{2,1,0:T(8,128)(2,1)S(1)}, bf16[4,32,1536]{2,1,0:T(8,128)(2,1)S(1)}, u32[]{:S(2)}, u32[]{:S(2)}) collective-permute-start(bf16[4,32,1536]{2,1,0:T(8,128)(2,1)S(1)} %pad_maximum_fusion.6), channel_id=1, source_target_pairs={{0,1},{1,0},{2,3},{3,2},{4,5},{5,4},{6,7},{7,6},{8,9},{9,8},{10,11... | collective-permute-start | bytes 1179656 | tf_op jit(solution)/shard_map/ppermute | solution.py:23
  23.3 10.3 %collective-permute-start.11 = (bf16[4,32,1536]{2,1,0:T(8,128)(2,1)S(1)}, bf16[4,32,1536]{2,1,0:T(8,128)(2,1)S(1)}, u32[]{:S(2)}, u32[]{:S(2)}) collective-permute-start(bf16[4,32,1536]{2,1,0:T(8,128)(2,1)S(1)} %pad_maximum_fusion.6), channel_id=1, source_target_pairs={{0,4},{1,5},{2,6},{3,7},{4,0},{5,1},{6,2},{7,3},{8,12},{9,13},{10,... | collective-permute-start | bytes 1179656 | tf_op jit(solution)/shard_map/ppermute | solution.py:23
  26.1 7.5 %collective-permute-start.5 = (bf16[768,1024]{1,0:T(8,128)(2,1)S(1)}, bf16[768,1024]{1,0:T(8,128)(2,1)S(1)}, u32[]{:S(2)}, u32[]{:S(2)}) collective-permute-start(bf16[768,1024]{1,0:T(8,128)(2,1)S(1)} %bitcast.238), channel_id=1, source_target_pairs={{0,8},{8,0},{16,24},{24,16},{32,40},{40,32},{48,56},{56,48},{1,9},... | collective-permute-start | bytes 4718600 | tf_op jit(solution)/shard_map/ppermute | solution.py:15
  28.6 24.5 %collective-permute-start.21 = (f32[2,1024]{1,0:T(2,128)S(1)}, f32[2,1024]{1,0:T(2,128)S(1)}, u32[]{:S(2)}, u32[]{:S(2)}) collective-permute-start(f32[2,1024]{1,0:T(2,128)S(1)} %pad_maximum_fusion.23), channel_id=1, source_target_pairs={{0,64},{64,0},{1,65},{65,1},{2,66},{66,2},{3,67},{67,3},{4,68},{68... | collective-permute-start | bytes 24584 | tf_op jit(solution)/shard_map/ppermute | solution.py:29
  28.7 14.7 %collective-permute-start.13 = (bf16[4,32,1536]{2,1,0:T(8,128)(2,1)S(1)}, bf16[4,32,1536]{2,1,0:T(8,128)(2,1)S(1)}, u32[]{:S(2)}, u32[]{:S(2)}) collective-permute-start(bf16[4,32,1536]{2,1,0:T(8,128)(2,1)S(1)} %collective-permute-done.1), channel_id=1, source_target_pairs={{0,6},{1,7},{2,0},{3,1},{4,2},{5,3},{6,4},{7,5},{8,14},{9,15},{10,... | collective-permute-start | bytes 1179656 | tf_op jit(solution)/shard_map/ppermute | solution.py:23
  29.6 15.5 %collective-permute-start.12 = (bf16[4,32,1536]{2,1,0:T(8,128)(2,1)S(1)}, bf16[4,32,1536]{2,1,0:T(8,128)(2,1)S(1)}, u32[]{:S(2)}, u32[]{:S(2)}) collective-permute-start(bf16[4,32,1536]{2,1,0:T(8,128)(2,1)S(1)} %collective-permute-done.1), channel_id=1, source_target_pairs={{0,2},{1,3},{2,4},{3,5},{4,6},{5,7},{6,0},{7,1},{8,10},{9,11},{10,... | collective-permute-start | bytes 1179656 | tf_op jit(solution)/shard_map/ppermute | solution.py:23
  33.6 14.3 %collective-permute-start.14 = (bf16[4,32,1536]{2,1,0:T(8,128)(2,1)S(1)}, bf16[4,32,1536]{2,1,0:T(8,128)(2,1)S(1)}, u32[]{:S(2)}, u32[]{:S(2)}) collective-permute-start(bf16[4,32,1536]{2,1,0:T(8,128)(2,1)S(1)} %collective-permute-done.11), channel_id=1, source_target_pairs={{0,1},{1,0},{2,3},{3,2},{4,5},{5,4},{6,7},{7,6},{8,9},{9,8},{10,11... | collective-permute-start | bytes 1179656 | tf_op jit(solution)/shard_map/ppermute | solution.py:23
  35.5 18.0 %collective-permute-start.18 = (bf16[2,2,32,1024]{3,2,1,0:T(8,128)(2,1)S(1)}, bf16[2,2,32,1024]{3,2,1,0:T(8,128)(2,1)S(1)}, u32[]{:S(2)}, u32[]{:S(2)}) collective-permute-start(bf16[2,2,32,1024]{3,2,1,0:T(8,128)(2,1)S(1)} %pad_maximum_fusion.15), channel_id=1, source_target_pairs={{0,2},{1,3},{2,4},{3,5},{4,6},{5,7},{6,0},{7,1},{8,10},{9,11},{10,... | collective-permute-start | bytes 786440 | tf_op jit(solution)/shard_map/ppermute | solution.py:23
  43.4 12.5 %collective-permute-start.19 = (bf16[2,2,32,1024]{3,2,1,0:T(8,128)(2,1)S(1)}, bf16[2,2,32,1024]{3,2,1,0:T(8,128)(2,1)S(1)}, u32[]{:S(2)}, u32[]{:S(2)}) collective-permute-start(bf16[2,2,32,1024]{3,2,1,0:T(8,128)(2,1)S(1)} %pad_maximum_fusion.16), channel_id=1, source_target_pairs={{0,4},{1,5},{2,6},{3,7},{4,0},{5,1},{6,2},{7,3},{8,12},{9,13},{10,... | collective-permute-start | bytes 786440 | tf_op jit(solution)/shard_map/ppermute | solution.py:23
  45.2 13.8 %collective-permute-start.20 = (bf16[2,2,32,1024]{3,2,1,0:T(8,128)(2,1)S(1)}, bf16[2,2,32,1024]{3,2,1,0:T(8,128)(2,1)S(1)}, u32[]{:S(2)}, u32[]{:S(2)}) collective-permute-start(bf16[2,2,32,1024]{3,2,1,0:T(8,128)(2,1)S(1)} %pad_maximum_fusion.17), channel_id=1, source_target_pairs={{0,6},{1,7},{2,0},{3,1},{4,2},{5,3},{6,4},{7,5},{8,14},{9,15},{10,... | collective-permute-start | bytes 786440 | tf_op jit(solution)/shard_map/ppermute | solution.py:23
  48.0 12.3 %collective-permute-start.8 = (bf16[128,1024]{1,0:T(8,128)(2,1)S(1)}, bf16[128,1024]{1,0:T(8,128)(2,1)S(1)}, u32[]{:S(2)}, u32[]{:S(2)}) collective-permute-start(bf16[128,1024]{1,0:T(8,128)(2,1)S(1)} %get-tuple-element.62), channel_id=1, source_target_pairs={{0,32},{8,40},{16,48},{24,56},{32,0},{40,8},{48,16},{56,24},{1,33}... | collective-permute-start | bytes 786440 | tf_op jit(solution)/shard_map/ppermute | solution.py:19
  53.1 10.5 %collective-permute-start.7 = (bf16[128,1024]{1,0:T(8,128)(2,1)S(1)}, bf16[128,1024]{1,0:T(8,128)(2,1)S(1)}, u32[]{:S(2)}, u32[]{:S(2)}) collective-permute-start(bf16[128,1024]{1,0:T(8,128)(2,1)S(1)} %get-tuple-element.63), channel_id=1, source_target_pairs={{0,16},{8,24},{16,32},{24,40},{32,48},{40,56},{48,0},{56,8},{1,17}... | collective-permute-start | bytes 786440 | tf_op jit(solution)/shard_map/ppermute | solution.py:19
  53.6 10.0 %collective-permute-start.6 = (bf16[128,1024]{1,0:T(8,128)(2,1)S(1)}, bf16[128,1024]{1,0:T(8,128)(2,1)S(1)}, u32[]{:S(2)}, u32[]{:S(2)}) collective-permute-start(bf16[128,1024]{1,0:T(8,128)(2,1)S(1)} %get-tuple-element.64), channel_id=1, source_target_pairs={{0,48},{8,56},{16,0},{24,8},{32,16},{40,24},{48,32},{56,40},{1,49}... | collective-permute-start | bytes 786440 | tf_op jit(solution)/shard_map/ppermute | solution.py:19
  55.9 11.9 %collective-permute-start.17 = (bf16[128,1024]{1,0:T(8,128)(2,1)S(1)}, bf16[128,1024]{1,0:T(8,128)(2,1)S(1)}, u32[]{:S(2)}, u32[]{:S(2)}) collective-permute-start(bf16[128,1024]{1,0:T(8,128)(2,1)S(1)} %get-tuple-element.58), channel_id=1, source_target_pairs={{0,32},{8,40},{16,48},{24,56},{32,0},{40,8},{48,16},{56,24},{1,33}... | collective-permute-start | bytes 786440 | tf_op jit(solution)/shard_map/ppermute | solution.py:19
  59.0 15.1 %collective-permute-start.16 = (bf16[128,1024]{1,0:T(8,128)(2,1)S(1)}, bf16[128,1024]{1,0:T(8,128)(2,1)S(1)}, u32[]{:S(2)}, u32[]{:S(2)}) collective-permute-start(bf16[128,1024]{1,0:T(8,128)(2,1)S(1)} %get-tuple-element.59), channel_id=1, source_target_pairs={{0,16},{8,24},{16,32},{24,40},{32,48},{40,56},{48,0},{56,8},{1,17}... | collective-permute-start | bytes 786440 | tf_op jit(solution)/shard_map/ppermute | solution.py:19
  60.3 13.8 %collective-permute-start.15 = (bf16[128,1024]{1,0:T(8,128)(2,1)S(1)}, bf16[128,1024]{1,0:T(8,128)(2,1)S(1)}, u32[]{:S(2)}, u32[]{:S(2)}) collective-permute-start(bf16[128,1024]{1,0:T(8,128)(2,1)S(1)} %get-tuple-element.60), channel_id=1, source_target_pairs={{0,48},{8,56},{16,0},{24,8},{32,16},{40,24},{48,32},{56,40},{1,49}... | collective-permute-start | bytes 786440 | tf_op jit(solution)/shard_map/ppermute | solution.py:19
  84.5 30.1 %collective-permute-start.33 = (bf16[8,32,1024]{2,1,0:T(8,128)(2,1)S(1)}, bf16[8,32,1024]{2,1,0:T(8,128)(2,1)S(1)}, u32[]{:S(2)}, u32[]{:S(2)}) collective-permute-start(bf16[8,32,1024]{2,1,0:T(8,128)(2,1)S(1)} %bitcast.209), channel_id=1, source_target_pairs={{0,48},{8,56},{16,0},{24,8},{32,16},{40,24},{48,32},{56,40},{1,49}... | collective-permute-start | bytes 1572872 | tf_op jit(solution)/shard_map/ppermute | solution.py:19
  87.3 30.5 %collective-permute-start.32 = (bf16[8,32,1024]{2,1,0:T(8,128)(2,1)S(1)}, bf16[8,32,1024]{2,1,0:T(8,128)(2,1)S(1)}, u32[]{:S(2)}, u32[]{:S(2)}) collective-permute-start(bf16[8,32,1024]{2,1,0:T(8,128)(2,1)S(1)} %bitcast.210), channel_id=1, source_target_pairs={{0,32},{8,40},{16,48},{24,56},{32,0},{40,8},{48,16},{56,24},{1,33}... | collective-permute-start | bytes 1572872 | tf_op jit(solution)/shard_map/ppermute | solution.py:19
  87.4 26.1 %collective-permute-start.31 = (bf16[8,32,1024]{2,1,0:T(8,128)(2,1)S(1)}, bf16[8,32,1024]{2,1,0:T(8,128)(2,1)S(1)}, u32[]{:S(2)}, u32[]{:S(2)}) collective-permute-start(bf16[8,32,1024]{2,1,0:T(8,128)(2,1)S(1)} %bitcast.211), channel_id=1, source_target_pairs={{0,16},{8,24},{16,32},{24,40},{32,48},{40,56},{48,0},{56,8},{1,17}... | collective-permute-start | bytes 1572872 | tf_op jit(solution)/shard_map/ppermute | solution.py:19
  96.9 18.8 %collective-permute-start.28 = (bf16[2,80,1024]{2,1,0:T(8,128)(2,1)S(1)}, bf16[2,80,1024]{2,1,0:T(8,128)(2,1)S(1)}, u32[]{:S(2)}, u32[]{:S(2)}) collective-permute-start(bf16[2,80,1024]{2,1,0:T(8,128)(2,1)S(1)} %get-tuple-element.49), channel_id=1, source_target_pairs={{0,4},{1,5},{2,6},{3,7},{4,0},{5,1},{6,2},{7,3},{8,12},{9,13},{10,... | collective-permute-start | bytes 983048 | tf_op jit(solution)/shard_map/ppermute | solution.py:23
  115.7 17.4 %collective-permute-start.30 = (bf16[4,40,1024]{2,1,0:T(8,128)(2,1)S(1)}, bf16[4,40,1024]{2,1,0:T(8,128)(2,1)S(1)}, u32[]{:S(2)}, u32[]{:S(2)}) collective-permute-start(bf16[4,40,1024]{2,1,0:T(8,128)(2,1)S(1)} %pad_maximum_fusion.10), channel_id=1, source_target_pairs={{0,65},{1,64},{2,67},{3,66},{4,69},{5,68},{6,71},{7,70},{64,1},{65... | collective-permute-start | bytes 983048 | tf_op jit(solution)/shard_map/ppermute | solution.py:34
  116.0 17.1 %collective-permute-start.29 = (bf16[4,40,1024]{2,1,0:T(8,128)(2,1)S(1)}, bf16[4,40,1024]{2,1,0:T(8,128)(2,1)S(1)}, u32[]{:S(2)}, u32[]{:S(2)}) collective-permute-start(bf16[4,40,1024]{2,1,0:T(8,128)(2,1)S(1)} %pad_maximum_fusion.9), channel_id=1, source_target_pairs={{0,64},{1,65},{2,66},{3,67},{4,68},{5,69},{6,70},{7,71},{64,0},{65... | collective-permute-start | bytes 983048 | tf_op jit(solution)/shard_map/ppermute | solution.py:34
  118.9 17.5 %collective-permute-start.34 = (bf16[4,32,1536]{2,1,0:T(8,128)(2,1)S(1)}, bf16[4,32,1536]{2,1,0:T(8,128)(2,1)S(1)}, u32[]{:S(2)}, u32[]{:S(2)}) collective-permute-start(bf16[4,32,1536]{2,1,0:T(8,128)(2,1)S(1)} %pad_maximum_fusion.7), channel_id=1, source_target_pairs={{0,1},{1,0},{2,3},{3,2},{4,5},{5,4},{6,7},{7,6},{8,9},{9,8},{10,11... | collective-permute-start | bytes 1179656 | tf_op jit(solution)/shard_map/ppermute | solution.py:23
  120.6 24.8 %collective-permute-start.36 = (bf16[2,4,32,1536]{3,2,1,0:T(8,128)(2,1)S(1)}, bf16[2,4,32,1536]{3,2,1,0:T(8,128)(2,1)S(1)}, u32[]{:S(2)}, u32[]{:S(2)}) collective-permute-start(bf16[2,4,32,1536]{3,2,1,0:T(8,128)(2,1)S(1)} %pad_maximum_fusion.4), channel_id=1, source_target_pairs={{0,6},{1,7},{2,0},{3,1},{4,2},{5,3},{6,4},{7,5},{8,14},{9,15},{10,... | collective-permute-start | bytes 2359304 | tf_op jit(solution)/shard_map/ppermute | solution.py:23
  122.1 23.5 %collective-permute-start.37 = (bf16[2,4,32,1536]{3,2,1,0:T(8,128)(2,1)S(1)}, bf16[2,4,32,1536]{3,2,1,0:T(8,128)(2,1)S(1)}, u32[]{:S(2)}, u32[]{:S(2)}) collective-permute-start(bf16[2,4,32,1536]{3,2,1,0:T(8,128)(2,1)S(1)} %pad_maximum_fusion.5), channel_id=1, source_target_pairs={{0,2},{1,3},{2,4},{3,5},{4,6},{5,7},{6,0},{7,1},{8,10},{9,11},{10,... | collective-permute-start | bytes 2359304 | tf_op jit(solution)/shard_map/ppermute | solution.py:23
  140.6 10.5 %collective-permute-start.39 = (bf16[4,32,1536]{2,1,0:T(8,128)(2,1)S(1)}, bf16[4,32,1536]{2,1,0:T(8,128)(2,1)S(1)}, u32[]{:S(2)}, u32[]{:S(2)}) collective-permute-start(bf16[4,32,1536]{2,1,0:T(8,128)(2,1)S(1)} %add_convert_fusion.1), channel_id=1, source_target_pairs={{0,4},{1,5},{2,6},{3,7},{4,0},{5,1},{6,2},{7,3},{8,12},{9,13},{10,... | collective-permute-start | bytes 1179656 | tf_op jit(solution)/shard_map/ppermute | solution.py:23
  146.2 8.0 %collective-permute-start.40 = (bf16[4,32,1536]{2,1,0:T(8,128)(2,1)S(1)}, bf16[4,32,1536]{2,1,0:T(8,128)(2,1)S(1)}, u32[]{:S(2)}, u32[]{:S(2)}) collective-permute-start(bf16[4,32,1536]{2,1,0:T(8,128)(2,1)S(1)} %get-tuple-element.57), channel_id=1, source_target_pairs={{0,1},{1,0},{2,3},{3,2},{4,5},{5,4},{6,7},{7,6},{8,9},{9,8},{10,11... | collective-permute-start | bytes 1179656 | tf_op jit(solution)/shard_map/ppermute | solution.py:23
  (29 other events, 167.4 us)

commit v3 on v2

--- a/solution.py
+++ b/solution.py
@@ -166,7 +166,6 @@
     weight_own = out_weight[0]
     weight_other = over_core(after(weight_own, cotangent[1]))
     weights = jnp.concatenate([weight_own, weight_other], axis=0)
-    got[(2, 1)] = over_dp(after(got[(2, 0)], weight_other), 0, 1)
     columns = jnp.concatenate(
         [
             lax.dynamic_slice_in_dim(ln_gain, dp * 1024, 1024, 1),
@@ -175,6 +174,7 @@
         axis=0,
     )
     columns = over_section(after(columns, got[(3, 0)]), -1)
+    got[(2, 1)] = over_dp(after(got[(2, 0)], weight_other, columns), 0, 1)
     gain, bias = columns[:1], columns[1:]
 
     attended, tokens = [], []
@@ -188,7 +188,7 @@
         attended += [part[0]] + [over_y(part[k], -k) for k in (1, 3, 2)]
 
     mixed = [jnp.stack([jnp.stack([stream[f][k], cotangent[f][k]]) for f in (0, 1)]) for k in range(4)]
-    turned = [mixed[0]] + [over_dp(after(mixed[k], attended[0]), k, 0) for k in (1, 2, 3)]
+    turned = [mixed[0]] + [over_dp(after(mixed[k], attended[4]), k, 0) for k in (1, 2, 3)]
 
     line = jax.ShapeDtypeStruct((32, LANES), F32)
     rows_here = jax.ShapeDtypeStruct((256, 1024), BF)
@@ -239,7 +239,7 @@
     near = [over_dp(jnp.stack([term[(k, 0)], term[(k, 1)]]), -k, 0).astype(F32) for k in (1, 3)]
     far = (term[(2, 0)].astype(F32) + crossing).astype(BF)
     far = over_dp(far, -2, 0).astype(F32)
-    upstream = to_rows(gradient[0], over_both(after(gradient[1], passing), 0, 1))
+    upstream = to_rows(gradient[0], after(over_both(after(gradient[1], passing), 0, 1), near[0], near[1]))
     other = term[(0, 1)].astype(F32) + near[0][1] + near[1][1]
     other = over_dp(other.astype(BF), 0, 1).astype(F32)
     spread = jnp.stack(flowing)

time: 160 us -> 154 us (0.963)
  waiting for transfers between devices: 79 us -> 73.4 us
    ppermute x12, waiting for transfers between devices: 33 us -> 25.1 us  [over_y(): lax.ppermute(value, 'mp', [(i, (i + 2 * steps) % 8) for i in range(8)])]
    ppermute x12, starting transfers between devices: 13.9 us -> 11.2 us  [over_y(): lax.ppermute(value, 'mp', [(i, (i + 2 * steps) % 8) for i in range(8)])]
    ppermute x1, waiting for transfers between devices: 0.01 us -> 2.05 us  [over_section(): lax.ppermute(value, 'section', [(s, (s + steps) % 2) for s in range(2)])]
where the time goes in v3:
time: 154 us
  waiting for transfers between devices  73.4 us (48%)
  starting transfers between devices  51.3 us (33%)
  matrix products  12.7 us (8%)
  local copies, waits for them, and re-layouts  6.81 us (4%)
  other arithmetic  6.04 us (4%)
  Pallas kernels  1.71 us (1%)
  between operations  1.66 us (1%)
    ppermute x22, waiting for transfers between devices, over_dp(): lax.ppermute(value, 'dp', [(j, 2 * (((j >> 1) + steps) % 4) + (j & 1 ^ fl...  29.2 us
    ppermute x12, waiting for transfers between devices, over_y(): lax.ppermute(value, 'mp', [(i, (i + 2 * steps) % 8) for i in range(8)])  25.1 us
    ppermute x22, starting transfers between devices, over_dp(): lax.ppermute(value, 'dp', [(j, 2 * (((j >> 1) + steps) % 4) + (j & 1 ^ fl...  23.5 us
    ppermute x6, waiting for transfers between devices, over_both(): return lax.ppermute(value, ('section', 'dp'), pairs)  15.5 us
    ppermute x12, starting transfers between devices, over_y(): lax.ppermute(value, 'mp', [(i, (i + 2 * steps) % 8) for i in range(8)])  11.2 us
    ppermute x5, starting transfers between devices, over_core(): return lax.ppermute(value, 'mp', [(i, i ^ 1) for i in range(8)])  9.42 us
    ppermute x6, starting transfers between devices, over_both(): return lax.ppermute(value, ('section', 'dp'), pairs)  7.05 us
    dot_general x4, matrix products, shards(): lax.dot_general(rows.reshape(256, 1024), weights, (((1,), (1,)), ((), ())...  5.46 us
  transfers between devices with their start and end apart: 46, of which 25 were waited for; matrix products, arithmetic and copies ran while one was open for 14% of the time, Pallas kernels for 0%

profile of v3, /device:TPU:1, one launch (start us, length us, event | category | flops | bytes accessed | tf_op | source)
XLA Modules:
  0.0 153.7 jit_solution(13367422101767908652)
XLA Ops:
  4.5 1.8 %collective-permute-start.10 = (bf16[4,32,1024]{2,1,0:T(8,128)(2,1)S(1)}, bf16[4,32,1024]{2,1,0:T(8,128)(2,1)S(1)}, u32[]{:S(2)}, u32[]{:S(2)}) collective-permute-start(bf16[4,32,1024]{2,1,0:T(8,128)(2,1)S(1)} %pad_maximum_fusion.13), channel_id=1, source_target_pairs={{0,1},{1,0},{2,3},{3,2},{4,5},{5,4},{6,7},{7,6},{64,65},{65,64},{6... | collective-permute-start | bytes 786440 | tf_op jit(solution)/shard_map/ppermute | solution.py:34
  6.3 3.3 %collective-permute-start.9 = (bf16[4,32,1024]{2,1,0:T(8,128)(2,1)S(1)}, bf16[4,32,1024]{2,1,0:T(8,128)(2,1)S(1)}, u32[]{:S(2)}, u32[]{:S(2)}) collective-permute-start(bf16[4,32,1024]{2,1,0:T(8,128)(2,1)S(1)} %get-tuple-element.34), channel_id=1, source_target_pairs={{0,64},{1,65},{2,66},{3,67},{4,68},{5,69},{6,70},{7,71},{64,0},{65... | collective-permute-start | bytes 786440 | tf_op jit(solution)/shard_map/ppermute | solution.py:34
  9.6 2.5 %collective-permute-start.3 = (bf16[4,32,1536]{2,1,0:T(8,128)(2,1)S(1)}, bf16[4,32,1536]{2,1,0:T(8,128)(2,1)S(1)}, u32[]{:S(2)}, u32[]{:S(2)}) collective-permute-start(bf16[4,32,1536]{2,1,0:T(8,128)(2,1)S(1)} %pad_maximum_fusion.6), channel_id=1, source_target_pairs={{0,6},{1,7},{2,0},{3,1},{4,2},{5,3},{6,4},{7,5},{8,14},{9,15},{10,... | collective-permute-start | bytes 1179656 | tf_op jit(solution)/shard_map/ppermute | solution.py:23
  13.9 7.5 %collective-permute-done.9 = bf16[4,32,1024]{2,1,0:T(8,128)(2,1)S(1)} collective-permute-done((bf16[4,32,1024]{2,1,0:T(8,128)(2,1)S(1)}, bf16[4,32,1024]{2,1,0:T(8,128)(2,1)S(1)}, u32[]{:S(2)}, u32[]{:S(2)}) %collective-permute-start.9) | collective-permute-done | bytes 262176 | tf_op jit(solution)/shard_map/ppermute | solution.py:34
  21.4 2.0 %collective-permute-done.4 = bf16[4,32,1024]{2,1,0:T(8,128)(2,1)S(1)} collective-permute-done((bf16[4,32,1024]{2,1,0:T(8,128)(2,1)S(1)}, bf16[4,32,1024]{2,1,0:T(8,128)(2,1)S(1)}, u32[]{:S(2)}, u32[]{:S(2)}) %collective-permute-start.4) | collective-permute-done | bytes 262176 | tf_op jit(solution)/shard_map/ppermute | solution.py:34
  23.3 2.7 %collective-permute-start.11 = (bf16[4,32,1536]{2,1,0:T(8,128)(2,1)S(1)}, bf16[4,32,1536]{2,1,0:T(8,128)(2,1)S(1)}, u32[]{:S(2)}, u32[]{:S(2)}) collective-permute-start(bf16[4,32,1536]{2,1,0:T(8,128)(2,1)S(1)} %pad_maximum_fusion.6), channel_id=1, source_target_pairs={{0,4},{1,5},{2,6},{3,7},{4,0},{5,1},{6,2},{7,3},{8,12},{9,13},{10,... | collective-permute-start | bytes 1179656 | tf_op jit(solution)/shard_map/ppermute | solution.py:23
  26.1 2.1 %collective-permute-start.5 = (bf16[768,1024]{1,0:T(8,128)(2,1)S(1)}, bf16[768,1024]{1,0:T(8,128)(2,1)S(1)}, u32[]{:S(2)}, u32[]{:S(2)}) collective-permute-start(bf16[768,1024]{1,0:T(8,128)(2,1)S(1)} %bitcast.238), channel_id=1, source_target_pairs={{0,8},{8,0},{16,24},{24,16},{32,40},{40,32},{48,56},{56,48},{1,9},... | collective-permute-start | bytes 4718600 | tf_op jit(solution)/shard_map/ppermute | solution.py:15
  30.8 2.0 %collective-permute-done.14 = f32[2,1024]{1,0:T(2,128)S(1)} collective-permute-done((f32[2,1024]{1,0:T(2,128)S(1)}, f32[2,1024]{1,0:T(2,128)S(1)}, u32[]{:S(2)}, u32[]{:S(2)}) %collective-permute-start.14) | collective-permute-done | bytes 8224 | tf_op jit(solution)/shard_map/ppermute | solution.py:29
  33.6 1.8 %convolution_convert_fusion.5 = bf16[512,1024]{1,0:T(8,128)(2,1)S(1)} fusion(bf16[512,1536]{1,0:T(8,128)(2,1)S(1)} %bitcast.215, bf16[768,1024]{1,0:T(8,128)(2,1)S(1)} %collective-permute-done.5, bf16[768,1024]{1,0:T(8,128)(2,1)S(1)} %bitcast.239), kind=kOutput, calls=%fused_computation.12 | convolution fusion | flops 1617428480 | bytes 5767168 | tf_op jit(solution)/shard_map/dot_general | solution.py:186
  35.5 3.0 %collective-permute-start.8 = (bf16[128,1024]{1,0:T(8,128)(2,1)S(1)}, bf16[128,1024]{1,0:T(8,128)(2,1)S(1)}, u32[]{:S(2)}, u32[]{:S(2)}) collective-permute-start(bf16[128,1024]{1,0:T(8,128)(2,1)S(1)} %get-tuple-element.64), channel_id=1, source_target_pairs={{0,32},{8,40},{16,48},{24,56},{32,0},{40,8},{48,16},{56,24},{1,33}... | collective-permute-start | bytes 786440 | tf_op jit(solution)/shard_map/ppermute | solution.py:19
  38.9 4.5 %collective-permute-done.13 = bf16[4,32,1536]{2,1,0:T(8,128)(2,1)S(1)} collective-permute-done((bf16[4,32,1536]{2,1,0:T(8,128)(2,1)S(1)}, bf16[4,32,1536]{2,1,0:T(8,128)(2,1)S(1)}, u32[]{:S(2)}, u32[]{:S(2)}) %collective-permute-start.13) | collective-permute-done | bytes 393248 | tf_op jit(solution)/shard_map/ppermute | solution.py:23
  43.4 2.7 %collective-permute-start.6 = (bf16[128,1024]{1,0:T(8,128)(2,1)S(1)}, bf16[128,1024]{1,0:T(8,128)(2,1)S(1)}, u32[]{:S(2)}, u32[]{:S(2)}) collective-permute-start(bf16[128,1024]{1,0:T(8,128)(2,1)S(1)} %get-tuple-element.66), channel_id=1, source_target_pairs={{0,48},{8,56},{16,0},{24,8},{32,16},{40,24},{48,32},{56,40},{1,49}... | collective-permute-start | bytes 786440 | tf_op jit(solution)/shard_map/ppermute | solution.py:19
  48.4 2.2 %collective-permute-start.19 = (bf16[2,2,32,1024]{3,2,1,0:T(8,128)(2,1)S(1)}, bf16[2,2,32,1024]{3,2,1,0:T(8,128)(2,1)S(1)}, u32[]{:S(2)}, u32[]{:S(2)}) collective-permute-start(bf16[2,2,32,1024]{3,2,1,0:T(8,128)(2,1)S(1)} %pad_maximum_fusion.15), channel_id=1, source_target_pairs={{0,2},{1,3},{2,4},{3,5},{4,6},{5,7},{6,0},{7,1},{8,10},{9,11},{10,... | collective-permute-start | bytes 786440 | tf_op jit(solution)/shard_map/ppermute | solution.py:23
  50.7 2.5 %collective-permute-start.20 = (bf16[2,2,32,1024]{3,2,1,0:T(8,128)(2,1)S(1)}, bf16[2,2,32,1024]{3,2,1,0:T(8,128)(2,1)S(1)}, u32[]{:S(2)}, u32[]{:S(2)}) collective-permute-start(bf16[2,2,32,1024]{3,2,1,0:T(8,128)(2,1)S(1)} %pad_maximum_fusion.16), channel_id=1, source_target_pairs={{0,4},{1,5},{2,6},{3,7},{4,0},{5,1},{6,2},{7,3},{8,12},{9,13},{10,... | collective-permute-start | bytes 786440 | tf_op jit(solution)/shard_map/ppermute | solution.py:23
  54.9 2.2 %collective-permute-done.19.turned_1 = bf16[2,2,32,1024]{3,2,1,0:T(8,128)(2,1)S(1)} collective-permute-done((bf16[2,2,32,1024]{3,2,1,0:T(8,128)(2,1)S(1)}, bf16[2,2,32,1024]{3,2,1,0:T(8,128)(2,1)S(1)}, u32[]{:S(2)}, u32[]{:S(2)}) %collective-permute-start.19) | collective-permute-done | bytes 262176 | tf_op jit(solution)/shard_map/ppermute | solution.py:23
  57.3 7.0 %collective-permute-done.20.turned_2 = bf16[2,2,32,1024]{3,2,1,0:T(8,128)(2,1)S(1)} collective-permute-done((bf16[2,2,32,1024]{3,2,1,0:T(8,128)(2,1)S(1)}, bf16[2,2,32,1024]{3,2,1,0:T(8,128)(2,1)S(1)}, u32[]{:S(2)}, u32[]{:S(2)}) %collective-permute-start.20) | collective-permute-done | bytes 262176 | tf_op jit(solution)/shard_map/ppermute | solution.py:23
  64.3 3.5 %collective-permute-done.17.second_2 = bf16[128,1024]{1,0:T(8,128)(2,1)S(1)} collective-permute-done((bf16[128,1024]{1,0:T(8,128)(2,1)S(1)}, bf16[128,1024]{1,0:T(8,128)(2,1)S(1)}, u32[]{:S(2)}, u32[]{:S(2)}) %collective-permute-start.17) | collective-permute-done | bytes 262176 | tf_op jit(solution)/shard_map/ppermute | solution.py:19
  68.7 2.6 %collective-permute-done.22 = f32[32,128]{1,0:T(8,128)S(1)} collective-permute-done((f32[32,128]{1,0:T(8,128)S(1)}, f32[32,128]{1,0:T(8,128)S(1)}, u32[]{:S(2)}, u32[]{:S(2)}) %collective-permute-start.22) | collective-permute-done | bytes 16416 | tf_op jit(solution)/shard_map/ppermute | solution.py:23
  71.3 2.2 %collective-permute-start.25 = (f32[2,32,128]{2,1,0:T(8,128)S(1)}, f32[2,32,128]{2,1,0:T(8,128)S(1)}, u32[]{:S(2)}, u32[]{:S(2)}) collective-permute-start(f32[2,32,128]{2,1,0:T(8,128)S(1)} %pad_maximum_fusion.22.stats), channel_id=1, source_target_pairs={{0,6},{1,7},{2,0},{3,1},{4,2},{5,3},{6,4},{7,5},{8,14},{9,15},{10,... | collective-permute-start | bytes 98312 | tf_op jit(solution)/shard_map/ppermute | solution.py:23
  75.3 2.5 %collective-permute-done.24.stats_2 = f32[2,32,128]{2,1,0:T(8,128)S(1)} collective-permute-done((f32[2,32,128]{2,1,0:T(8,128)S(1)}, f32[2,32,128]{2,1,0:T(8,128)S(1)}, u32[]{:S(2)}, u32[]{:S(2)}) %collective-permute-start.24) | collective-permute-done | bytes 32800 | tf_op jit(solution)/shard_map/ppermute | solution.py:23
  83.4 2.4 %convolution_convert_fusion.3 = bf16[256,1536]{1,0:T(8,128)(2,1)S(1)} fusion(bf16[256,1024]{1,0:T(8,128)(2,1)S(1)} %get-tuple-element.51, bf16[768,1024]{1,0:T(8,128)(2,1)} %copy-done.13, bf16[768,1024]{1,0:T(8,128)(2,1)S(1)} %bitcast.241), kind=kOutput, calls=%fused_computation.7 | convolution fusion | flops 811991040 | bytes 4456448 | tf_op jit(solution)/shard_map/dot_general | solution.py:229
  85.9 2.2 %collective-permute-done.26 = bf16[2,80,1024]{2,1,0:T(8,128)(2,1)S(1)} collective-permute-done((bf16[2,80,1024]{2,1,0:T(8,128)(2,1)S(1)}, bf16[2,80,1024]{2,1,0:T(8,128)(2,1)S(1)}, u32[]{:S(2)}, u32[]{:S(2)}) %collective-permute-start.26) | collective-permute-done | bytes 327712 | tf_op jit(solution)/shard_map/ppermute | solution.py:23
  90.0 17.6 %collective-permute-done.31 = bf16[8,32,1024]{2,1,0:T(8,128)(2,1)S(1)} collective-permute-done((bf16[8,32,1024]{2,1,0:T(8,128)(2,1)S(1)}, bf16[8,32,1024]{2,1,0:T(8,128)(2,1)S(1)}, u32[]{:S(2)}, u32[]{:S(2)}) %collective-permute-start.31) | collective-permute-done | bytes 524320 | tf_op jit(solution)/shard_map/ppermute | solution.py:19
  110.0 1.9 %collective-permute-start.29 = (bf16[4,40,1024]{2,1,0:T(8,128)(2,1)S(1)}, bf16[4,40,1024]{2,1,0:T(8,128)(2,1)S(1)}, u32[]{:S(2)}, u32[]{:S(2)}) collective-permute-start(bf16[4,40,1024]{2,1,0:T(8,128)(2,1)S(1)} %pad_maximum_fusion.9), channel_id=1, source_target_pairs={{0,64},{1,65},{2,66},{3,67},{4,68},{5,69},{6,70},{7,71},{64,0},{65... | collective-permute-start | bytes 983048 | tf_op jit(solution)/shard_map/ppermute | solution.py:34
  118.1 1.8 %fusion.1 = f32[1536,1024,1,1]{1,0,3,2:T(8,128)S(1)} fusion(bf16[4,8,32,1024]{3,2,1,0:T(8,128)(2,1)S(1)} %pad_maximum_fusion.1, bf16[4,1,32,1536]{3,2,1,0:T(8,128)(2,1)S(1)} %bitcast.224, bf16[4,1,32,1536]{3,2,1,0:T(8,128)(2,1)S(1)} %bitcast.226, bf16[4,1,32,1536]{3,2,1,0:T(8,128)(2,1)S(1)} %bitcast.228, bf16[4,1,32,1536]{3,2,1,0:T(8,128)(2,1)S(1)} %copy-done.1), kind=kOutput, calls=%fused_computation.14 | convolution fusion | flops 1612972032 | bytes 8912896 | tf_op jit(solution)/shard_map/dot_general | solution.py:247
  120.0 1.8 %bitcast_add_fusion = f32[1536,1024]{1,0:T(8,128)S(1)} fusion(f32[1536,1024,1,1]{1,0,3,2:T(8,128)S(1)} %fusion.1, bf16[4,8,32,1024]{3,2,1,0:T(8,128)(2,1)S(1)} %pad_maximum_fusion.1, bf16[4,4,32,1536]{3,2,0,1:T(8,128)(2,1)S(1)} %pad_maximum_fusion.3), kind=kOutput, calls=%fused_computation | convolution fusion | flops 1612185600 | bytes 15204352 | tf_op jit(solution)/shard_map/dot_general | solution.py:247
  122.2 5.2 %collective-permute-done.30 = bf16[4,40,1024]{2,1,0:T(8,128)(2,1)S(1)} collective-permute-done((bf16[4,40,1024]{2,1,0:T(8,128)(2,1)S(1)}, bf16[4,40,1024]{2,1,0:T(8,128)(2,1)S(1)}, u32[]{:S(2)}, u32[]{:S(2)}) %collective-permute-start.30) | collective-permute-done | bytes 327712 | tf_op jit(solution)/shard_map/ppermute | solution.py:34
  131.5 1.8 %collective-permute-done.45 = f32[2,8192]{1,0:T(2,128)S(1)} collective-permute-done((f32[2,8192]{1,0:T(2,128)S(1)}, f32[2,8192]{1,0:T(2,128)S(1)}, u32[]{:S(2)}, u32[]{:S(2)}) %collective-permute-start.45) | collective-permute-done | bytes 65568 | tf_op jit(solution)/shard_map/ppermute | solution.py:19
  140.9 2.4 %slice_add_fusion = f32[768,1024]{1,0:T(8,128)} fusion(f32[1536,1024]{1,0:T(8,128)S(1)} %bitcast_add_fusion, bf16[768,1024]{1,0:T(8,128)(2,1)S(1)} %collective-permute-done.38), kind=kLoop, calls=%fused_computation.2 | loop fusion | flops 1572864 | bytes 7864320 | tf_op jit(solution)/shard_map/add | solution.py:252
  143.3 1.9 %collective-permute-done.39 = bf16[4,32,1536]{2,1,0:T(8,128)(2,1)S(1)} collective-permute-done((bf16[4,32,1536]{2,1,0:T(8,128)(2,1)S(1)}, bf16[4,32,1536]{2,1,0:T(8,128)(2,1)S(1)}, u32[]{:S(2)}, u32[]{:S(2)}) %collective-permute-start.39) | collective-permute-done | bytes 393248 | tf_op jit(solution)/shard_map/ppermute | solution.py:23
  145.2 2.6 %collective-permute-done.40 = bf16[4,32,1536]{2,1,0:T(8,128)(2,1)S(1)} collective-permute-done((bf16[4,32,1536]{2,1,0:T(8,128)(2,1)S(1)}, bf16[4,32,1536]{2,1,0:T(8,128)(2,1)S(1)}, u32[]{:S(2)}, u32[]{:S(2)}) %collective-permute-start.40) | collective-permute-done | bytes 393248 | tf_op jit(solution)/shard_map/ppermute | solution.py:23
  147.9 3.7 %collective-permute-start.41 = (bf16[4,32,768]{2,1,0:T(8,128)(2,1)S(1)}, bf16[4,32,768]{2,1,0:T(8,128)(2,1)S(1)}, u32[]{:S(2)}, u32[]{:S(2)}) collective-permute-start(bf16[4,32,768]{2,1,0:T(8,128)(2,1)S(1)} %get-tuple-element.120), channel_id=1, source_target_pairs={{0,8},{8,0},{16,24},{24,16},{32,40},{40,32},{48,56},{56,48},{1,9},... | collective-permute-start | bytes 589832 | tf_op jit(solution)/shard_map/ppermute | solution.py:15
  (191 shorter events, 45.7 us)
Async XLA Ops:
  4.5 8.2 %collective-permute-start.10 = (bf16[4,32,1024]{2,1,0:T(8,128)(2,1)S(1)}, bf16[4,32,1024]{2,1,0:T(8,128)(2,1)S(1)}, u32[]{:S(2)}, u32[]{:S(2)}) collective-permute-start(bf16[4,32,1024]{2,1,0:T(8,128)(2,1)S(1)} %pad_maximum_fusion.13), channel_id=1, source_target_pairs={{0,1},{1,0},{2,3},{3,2},{4,5},{5,4},{6,7},{7,6},{64,65},{65,64},{6... | collective-permute-start | bytes 786440 | tf_op jit(solution)/shard_map/ppermute | solution.py:34
  6.3 15.0 %collective-permute-start.9 = (bf16[4,32,1024]{2,1,0:T(8,128)(2,1)S(1)}, bf16[4,32,1024]{2,1,0:T(8,128)(2,1)S(1)}, u32[]{:S(2)}, u32[]{:S(2)}) collective-permute-start(bf16[4,32,1024]{2,1,0:T(8,128)(2,1)S(1)} %get-tuple-element.34), channel_id=1, source_target_pairs={{0,64},{1,65},{2,66},{3,67},{4,68},{5,69},{6,70},{7,71},{64,0},{65... | collective-permute-start | bytes 786440 | tf_op jit(solution)/shard_map/ppermute | solution.py:34
  9.6 13.7 %collective-permute-start.4 = (bf16[4,32,1024]{2,1,0:T(8,128)(2,1)S(1)}, bf16[4,32,1024]{2,1,0:T(8,128)(2,1)S(1)}, u32[]{:S(2)}, u32[]{:S(2)}) collective-permute-start(bf16[4,32,1024]{2,1,0:T(8,128)(2,1)S(1)} %get-tuple-element.32), channel_id=1, source_target_pairs={{0,65},{1,64},{2,67},{3,66},{4,69},{5,68},{6,71},{7,70},{64,1},{65... | collective-permute-start | bytes 786440 | tf_op jit(solution)/shard_map/ppermute | solution.py:34
  9.6 18.8 %collective-permute-start.3 = (bf16[4,32,1536]{2,1,0:T(8,128)(2,1)S(1)}, bf16[4,32,1536]{2,1,0:T(8,128)(2,1)S(1)}, u32[]{:S(2)}, u32[]{:S(2)}) collective-permute-start(bf16[4,32,1536]{2,1,0:T(8,128)(2,1)S(1)} %pad_maximum_fusion.6), channel_id=1, source_target_pairs={{0,6},{1,7},{2,0},{3,1},{4,2},{5,3},{6,4},{7,5},{8,14},{9,15},{10,... | collective-permute-start | bytes 1179656 | tf_op jit(solution)/shard_map/ppermute | solution.py:23
  12.2 16.4 %collective-permute-start.2 = (bf16[4,32,1536]{2,1,0:T(8,128)(2,1)S(1)}, bf16[4,32,1536]{2,1,0:T(8,128)(2,1)S(1)}, u32[]{:S(2)}, u32[]{:S(2)}) collective-permute-start(bf16[4,32,1536]{2,1,0:T(8,128)(2,1)S(1)} %pad_maximum_fusion.6), channel_id=1, source_target_pairs={{0,2},{1,3},{2,4},{3,5},{4,6},{5,7},{6,0},{7,1},{8,10},{9,11},{10,... | collective-permute-start | bytes 1179656 | tf_op jit(solution)/shard_map/ppermute | solution.py:23
  12.7 15.9 %collective-permute-start.1 = (bf16[4,32,1536]{2,1,0:T(8,128)(2,1)S(1)}, bf16[4,32,1536]{2,1,0:T(8,128)(2,1)S(1)}, u32[]{:S(2)}, u32[]{:S(2)}) collective-permute-start(bf16[4,32,1536]{2,1,0:T(8,128)(2,1)S(1)} %pad_maximum_fusion.6), channel_id=1, source_target_pairs={{0,1},{1,0},{2,3},{3,2},{4,5},{5,4},{6,7},{7,6},{8,9},{9,8},{10,11... | collective-permute-start | bytes 1179656 | tf_op jit(solution)/shard_map/ppermute | solution.py:23
  23.3 10.3 %collective-permute-start.11 = (bf16[4,32,1536]{2,1,0:T(8,128)(2,1)S(1)}, bf16[4,32,1536]{2,1,0:T(8,128)(2,1)S(1)}, u32[]{:S(2)}, u32[]{:S(2)}) collective-permute-start(bf16[4,32,1536]{2,1,0:T(8,128)(2,1)S(1)} %pad_maximum_fusion.6), channel_id=1, source_target_pairs={{0,4},{1,5},{2,6},{3,7},{4,0},{5,1},{6,2},{7,3},{8,12},{9,13},{10,... | collective-permute-start | bytes 1179656 | tf_op jit(solution)/shard_map/ppermute | solution.py:23
  26.1 7.5 %collective-permute-start.5 = (bf16[768,1024]{1,0:T(8,128)(2,1)S(1)}, bf16[768,1024]{1,0:T(8,128)(2,1)S(1)}, u32[]{:S(2)}, u32[]{:S(2)}) collective-permute-start(bf16[768,1024]{1,0:T(8,128)(2,1)S(1)} %bitcast.238), channel_id=1, source_target_pairs={{0,8},{8,0},{16,24},{24,16},{32,40},{40,32},{48,56},{56,48},{1,9},... | collective-permute-start | bytes 4718600 | tf_op jit(solution)/shard_map/ppermute | solution.py:15
  29.4 14.1 %collective-permute-start.13 = (bf16[4,32,1536]{2,1,0:T(8,128)(2,1)S(1)}, bf16[4,32,1536]{2,1,0:T(8,128)(2,1)S(1)}, u32[]{:S(2)}, u32[]{:S(2)}) collective-permute-start(bf16[4,32,1536]{2,1,0:T(8,128)(2,1)S(1)} %collective-permute-done.1), channel_id=1, source_target_pairs={{0,6},{1,7},{2,0},{3,1},{4,2},{5,3},{6,4},{7,5},{8,14},{9,15},{10,... | collective-permute-start | bytes 1179656 | tf_op jit(solution)/shard_map/ppermute | solution.py:23
  30.2 15.9 %collective-permute-start.12 = (bf16[4,32,1536]{2,1,0:T(8,128)(2,1)S(1)}, bf16[4,32,1536]{2,1,0:T(8,128)(2,1)S(1)}, u32[]{:S(2)}, u32[]{:S(2)}) collective-permute-start(bf16[4,32,1536]{2,1,0:T(8,128)(2,1)S(1)} %collective-permute-done.1), channel_id=1, source_target_pairs={{0,2},{1,3},{2,4},{3,5},{4,6},{5,7},{6,0},{7,1},{8,10},{9,11},{10,... | collective-permute-start | bytes 1179656 | tf_op jit(solution)/shard_map/ppermute | solution.py:23
  33.6 12.5 %collective-permute-start.15 = (bf16[4,32,1536]{2,1,0:T(8,128)(2,1)S(1)}, bf16[4,32,1536]{2,1,0:T(8,128)(2,1)S(1)}, u32[]{:S(2)}, u32[]{:S(2)}) collective-permute-start(bf16[4,32,1536]{2,1,0:T(8,128)(2,1)S(1)} %collective-permute-done.11), channel_id=1, source_target_pairs={{0,1},{1,0},{2,3},{3,2},{4,5},{5,4},{6,7},{7,6},{8,9},{9,8},{10,11... | collective-permute-start | bytes 1179656 | tf_op jit(solution)/shard_map/ppermute | solution.py:23
  35.5 17.7 %collective-permute-start.8 = (bf16[128,1024]{1,0:T(8,128)(2,1)S(1)}, bf16[128,1024]{1,0:T(8,128)(2,1)S(1)}, u32[]{:S(2)}, u32[]{:S(2)}) collective-permute-start(bf16[128,1024]{1,0:T(8,128)(2,1)S(1)} %get-tuple-element.64), channel_id=1, source_target_pairs={{0,32},{8,40},{16,48},{24,56},{32,0},{40,8},{48,16},{56,24},{1,33}... | collective-permute-start | bytes 786440 | tf_op jit(solution)/shard_map/ppermute | solution.py:19
  38.5 14.7 %collective-permute-start.7 = (bf16[128,1024]{1,0:T(8,128)(2,1)S(1)}, bf16[128,1024]{1,0:T(8,128)(2,1)S(1)}, u32[]{:S(2)}, u32[]{:S(2)}) collective-permute-start(bf16[128,1024]{1,0:T(8,128)(2,1)S(1)} %get-tuple-element.65), channel_id=1, source_target_pairs={{0,16},{8,24},{16,32},{24,40},{32,48},{40,56},{48,0},{56,8},{1,17}... | collective-permute-start | bytes 786440 | tf_op jit(solution)/shard_map/ppermute | solution.py:19
  43.4 11.1 %collective-permute-start.6 = (bf16[128,1024]{1,0:T(8,128)(2,1)S(1)}, bf16[128,1024]{1,0:T(8,128)(2,1)S(1)}, u32[]{:S(2)}, u32[]{:S(2)}) collective-permute-start(bf16[128,1024]{1,0:T(8,128)(2,1)S(1)} %get-tuple-element.66), channel_id=1, source_target_pairs={{0,48},{8,56},{16,0},{24,8},{32,16},{40,24},{48,32},{56,40},{1,49}... | collective-permute-start | bytes 786440 | tf_op jit(solution)/shard_map/ppermute | solution.py:19
  48.4 8.8 %collective-permute-start.19 = (bf16[2,2,32,1024]{3,2,1,0:T(8,128)(2,1)S(1)}, bf16[2,2,32,1024]{3,2,1,0:T(8,128)(2,1)S(1)}, u32[]{:S(2)}, u32[]{:S(2)}) collective-permute-start(bf16[2,2,32,1024]{3,2,1,0:T(8,128)(2,1)S(1)} %pad_maximum_fusion.15), channel_id=1, source_target_pairs={{0,2},{1,3},{2,4},{3,5},{4,6},{5,7},{6,0},{7,1},{8,10},{9,11},{10,... | collective-permute-start | bytes 786440 | tf_op jit(solution)/shard_map/ppermute | solution.py:23
  50.7 13.6 %collective-permute-start.20 = (bf16[2,2,32,1024]{3,2,1,0:T(8,128)(2,1)S(1)}, bf16[2,2,32,1024]{3,2,1,0:T(8,128)(2,1)S(1)}, u32[]{:S(2)}, u32[]{:S(2)}) collective-permute-start(bf16[2,2,32,1024]{3,2,1,0:T(8,128)(2,1)S(1)} %pad_maximum_fusion.16), channel_id=1, source_target_pairs={{0,4},{1,5},{2,6},{3,7},{4,0},{5,1},{6,2},{7,3},{8,12},{9,13},{10,... | collective-permute-start | bytes 786440 | tf_op jit(solution)/shard_map/ppermute | solution.py:23
  53.2 11.1 %collective-permute-start.21 = (bf16[2,2,32,1024]{3,2,1,0:T(8,128)(2,1)S(1)}, bf16[2,2,32,1024]{3,2,1,0:T(8,128)(2,1)S(1)}, u32[]{:S(2)}, u32[]{:S(2)}) collective-permute-start(bf16[2,2,32,1024]{3,2,1,0:T(8,128)(2,1)S(1)} %pad_maximum_fusion.17), channel_id=1, source_target_pairs={{0,6},{1,7},{2,0},{3,1},{4,2},{5,3},{6,4},{7,5},{8,14},{9,15},{10,... | collective-permute-start | bytes 786440 | tf_op jit(solution)/shard_map/ppermute | solution.py:23
  53.2 11.1 %collective-permute-start.18 = (bf16[128,1024]{1,0:T(8,128)(2,1)S(1)}, bf16[128,1024]{1,0:T(8,128)(2,1)S(1)}, u32[]{:S(2)}, u32[]{:S(2)}) collective-permute-start(bf16[128,1024]{1,0:T(8,128)(2,1)S(1)} %get-tuple-element.60), channel_id=1, source_target_pairs={{0,32},{8,40},{16,48},{24,56},{32,0},{40,8},{48,16},{56,24},{1,33}... | collective-permute-start | bytes 786440 | tf_op jit(solution)/shard_map/ppermute | solution.py:19
  54.5 13.3 %collective-permute-start.17 = (bf16[128,1024]{1,0:T(8,128)(2,1)S(1)}, bf16[128,1024]{1,0:T(8,128)(2,1)S(1)}, u32[]{:S(2)}, u32[]{:S(2)}) collective-permute-start(bf16[128,1024]{1,0:T(8,128)(2,1)S(1)} %get-tuple-element.61), channel_id=1, source_target_pairs={{0,16},{8,24},{16,32},{24,40},{32,48},{40,56},{48,0},{56,8},{1,17}... | collective-permute-start | bytes 786440 | tf_op jit(solution)/shard_map/ppermute | solution.py:19
  57.1 10.7 %collective-permute-start.16 = (bf16[128,1024]{1,0:T(8,128)(2,1)S(1)}, bf16[128,1024]{1,0:T(8,128)(2,1)S(1)}, u32[]{:S(2)}, u32[]{:S(2)}) collective-permute-start(bf16[128,1024]{1,0:T(8,128)(2,1)S(1)} %get-tuple-element.62), channel_id=1, source_target_pairs={{0,48},{8,56},{16,0},{24,8},{32,16},{40,24},{48,32},{56,40},{1,49}... | collective-permute-start | bytes 786440 | tf_op jit(solution)/shard_map/ppermute | solution.py:19
  80.2 28.5 %collective-permute-start.33 = (bf16[8,32,1024]{2,1,0:T(8,128)(2,1)S(1)}, bf16[8,32,1024]{2,1,0:T(8,128)(2,1)S(1)}, u32[]{:S(2)}, u32[]{:S(2)}) collective-permute-start(bf16[8,32,1024]{2,1,0:T(8,128)(2,1)S(1)} %bitcast.209), channel_id=1, source_target_pairs={{0,48},{8,56},{16,0},{24,8},{32,16},{40,24},{48,32},{56,40},{1,49}... | collective-permute-start | bytes 1572872 | tf_op jit(solution)/shard_map/ppermute | solution.py:19
  81.2 30.6 %collective-permute-start.32 = (bf16[8,32,1024]{2,1,0:T(8,128)(2,1)S(1)}, bf16[8,32,1024]{2,1,0:T(8,128)(2,1)S(1)}, u32[]{:S(2)}, u32[]{:S(2)}) collective-permute-start(bf16[8,32,1024]{2,1,0:T(8,128)(2,1)S(1)} %bitcast.210), channel_id=1, source_target_pairs={{0,32},{8,40},{16,48},{24,56},{32,0},{40,8},{48,16},{56,24},{1,33}... | collective-permute-start | bytes 1572872 | tf_op jit(solution)/shard_map/ppermute | solution.py:19
  81.3 26.4 %collective-permute-start.31 = (bf16[8,32,1024]{2,1,0:T(8,128)(2,1)S(1)}, bf16[8,32,1024]{2,1,0:T(8,128)(2,1)S(1)}, u32[]{:S(2)}, u32[]{:S(2)}) collective-permute-start(bf16[8,32,1024]{2,1,0:T(8,128)(2,1)S(1)} %bitcast.211), channel_id=1, source_target_pairs={{0,16},{8,24},{16,32},{24,40},{32,48},{40,56},{48,0},{56,8},{1,17}... | collective-permute-start | bytes 1572872 | tf_op jit(solution)/shard_map/ppermute | solution.py:19
  82.5 7.1 %collective-permute-start.27 = (bf16[2,80,1024]{2,1,0:T(8,128)(2,1)S(1)}, bf16[2,80,1024]{2,1,0:T(8,128)(2,1)S(1)}, u32[]{:S(2)}, u32[]{:S(2)}) collective-permute-start(bf16[2,80,1024]{2,1,0:T(8,128)(2,1)S(1)} %get-tuple-element.49), channel_id=1, source_target_pairs={{0,2},{1,3},{2,4},{3,5},{4,6},{5,7},{6,0},{7,1},{8,10},{9,11},{10,... | collective-permute-start | bytes 983048 | tf_op jit(solution)/shard_map/ppermute | solution.py:23
  89.6 20.2 %collective-permute-start.28 = (bf16[2,80,1024]{2,1,0:T(8,128)(2,1)S(1)}, bf16[2,80,1024]{2,1,0:T(8,128)(2,1)S(1)}, u32[]{:S(2)}, u32[]{:S(2)}) collective-permute-start(bf16[2,80,1024]{2,1,0:T(8,128)(2,1)S(1)} %get-tuple-element.50), channel_id=1, source_target_pairs={{0,4},{1,5},{2,6},{3,7},{4,0},{5,1},{6,2},{7,3},{8,12},{9,13},{10,... | collective-permute-start | bytes 983048 | tf_op jit(solution)/shard_map/ppermute | solution.py:23
  109.9 17.5 %collective-permute-start.30 = (bf16[4,40,1024]{2,1,0:T(8,128)(2,1)S(1)}, bf16[4,40,1024]{2,1,0:T(8,128)(2,1)S(1)}, u32[]{:S(2)}, u32[]{:S(2)}) collective-permute-start(bf16[4,40,1024]{2,1,0:T(8,128)(2,1)S(1)} %pad_maximum_fusion.10), channel_id=1, source_target_pairs={{0,65},{1,64},{2,67},{3,66},{4,69},{5,68},{6,71},{7,70},{64,1},{65... | collective-permute-start | bytes 983048 | tf_op jit(solution)/shard_map/ppermute | solution.py:34
  110.0 17.4 %collective-permute-start.29 = (bf16[4,40,1024]{2,1,0:T(8,128)(2,1)S(1)}, bf16[4,40,1024]{2,1,0:T(8,128)(2,1)S(1)}, u32[]{:S(2)}, u32[]{:S(2)}) collective-permute-start(bf16[4,40,1024]{2,1,0:T(8,128)(2,1)S(1)} %pad_maximum_fusion.9), channel_id=1, source_target_pairs={{0,64},{1,65},{2,66},{3,67},{4,68},{5,69},{6,70},{7,71},{64,0},{65... | collective-permute-start | bytes 983048 | tf_op jit(solution)/shard_map/ppermute | solution.py:34
  113.0 17.1 %collective-permute-start.34 = (bf16[4,32,1536]{2,1,0:T(8,128)(2,1)S(1)}, bf16[4,32,1536]{2,1,0:T(8,128)(2,1)S(1)}, u32[]{:S(2)}, u32[]{:S(2)}) collective-permute-start(bf16[4,32,1536]{2,1,0:T(8,128)(2,1)S(1)} %pad_maximum_fusion.7), channel_id=1, source_target_pairs={{0,1},{1,0},{2,3},{3,2},{4,5},{5,4},{6,7},{7,6},{8,9},{9,8},{10,11... | collective-permute-start | bytes 1179656 | tf_op jit(solution)/shard_map/ppermute | solution.py:23
  114.8 23.9 %collective-permute-start.36 = (bf16[2,4,32,1536]{3,2,1,0:T(8,128)(2,1)S(1)}, bf16[2,4,32,1536]{3,2,1,0:T(8,128)(2,1)S(1)}, u32[]{:S(2)}, u32[]{:S(2)}) collective-permute-start(bf16[2,4,32,1536]{3,2,1,0:T(8,128)(2,1)S(1)} %pad_maximum_fusion.4), channel_id=1, source_target_pairs={{0,6},{1,7},{2,0},{3,1},{4,2},{5,3},{6,4},{7,5},{8,14},{9,15},{10,... | collective-permute-start | bytes 2359304 | tf_op jit(solution)/shard_map/ppermute | solution.py:23
  115.2 23.7 %collective-permute-start.37 = (bf16[2,4,32,1536]{3,2,1,0:T(8,128)(2,1)S(1)}, bf16[2,4,32,1536]{3,2,1,0:T(8,128)(2,1)S(1)}, u32[]{:S(2)}, u32[]{:S(2)}) collective-permute-start(bf16[2,4,32,1536]{3,2,1,0:T(8,128)(2,1)S(1)} %pad_maximum_fusion.5), channel_id=1, source_target_pairs={{0,2},{1,3},{2,4},{3,5},{4,6},{5,7},{6,0},{7,1},{8,10},{9,11},{10,... | collective-permute-start | bytes 2359304 | tf_op jit(solution)/shard_map/ppermute | solution.py:23
  134.7 10.5 %collective-permute-start.39 = (bf16[4,32,1536]{2,1,0:T(8,128)(2,1)S(1)}, bf16[4,32,1536]{2,1,0:T(8,128)(2,1)S(1)}, u32[]{:S(2)}, u32[]{:S(2)}) collective-permute-start(bf16[4,32,1536]{2,1,0:T(8,128)(2,1)S(1)} %add_convert_fusion.1), channel_id=1, source_target_pairs={{0,4},{1,5},{2,6},{3,7},{4,0},{5,1},{6,2},{7,3},{8,12},{9,13},{10,... | collective-permute-start | bytes 1179656 | tf_op jit(solution)/shard_map/ppermute | solution.py:23
  139.8 8.0 %collective-permute-start.40 = (bf16[4,32,1536]{2,1,0:T(8,128)(2,1)S(1)}, bf16[4,32,1536]{2,1,0:T(8,128)(2,1)S(1)}, u32[]{:S(2)}, u32[]{:S(2)}) collective-permute-start(bf16[4,32,1536]{2,1,0:T(8,128)(2,1)S(1)} %get-tuple-element.59), channel_id=1, source_target_pairs={{0,1},{1,0},{2,3},{3,2},{4,5},{5,4},{6,7},{7,6},{8,9},{9,8},{10,11... | collective-permute-start | bytes 1179656 | tf_op jit(solution)/shard_map/ppermute | solution.py:23
  (29 other events, 156.8 us)

commit v4 on v3

--- a/solution.py
+++ b/solution.py
@@ -152,14 +152,15 @@
         ]
         for rows in (residual, out_grad)
     ]
-    stream = [sides[0][0], over_both(after(sides[0][1], half), 0, 1)]
+    stream = [sides[0][0], None]
     cotangent = [over_both(after(sides[1][f], half), -1, f) for f in (0, 1)]
 
     got = {(0, 0): half}
     got[(0, 1)] = over_dp(half, 0, 1)
+    stream[1] = over_both(after(sides[0][1], got[(0, 1)]), 0, 1)
     got[(3, 0)] = over_dp(half, 3, 0)
     got[(1, 0)] = over_dp(half, 1, 0)
-    got[(2, 0)] = over_dp(after(half, *cotangent, stream[1]), 2, 0)
+    got[(2, 0)] = over_dp(after(half, cotangent[0]), 2, 0)
     for k in (1, 3):
         got[(k, 1)] = over_dp(got[(0, 1)], k, 0)
 
@@ -239,7 +240,7 @@
     near = [over_dp(jnp.stack([term[(k, 0)], term[(k, 1)]]), -k, 0).astype(F32) for k in (1, 3)]
     far = (term[(2, 0)].astype(F32) + crossing).astype(BF)
     far = over_dp(far, -2, 0).astype(F32)
-    upstream = to_rows(gradient[0], after(over_both(after(gradient[1], passing), 0, 1), near[0], near[1]))
+    aside = over_both(after(gradient[1], passing), 0, 1)
     other = term[(0, 1)].astype(F32) + near[0][1] + near[1][1]
     other = over_dp(other.astype(BF), 0, 1).astype(F32)
     spread = jnp.stack(flowing)
@@ -252,6 +253,7 @@
     grad_weight = weight_sum[:768] + over_core(after(weight_sum[768:].astype(BF), passing)).astype(F32)
     here = after(term[(0, 0)].astype(F32) + near[0][0] + near[1][0], grad_weight)
     context_sum = (here + far + other).astype(BF)
+    upstream = to_rows(gradient[0], after(aside, context_sum))
     kept, given = context_sum[..., :768], over_core(context_sum[..., 768:])
     both = jnp.stack([kept, given], axis=1)
     both = jnp.stack(

time: 154 us -> 152 us (0.987)
  waiting for transfers between devices: 73.4 us -> 71.7 us
    ppermute x22, waiting for transfers between devices: 29.2 us -> 23.2 us  [over_dp(): lax.ppermute(value, 'dp', [(j, 2 * (((j >> 1) + steps) % 4) + (j & 1 ^ fl...]
    ppermute x6, waiting for transfers between devices: 15.5 us -> 18.9 us  [over_both(): return lax.ppermute(value, ('section', 'dp'), pairs)]
    ppermute x5, starting transfers between devices: 9.42 us -> 6.19 us  [over_core(): return lax.ppermute(value, 'mp', [(i, i ^ 1) for i in range(8)])]
    ppermute x12, waiting for transfers between devices: 25.1 us -> 27.9 us  [over_y(): lax.ppermute(value, 'mp', [(i, (i + 2 * steps) % 8) for i in range(8)])]
    ppermute x12, starting transfers between devices: 11.2 us -> 13.7 us  [over_y(): lax.ppermute(value, 'mp', [(i, (i + 2 * steps) % 8) for i in range(8)])]
    ppermute x1, starting transfers between devices: 0.09 us -> 2.6 us  [over_section(): lax.ppermute(value, 'section', [(s, (s + steps) % 2) for s in range(2)])]
    ppermute x1, waiting for transfers between devices: 2.05 us -> 0.01 us  [over_section(): lax.ppermute(value, 'section', [(s, (s + steps) % 2) for s in range(2)])]
    ppermute x22, starting transfers between devices: 23.5 us -> 21.9 us  [over_dp(): lax.ppermute(value, 'dp', [(j, 2 * (((j >> 1) + steps) % 4) + (j & 1 ^ fl...]
  transfers between devices with their start and end apart: 46 -> 46, of which waited for: 25 -> 24; matrix products, arithmetic and copies ran while one was open for 14% -> 14% of each run, Pallas kernels for 0% -> 0%
where the time goes in v4:
time: 152 us; the launch traced here: 151 us
  waiting for transfers between devices  71.7 us (47%)
  starting transfers between devices  51.3 us (34%)
  matrix products  12.7 us (8%)
  local copies, waits for them, and re-layouts  6.31 us (4%)
  other arithmetic  6.06 us (4%)
  Pallas kernels  1.72 us (1%)
  between operations  1.66 us (1%)
    ppermute x12, waiting for transfers between devices, over_y(): lax.ppermute(value, 'mp', [(i, (i + 2 * steps) % 8) for i in range(8)])  27.9 us
    ppermute x22, waiting for transfers between devices, over_dp(): lax.ppermute(value, 'dp', [(j, 2 * (((j >> 1) + steps) % 4) + (j & 1 ^ fl...  23.2 us
    ppermute x22, starting transfers between devices, over_dp(): lax.ppermute(value, 'dp', [(j, 2 * (((j >> 1) + steps) % 4) + (j & 1 ^ fl...  21.9 us
    ppermute x6, waiting for transfers between devices, over_both(): return lax.ppermute(value, ('section', 'dp'), pairs)  18.9 us
    ppermute x12, starting transfers between devices, over_y(): lax.ppermute(value, 'mp', [(i, (i + 2 * steps) % 8) for i in range(8)])  13.7 us
    ppermute x6, starting transfers between devices, over_both(): return lax.ppermute(value, ('section', 'dp'), pairs)  6.86 us
    ppermute x5, starting transfers between devices, over_core(): return lax.ppermute(value, 'mp', [(i, i ^ 1) for i in range(8)])  6.19 us
    dot_general x4, matrix products, shards(): lax.dot_general(rows.reshape(256, 1024), weights, (((1,), (1,)), ((), ())...  5.47 us
  transfers between devices with their start and end apart: 46, of which 24 were waited for; matrix products, arithmetic and copies ran while one was open for 14% of the time, Pallas kernels for 0%

profile of v4, /device:TPU:1, one launch (start us, length us, event | category | flops | bytes accessed | tf_op | source)
XLA Modules:
  0.0 151.4 jit_solution(16706912532397167405)
XLA Ops:
  4.5 3.8 %collective-permute-start.9 = (bf16[4,32,1024]{2,1,0:T(8,128)(2,1)S(1)}, bf16[4,32,1024]{2,1,0:T(8,128)(2,1)S(1)}, u32[]{:S(2)}, u32[]{:S(2)}) collective-permute-start(bf16[4,32,1024]{2,1,0:T(8,128)(2,1)S(1)} %get-tuple-element.34), channel_id=1, source_target_pairs={{0,64},{1,65},{2,66},{3,67},{4,68},{5,69},{6,70},{7,71},{64,0},{65... | collective-permute-start | bytes 786440 | tf_op jit(solution)/shard_map/ppermute | solution.py:34
  8.7 2.5 %collective-permute-start.3 = (bf16[4,32,1536]{2,1,0:T(8,128)(2,1)S(1)}, bf16[4,32,1536]{2,1,0:T(8,128)(2,1)S(1)}, u32[]{:S(2)}, u32[]{:S(2)}) collective-permute-start(bf16[4,32,1536]{2,1,0:T(8,128)(2,1)S(1)} %pad_maximum_fusion.6), channel_id=1, source_target_pairs={{0,6},{1,7},{2,0},{3,1},{4,2},{5,3},{6,4},{7,5},{8,14},{9,15},{10,... | collective-permute-start | bytes 1179656 | tf_op jit(solution)/shard_map/ppermute | solution.py:23
  11.6 3.1 %collective-permute-done.9 = bf16[4,32,1024]{2,1,0:T(8,128)(2,1)S(1)} collective-permute-done((bf16[4,32,1024]{2,1,0:T(8,128)(2,1)S(1)}, bf16[4,32,1024]{2,1,0:T(8,128)(2,1)S(1)}, u32[]{:S(2)}, u32[]{:S(2)}) %collective-permute-start.9) | collective-permute-done | bytes 262176 | tf_op jit(solution)/shard_map/ppermute | solution.py:34
  14.7 5.9 %collective-permute-done.4 = bf16[4,32,1024]{2,1,0:T(8,128)(2,1)S(1)} collective-permute-done((bf16[4,32,1024]{2,1,0:T(8,128)(2,1)S(1)}, bf16[4,32,1024]{2,1,0:T(8,128)(2,1)S(1)}, u32[]{:S(2)}, u32[]{:S(2)}) %collective-permute-start.4) | collective-permute-done | bytes 262176 | tf_op jit(solution)/shard_map/ppermute | solution.py:34
  20.7 2.7 %collective-permute-start.10 = (bf16[4,32,1536]{2,1,0:T(8,128)(2,1)S(1)}, bf16[4,32,1536]{2,1,0:T(8,128)(2,1)S(1)}, u32[]{:S(2)}, u32[]{:S(2)}) collective-permute-start(bf16[4,32,1536]{2,1,0:T(8,128)(2,1)S(1)} %pad_maximum_fusion.6), channel_id=1, source_target_pairs={{0,4},{1,5},{2,6},{3,7},{4,0},{5,1},{6,2},{7,3},{8,12},{9,13},{10,... | collective-permute-start | bytes 1179656 | tf_op jit(solution)/shard_map/ppermute | solution.py:23
  24.4 2.6 %collective-permute-start.13 = (f32[2,1024]{1,0:T(2,128)S(1)}, f32[2,1024]{1,0:T(2,128)S(1)}, u32[]{:S(2)}, u32[]{:S(2)}) collective-permute-start(f32[2,1024]{1,0:T(2,128)S(1)} %pad_maximum_fusion.23), channel_id=1, source_target_pairs={{0,64},{64,0},{1,65},{65,1},{2,66},{66,2},{3,67},{67,3},{4,68},{68... | collective-permute-start | bytes 24584 | tf_op jit(solution)/shard_map/ppermute | solution.py:29
  29.2 5.5 %collective-permute-done.18 = bf16[4,32,1024]{2,1,0:T(8,128)(2,1)S(1)} collective-permute-done((bf16[4,32,1024]{2,1,0:T(8,128)(2,1)S(1)}, bf16[4,32,1024]{2,1,0:T(8,128)(2,1)S(1)}, u32[]{:S(2)}, u32[]{:S(2)}) %collective-permute-start.18) | collective-permute-done | bytes 262176 | tf_op jit(solution)/shard_map/ppermute | solution.py:34
  38.2 3.0 %collective-permute-start.8 = (bf16[128,1024]{1,0:T(8,128)(2,1)S(1)}, bf16[128,1024]{1,0:T(8,128)(2,1)S(1)}, u32[]{:S(2)}, u32[]{:S(2)}) collective-permute-start(bf16[128,1024]{1,0:T(8,128)(2,1)S(1)} %get-tuple-element.64), channel_id=1, source_target_pairs={{0,32},{8,40},{16,48},{24,56},{32,0},{40,8},{48,16},{56,24},{1,33}... | collective-permute-start | bytes 786440 | tf_op jit(solution)/shard_map/ppermute | solution.py:19
  41.6 2.3 %collective-permute-start.6 = (bf16[128,1024]{1,0:T(8,128)(2,1)S(1)}, bf16[128,1024]{1,0:T(8,128)(2,1)S(1)}, u32[]{:S(2)}, u32[]{:S(2)}) collective-permute-start(bf16[128,1024]{1,0:T(8,128)(2,1)S(1)} %get-tuple-element.66), channel_id=1, source_target_pairs={{0,48},{8,56},{16,0},{24,8},{32,16},{40,24},{48,32},{56,40},{1,49}... | collective-permute-start | bytes 786440 | tf_op jit(solution)/shard_map/ppermute | solution.py:19
  45.9 1.8 %convolution_convert_fusion.4 = bf16[512,1024]{1,0:T(8,128)(2,1)S(1)} fusion(bf16[512,1536]{1,0:T(8,128)(2,1)S(1)} %bitcast.216, bf16[768,1024]{1,0:T(8,128)(2,1)S(1)} %collective-permute-done.5, bf16[768,1024]{1,0:T(8,128)(2,1)S(1)} %bitcast.240), kind=kOutput, calls=%fused_computation.11 | convolution fusion | flops 1617428480 | bytes 5767168 | tf_op jit(solution)/shard_map/dot_general | solution.py:187
  48.0 2.6 %collective-permute-start.20 = (bf16[2,2,32,1024]{3,2,1,0:T(8,128)(2,1)S(1)}, bf16[2,2,32,1024]{3,2,1,0:T(8,128)(2,1)S(1)}, u32[]{:S(2)}, u32[]{:S(2)}) collective-permute-start(bf16[2,2,32,1024]{3,2,1,0:T(8,128)(2,1)S(1)} %pad_maximum_fusion.16), channel_id=1, source_target_pairs={{0,4},{1,5},{2,6},{3,7},{4,0},{5,1},{6,2},{7,3},{8,12},{9,13},{10,... | collective-permute-start | bytes 786440 | tf_op jit(solution)/shard_map/ppermute | solution.py:23
  50.9 2.0 %collective-permute-done.7.first_2 = bf16[128,1024]{1,0:T(8,128)(2,1)S(1)} collective-permute-done((bf16[128,1024]{1,0:T(8,128)(2,1)S(1)}, bf16[128,1024]{1,0:T(8,128)(2,1)S(1)}, u32[]{:S(2)}, u32[]{:S(2)}) %collective-permute-start.7) | collective-permute-done | bytes 262176 | tf_op jit(solution)/shard_map/ppermute | solution.py:19
  52.8 2.0 %collective-permute-start.17 = (bf16[128,1024]{1,0:T(8,128)(2,1)S(1)}, bf16[128,1024]{1,0:T(8,128)(2,1)S(1)}, u32[]{:S(2)}, u32[]{:S(2)}) collective-permute-start(bf16[128,1024]{1,0:T(8,128)(2,1)S(1)} %get-tuple-element.60), channel_id=1, source_target_pairs={{0,32},{8,40},{16,48},{24,56},{32,0},{40,8},{48,16},{56,24},{1,33}... | collective-permute-start | bytes 786440 | tf_op jit(solution)/shard_map/ppermute | solution.py:19
  55.3 2.7 %collective-permute-start.15 = (bf16[128,1024]{1,0:T(8,128)(2,1)S(1)}, bf16[128,1024]{1,0:T(8,128)(2,1)S(1)}, u32[]{:S(2)}, u32[]{:S(2)}) collective-permute-start(bf16[128,1024]{1,0:T(8,128)(2,1)S(1)} %get-tuple-element.62), channel_id=1, source_target_pairs={{0,48},{8,56},{16,0},{24,8},{32,16},{40,24},{48,32},{56,40},{1,49}... | collective-permute-start | bytes 786440 | tf_op jit(solution)/shard_map/ppermute | solution.py:19
  58.1 2.1 %collective-permute-done.20.turned_2 = bf16[2,2,32,1024]{3,2,1,0:T(8,128)(2,1)S(1)} collective-permute-done((bf16[2,2,32,1024]{3,2,1,0:T(8,128)(2,1)S(1)}, bf16[2,2,32,1024]{3,2,1,0:T(8,128)(2,1)S(1)}, u32[]{:S(2)}, u32[]{:S(2)}) %collective-permute-start.20) | collective-permute-done | bytes 262176 | tf_op jit(solution)/shard_map/ppermute | solution.py:23
  60.2 2.2 %collective-permute-done.21.turned_3 = bf16[2,2,32,1024]{3,2,1,0:T(8,128)(2,1)S(1)} collective-permute-done((bf16[2,2,32,1024]{3,2,1,0:T(8,128)(2,1)S(1)}, bf16[2,2,32,1024]{3,2,1,0:T(8,128)(2,1)S(1)}, u32[]{:S(2)}, u32[]{:S(2)}) %collective-permute-start.21) | collective-permute-done | bytes 262176 | tf_op jit(solution)/shard_map/ppermute | solution.py:23
  62.4 5.6 %collective-permute-done.16.second_2 = bf16[128,1024]{1,0:T(8,128)(2,1)S(1)} collective-permute-done((bf16[128,1024]{1,0:T(8,128)(2,1)S(1)}, bf16[128,1024]{1,0:T(8,128)(2,1)S(1)}, u32[]{:S(2)}, u32[]{:S(2)}) %collective-permute-start.16) | collective-permute-done | bytes 262176 | tf_op jit(solution)/shard_map/ppermute | solution.py:19
  69.0 2.4 %collective-permute-done.22 = f32[32,128]{1,0:T(8,128)S(1)} collective-permute-done((f32[32,128]{1,0:T(8,128)S(1)}, f32[32,128]{1,0:T(8,128)S(1)}, u32[]{:S(2)}, u32[]{:S(2)}) %collective-permute-start.22) | collective-permute-done | bytes 16416 | tf_op jit(solution)/shard_map/ppermute | solution.py:23
  71.4 2.6 %collective-permute-start.25 = (f32[2,32,128]{2,1,0:T(8,128)S(1)}, f32[2,32,128]{2,1,0:T(8,128)S(1)}, u32[]{:S(2)}, u32[]{:S(2)}) collective-permute-start(f32[2,32,128]{2,1,0:T(8,128)S(1)} %pad_maximum_fusion.22.stats), channel_id=1, source_target_pairs={{0,6},{1,7},{2,0},{3,1},{4,2},{5,3},{6,4},{7,5},{8,14},{9,15},{10,... | collective-permute-start | bytes 98312 | tf_op jit(solution)/shard_map/ppermute | solution.py:23
  75.1 3.3 %collective-permute-done.24.stats_2 = f32[2,32,128]{2,1,0:T(8,128)S(1)} collective-permute-done((f32[2,32,128]{2,1,0:T(8,128)S(1)}, f32[2,32,128]{2,1,0:T(8,128)S(1)}, u32[]{:S(2)}, u32[]{:S(2)}) %collective-permute-start.24) | collective-permute-done | bytes 32800 | tf_op jit(solution)/shard_map/ppermute | solution.py:23
  82.5 2.4 %convolution_convert_fusion.3 = bf16[256,1536]{1,0:T(8,128)(2,1)S(1)} fusion(bf16[256,1024]{1,0:T(8,128)(2,1)S(1)} %get-tuple-element.51, bf16[768,1024]{1,0:T(8,128)(2,1)} %copy-done.13, bf16[768,1024]{1,0:T(8,128)(2,1)S(1)} %bitcast.241), kind=kOutput, calls=%fused_computation.7 | convolution fusion | flops 811991040 | bytes 4456448 | tf_op jit(solution)/shard_map/dot_general | solution.py:230
  85.1 2.2 %collective-permute-done.26 = bf16[2,80,1024]{2,1,0:T(8,128)(2,1)S(1)} collective-permute-done((bf16[2,80,1024]{2,1,0:T(8,128)(2,1)S(1)}, bf16[2,80,1024]{2,1,0:T(8,128)(2,1)S(1)}, u32[]{:S(2)}, u32[]{:S(2)}) %collective-permute-start.26) | collective-permute-done | bytes 327712 | tf_op jit(solution)/shard_map/ppermute | solution.py:23
  89.1 16.5 %collective-permute-done.31 = bf16[8,32,1024]{2,1,0:T(8,128)(2,1)S(1)} collective-permute-done((bf16[8,32,1024]{2,1,0:T(8,128)(2,1)S(1)}, bf16[8,32,1024]{2,1,0:T(8,128)(2,1)S(1)}, u32[]{:S(2)}, u32[]{:S(2)}) %collective-permute-start.31) | collective-permute-done | bytes 524320 | tf_op jit(solution)/shard_map/ppermute | solution.py:19
  110.6 2.0 %collective-permute-start.34 = (bf16[4,32,1536]{2,1,0:T(8,128)(2,1)S(1)}, bf16[4,32,1536]{2,1,0:T(8,128)(2,1)S(1)}, u32[]{:S(2)}, u32[]{:S(2)}) collective-permute-start(bf16[4,32,1536]{2,1,0:T(8,128)(2,1)S(1)} %pad_maximum_fusion.7), channel_id=1, source_target_pairs={{0,1},{1,0},{2,3},{3,2},{4,5},{5,4},{6,7},{7,6},{8,9},{9,8},{10,11... | collective-permute-start | bytes 1179656 | tf_op jit(solution)/shard_map/ppermute | solution.py:23
  116.1 1.8 %fusion.1 = f32[1536,1024,1,1]{1,0,3,2:T(8,128)S(1)} fusion(bf16[4,8,32,1024]{3,2,1,0:T(8,128)(2,1)S(1)} %pad_maximum_fusion.1, bf16[4,1,32,1536]{3,2,1,0:T(8,128)(2,1)S(1)} %bitcast.224, bf16[4,1,32,1536]{3,2,1,0:T(8,128)(2,1)S(1)} %bitcast.226, bf16[4,1,32,1536]{3,2,1,0:T(8,128)(2,1)S(1)} %bitcast.228, bf16[4,1,32,1536]{3,2,1,0:T(8,128)(2,1)S(1)} %copy-done.1), kind=kOutput, calls=%fused_computation.14 | convolution fusion | flops 1612972032 | bytes 8912896 | tf_op jit(solution)/shard_map/dot_general | solution.py:248
  118.0 1.8 %bitcast_add_fusion = f32[1536,1024]{1,0:T(8,128)S(1)} fusion(f32[1536,1024,1,1]{1,0,3,2:T(8,128)S(1)} %fusion.1, bf16[4,8,32,1024]{3,2,1,0:T(8,128)(2,1)S(1)} %pad_maximum_fusion.1, bf16[4,4,32,1536]{3,2,0,1:T(8,128)(2,1)S(1)} %pad_maximum_fusion.3), kind=kOutput, calls=%fused_computation | convolution fusion | flops 1612185600 | bytes 15204352 | tf_op jit(solution)/shard_map/dot_general | solution.py:248
  120.2 4.3 %collective-permute-done.30 = bf16[4,40,1024]{2,1,0:T(8,128)(2,1)S(1)} collective-permute-done((bf16[4,40,1024]{2,1,0:T(8,128)(2,1)S(1)}, bf16[4,40,1024]{2,1,0:T(8,128)(2,1)S(1)}, u32[]{:S(2)}, u32[]{:S(2)}) %collective-permute-start.30) | collective-permute-done | bytes 327712 | tf_op jit(solution)/shard_map/ppermute | solution.py:34
  125.0 1.9 %collective-permute-start.42 = (f32[2,8192]{1,0:T(2,128)S(1)}, f32[2,8192]{1,0:T(2,128)S(1)}, u32[]{:S(2)}, u32[]{:S(2)}) collective-permute-start(f32[2,8192]{1,0:T(2,128)S(1)} %pad_maximum_fusion.21), channel_id=1, source_target_pairs={{0,8},{8,0},{16,24},{24,16},{32,40},{40,32},{48,56},{56,48},{1,9},... | collective-permute-start | bytes 196616 | tf_op jit(solution)/shard_map/ppermute | solution.py:15
  129.5 1.8 %collective-permute-done.45 = f32[2,8192]{1,0:T(2,128)S(1)} collective-permute-done((f32[2,8192]{1,0:T(2,128)S(1)}, f32[2,8192]{1,0:T(2,128)S(1)}, u32[]{:S(2)}, u32[]{:S(2)}) %collective-permute-start.45) | collective-permute-done | bytes 65568 | tf_op jit(solution)/shard_map/ppermute | solution.py:19
  139.0 2.4 %slice_add_fusion = f32[768,1024]{1,0:T(8,128)} fusion(f32[1536,1024]{1,0:T(8,128)S(1)} %bitcast_add_fusion, bf16[768,1024]{1,0:T(8,128)(2,1)S(1)} %collective-permute-done.38), kind=kLoop, calls=%fused_computation.2 | loop fusion | flops 1572864 | bytes 7864320 | tf_op jit(solution)/shard_map/add | solution.py:253
  141.4 1.8 %collective-permute-done.39 = bf16[4,32,1536]{2,1,0:T(8,128)(2,1)S(1)} collective-permute-done((bf16[4,32,1536]{2,1,0:T(8,128)(2,1)S(1)}, bf16[4,32,1536]{2,1,0:T(8,128)(2,1)S(1)}, u32[]{:S(2)}, u32[]{:S(2)}) %collective-permute-start.39) | collective-permute-done | bytes 393248 | tf_op jit(solution)/shard_map/ppermute | solution.py:23
  143.2 5.1 %collective-permute-done.40 = bf16[4,32,1536]{2,1,0:T(8,128)(2,1)S(1)} collective-permute-done((bf16[4,32,1536]{2,1,0:T(8,128)(2,1)S(1)}, bf16[4,32,1536]{2,1,0:T(8,128)(2,1)S(1)}, u32[]{:S(2)}, u32[]{:S(2)}) %collective-permute-start.40) | collective-permute-done | bytes 393248 | tf_op jit(solution)/shard_map/ppermute | solution.py:23
  (191 shorter events, 44.7 us)
Async XLA Ops:
  4.5 10.2 %collective-permute-start.9 = (bf16[4,32,1024]{2,1,0:T(8,128)(2,1)S(1)}, bf16[4,32,1024]{2,1,0:T(8,128)(2,1)S(1)}, u32[]{:S(2)}, u32[]{:S(2)}) collective-permute-start(bf16[4,32,1024]{2,1,0:T(8,128)(2,1)S(1)} %get-tuple-element.34), channel_id=1, source_target_pairs={{0,64},{1,65},{2,66},{3,67},{4,68},{5,69},{6,70},{7,71},{64,0},{65... | collective-permute-start | bytes 786440 | tf_op jit(solution)/shard_map/ppermute | solution.py:34
  8.3 12.4 %collective-permute-start.4 = (bf16[4,32,1024]{2,1,0:T(8,128)(2,1)S(1)}, bf16[4,32,1024]{2,1,0:T(8,128)(2,1)S(1)}, u32[]{:S(2)}, u32[]{:S(2)}) collective-permute-start(bf16[4,32,1024]{2,1,0:T(8,128)(2,1)S(1)} %get-tuple-element.32), channel_id=1, source_target_pairs={{0,65},{1,64},{2,67},{3,66},{4,69},{5,68},{6,71},{7,70},{64,1},{65... | collective-permute-start | bytes 786440 | tf_op jit(solution)/shard_map/ppermute | solution.py:34
  8.7 15.6 %collective-permute-start.3 = (bf16[4,32,1536]{2,1,0:T(8,128)(2,1)S(1)}, bf16[4,32,1536]{2,1,0:T(8,128)(2,1)S(1)}, u32[]{:S(2)}, u32[]{:S(2)}) collective-permute-start(bf16[4,32,1536]{2,1,0:T(8,128)(2,1)S(1)} %pad_maximum_fusion.6), channel_id=1, source_target_pairs={{0,6},{1,7},{2,0},{3,1},{4,2},{5,3},{6,4},{7,5},{8,14},{9,15},{10,... | collective-permute-start | bytes 1179656 | tf_op jit(solution)/shard_map/ppermute | solution.py:23
  11.3 16.8 %collective-permute-start.2 = (bf16[4,32,1536]{2,1,0:T(8,128)(2,1)S(1)}, bf16[4,32,1536]{2,1,0:T(8,128)(2,1)S(1)}, u32[]{:S(2)}, u32[]{:S(2)}) collective-permute-start(bf16[4,32,1536]{2,1,0:T(8,128)(2,1)S(1)} %pad_maximum_fusion.6), channel_id=1, source_target_pairs={{0,2},{1,3},{2,4},{3,5},{4,6},{5,7},{6,0},{7,1},{8,10},{9,11},{10,... | collective-permute-start | bytes 1179656 | tf_op jit(solution)/shard_map/ppermute | solution.py:23
  11.3 15.7 %collective-permute-start.1 = (bf16[4,32,1536]{2,1,0:T(8,128)(2,1)S(1)}, bf16[4,32,1536]{2,1,0:T(8,128)(2,1)S(1)}, u32[]{:S(2)}, u32[]{:S(2)}) collective-permute-start(bf16[4,32,1536]{2,1,0:T(8,128)(2,1)S(1)} %pad_maximum_fusion.6), channel_id=1, source_target_pairs={{0,1},{1,0},{2,3},{3,2},{4,5},{5,4},{6,7},{7,6},{8,9},{9,8},{10,11... | collective-permute-start | bytes 1179656 | tf_op jit(solution)/shard_map/ppermute | solution.py:23
  20.7 14.5 %collective-permute-start.10 = (bf16[4,32,1536]{2,1,0:T(8,128)(2,1)S(1)}, bf16[4,32,1536]{2,1,0:T(8,128)(2,1)S(1)}, u32[]{:S(2)}, u32[]{:S(2)}) collective-permute-start(bf16[4,32,1536]{2,1,0:T(8,128)(2,1)S(1)} %pad_maximum_fusion.6), channel_id=1, source_target_pairs={{0,4},{1,5},{2,6},{3,7},{4,0},{5,1},{6,2},{7,3},{8,12},{9,13},{10,... | collective-permute-start | bytes 1179656 | tf_op jit(solution)/shard_map/ppermute | solution.py:23
  23.4 11.8 %collective-permute-start.5 = (bf16[768,1024]{1,0:T(8,128)(2,1)S(1)}, bf16[768,1024]{1,0:T(8,128)(2,1)S(1)}, u32[]{:S(2)}, u32[]{:S(2)}) collective-permute-start(bf16[768,1024]{1,0:T(8,128)(2,1)S(1)} %bitcast.238), channel_id=1, source_target_pairs={{0,8},{8,0},{16,24},{24,16},{32,40},{40,32},{48,56},{56,48},{1,9},... | collective-permute-start | bytes 4718600 | tf_op jit(solution)/shard_map/ppermute | solution.py:15
  24.4 10.8 %collective-permute-start.13 = (f32[2,1024]{1,0:T(2,128)S(1)}, f32[2,1024]{1,0:T(2,128)S(1)}, u32[]{:S(2)}, u32[]{:S(2)}) collective-permute-start(f32[2,1024]{1,0:T(2,128)S(1)} %pad_maximum_fusion.23), channel_id=1, source_target_pairs={{0,64},{64,0},{1,65},{65,1},{2,66},{66,2},{3,67},{67,3},{4,68},{68... | collective-permute-start | bytes 24584 | tf_op jit(solution)/shard_map/ppermute | solution.py:29
  27.0 7.8 %collective-permute-start.18 = (bf16[4,32,1024]{2,1,0:T(8,128)(2,1)S(1)}, bf16[4,32,1024]{2,1,0:T(8,128)(2,1)S(1)}, u32[]{:S(2)}, u32[]{:S(2)}) collective-permute-start(bf16[4,32,1024]{2,1,0:T(8,128)(2,1)S(1)} %pad_maximum_fusion.13), channel_id=1, source_target_pairs={{0,1},{1,0},{2,3},{3,2},{4,5},{5,4},{6,7},{7,6},{64,65},{65,64},{6... | collective-permute-start | bytes 786440 | tf_op jit(solution)/shard_map/ppermute | solution.py:34
  28.1 13.4 %collective-permute-start.12 = (bf16[4,32,1536]{2,1,0:T(8,128)(2,1)S(1)}, bf16[4,32,1536]{2,1,0:T(8,128)(2,1)S(1)}, u32[]{:S(2)}, u32[]{:S(2)}) collective-permute-start(bf16[4,32,1536]{2,1,0:T(8,128)(2,1)S(1)} %collective-permute-done.1), channel_id=1, source_target_pairs={{0,6},{1,7},{2,0},{3,1},{4,2},{5,3},{6,4},{7,5},{8,14},{9,15},{10,... | collective-permute-start | bytes 1179656 | tf_op jit(solution)/shard_map/ppermute | solution.py:23
  34.8 10.8 %collective-permute-start.11 = (bf16[4,32,1536]{2,1,0:T(8,128)(2,1)S(1)}, bf16[4,32,1536]{2,1,0:T(8,128)(2,1)S(1)}, u32[]{:S(2)}, u32[]{:S(2)}) collective-permute-start(bf16[4,32,1536]{2,1,0:T(8,128)(2,1)S(1)} %collective-permute-done.1), channel_id=1, source_target_pairs={{0,2},{1,3},{2,4},{3,5},{4,6},{5,7},{6,0},{7,1},{8,10},{9,11},{10,... | collective-permute-start | bytes 1179656 | tf_op jit(solution)/shard_map/ppermute | solution.py:23
  35.2 10.3 %collective-permute-start.14 = (bf16[4,32,1536]{2,1,0:T(8,128)(2,1)S(1)}, bf16[4,32,1536]{2,1,0:T(8,128)(2,1)S(1)}, u32[]{:S(2)}, u32[]{:S(2)}) collective-permute-start(bf16[4,32,1536]{2,1,0:T(8,128)(2,1)S(1)} %collective-permute-done.10), channel_id=1, source_target_pairs={{0,1},{1,0},{2,3},{3,2},{4,5},{5,4},{6,7},{7,6},{8,9},{9,8},{10,11... | collective-permute-start | bytes 1179656 | tf_op jit(solution)/shard_map/ppermute | solution.py:23
  38.2 12.4 %collective-permute-start.8 = (bf16[128,1024]{1,0:T(8,128)(2,1)S(1)}, bf16[128,1024]{1,0:T(8,128)(2,1)S(1)}, u32[]{:S(2)}, u32[]{:S(2)}) collective-permute-start(bf16[128,1024]{1,0:T(8,128)(2,1)S(1)} %get-tuple-element.64), channel_id=1, source_target_pairs={{0,32},{8,40},{16,48},{24,56},{32,0},{40,8},{48,16},{56,24},{1,33}... | collective-permute-start | bytes 786440 | tf_op jit(solution)/shard_map/ppermute | solution.py:19
  41.2 11.7 %collective-permute-start.7 = (bf16[128,1024]{1,0:T(8,128)(2,1)S(1)}, bf16[128,1024]{1,0:T(8,128)(2,1)S(1)}, u32[]{:S(2)}, u32[]{:S(2)}) collective-permute-start(bf16[128,1024]{1,0:T(8,128)(2,1)S(1)} %get-tuple-element.65), channel_id=1, source_target_pairs={{0,16},{8,24},{16,32},{24,40},{32,48},{40,56},{48,0},{56,8},{1,17}... | collective-permute-start | bytes 786440 | tf_op jit(solution)/shard_map/ppermute | solution.py:19
  41.6 13.3 %collective-permute-start.6 = (bf16[128,1024]{1,0:T(8,128)(2,1)S(1)}, bf16[128,1024]{1,0:T(8,128)(2,1)S(1)}, u32[]{:S(2)}, u32[]{:S(2)}) collective-permute-start(bf16[128,1024]{1,0:T(8,128)(2,1)S(1)} %get-tuple-element.66), channel_id=1, source_target_pairs={{0,48},{8,56},{16,0},{24,8},{32,16},{40,24},{48,32},{56,40},{1,49}... | collective-permute-start | bytes 786440 | tf_op jit(solution)/shard_map/ppermute | solution.py:19
  48.0 12.2 %collective-permute-start.20 = (bf16[2,2,32,1024]{3,2,1,0:T(8,128)(2,1)S(1)}, bf16[2,2,32,1024]{3,2,1,0:T(8,128)(2,1)S(1)}, u32[]{:S(2)}, u32[]{:S(2)}) collective-permute-start(bf16[2,2,32,1024]{3,2,1,0:T(8,128)(2,1)S(1)} %pad_maximum_fusion.16), channel_id=1, source_target_pairs={{0,4},{1,5},{2,6},{3,7},{4,0},{5,1},{6,2},{7,3},{8,12},{9,13},{10,... | collective-permute-start | bytes 786440 | tf_op jit(solution)/shard_map/ppermute | solution.py:23
  50.6 11.8 %collective-permute-start.21 = (bf16[2,2,32,1024]{3,2,1,0:T(8,128)(2,1)S(1)}, bf16[2,2,32,1024]{3,2,1,0:T(8,128)(2,1)S(1)}, u32[]{:S(2)}, u32[]{:S(2)}) collective-permute-start(bf16[2,2,32,1024]{3,2,1,0:T(8,128)(2,1)S(1)} %pad_maximum_fusion.17), channel_id=1, source_target_pairs={{0,6},{1,7},{2,0},{3,1},{4,2},{5,3},{6,4},{7,5},{8,14},{9,15},{10,... | collective-permute-start | bytes 786440 | tf_op jit(solution)/shard_map/ppermute | solution.py:23
  52.8 9.5 %collective-permute-start.17 = (bf16[128,1024]{1,0:T(8,128)(2,1)S(1)}, bf16[128,1024]{1,0:T(8,128)(2,1)S(1)}, u32[]{:S(2)}, u32[]{:S(2)}) collective-permute-start(bf16[128,1024]{1,0:T(8,128)(2,1)S(1)} %get-tuple-element.60), channel_id=1, source_target_pairs={{0,32},{8,40},{16,48},{24,56},{32,0},{40,8},{48,16},{56,24},{1,33}... | collective-permute-start | bytes 786440 | tf_op jit(solution)/shard_map/ppermute | solution.py:19
  54.9 13.1 %collective-permute-start.16 = (bf16[128,1024]{1,0:T(8,128)(2,1)S(1)}, bf16[128,1024]{1,0:T(8,128)(2,1)S(1)}, u32[]{:S(2)}, u32[]{:S(2)}) collective-permute-start(bf16[128,1024]{1,0:T(8,128)(2,1)S(1)} %get-tuple-element.61), channel_id=1, source_target_pairs={{0,16},{8,24},{16,32},{24,40},{32,48},{40,56},{48,0},{56,8},{1,17}... | collective-permute-start | bytes 786440 | tf_op jit(solution)/shard_map/ppermute | solution.py:19
  55.3 12.7 %collective-permute-start.15 = (bf16[128,1024]{1,0:T(8,128)(2,1)S(1)}, bf16[128,1024]{1,0:T(8,128)(2,1)S(1)}, u32[]{:S(2)}, u32[]{:S(2)}) collective-permute-start(bf16[128,1024]{1,0:T(8,128)(2,1)S(1)} %get-tuple-element.62), channel_id=1, source_target_pairs={{0,48},{8,56},{16,0},{24,8},{32,16},{40,24},{48,32},{56,40},{1,49}... | collective-permute-start | bytes 786440 | tf_op jit(solution)/shard_map/ppermute | solution.py:19
  79.3 27.4 %collective-permute-start.33 = (bf16[8,32,1024]{2,1,0:T(8,128)(2,1)S(1)}, bf16[8,32,1024]{2,1,0:T(8,128)(2,1)S(1)}, u32[]{:S(2)}, u32[]{:S(2)}) collective-permute-start(bf16[8,32,1024]{2,1,0:T(8,128)(2,1)S(1)} %bitcast.209), channel_id=1, source_target_pairs={{0,48},{8,56},{16,0},{24,8},{32,16},{40,24},{48,32},{56,40},{1,49}... | collective-permute-start | bytes 1572872 | tf_op jit(solution)/shard_map/ppermute | solution.py:19
  79.4 30.1 %collective-permute-start.32 = (bf16[8,32,1024]{2,1,0:T(8,128)(2,1)S(1)}, bf16[8,32,1024]{2,1,0:T(8,128)(2,1)S(1)}, u32[]{:S(2)}, u32[]{:S(2)}) collective-permute-start(bf16[8,32,1024]{2,1,0:T(8,128)(2,1)S(1)} %bitcast.210), channel_id=1, source_target_pairs={{0,32},{8,40},{16,48},{24,56},{32,0},{40,8},{48,16},{56,24},{1,33}... | collective-permute-start | bytes 1572872 | tf_op jit(solution)/shard_map/ppermute | solution.py:19
  80.3 25.3 %collective-permute-start.31 = (bf16[8,32,1024]{2,1,0:T(8,128)(2,1)S(1)}, bf16[8,32,1024]{2,1,0:T(8,128)(2,1)S(1)}, u32[]{:S(2)}, u32[]{:S(2)}) collective-permute-start(bf16[8,32,1024]{2,1,0:T(8,128)(2,1)S(1)} %bitcast.211), channel_id=1, source_target_pairs={{0,16},{8,24},{16,32},{24,40},{32,48},{40,56},{48,0},{56,8},{1,17}... | collective-permute-start | bytes 1572872 | tf_op jit(solution)/shard_map/ppermute | solution.py:19
  88.8 19.0 %collective-permute-start.28 = (bf16[2,80,1024]{2,1,0:T(8,128)(2,1)S(1)}, bf16[2,80,1024]{2,1,0:T(8,128)(2,1)S(1)}, u32[]{:S(2)}, u32[]{:S(2)}) collective-permute-start(bf16[2,80,1024]{2,1,0:T(8,128)(2,1)S(1)} %get-tuple-element.50), channel_id=1, source_target_pairs={{0,4},{1,5},{2,6},{3,7},{4,0},{5,1},{6,2},{7,3},{8,12},{9,13},{10,... | collective-permute-start | bytes 983048 | tf_op jit(solution)/shard_map/ppermute | solution.py:23
  107.9 16.6 %collective-permute-start.30 = (bf16[4,40,1024]{2,1,0:T(8,128)(2,1)S(1)}, bf16[4,40,1024]{2,1,0:T(8,128)(2,1)S(1)}, u32[]{:S(2)}, u32[]{:S(2)}) collective-permute-start(bf16[4,40,1024]{2,1,0:T(8,128)(2,1)S(1)} %pad_maximum_fusion.10), channel_id=1, source_target_pairs={{0,65},{1,64},{2,67},{3,66},{4,69},{5,68},{6,71},{7,70},{64,1},{65... | collective-permute-start | bytes 983048 | tf_op jit(solution)/shard_map/ppermute | solution.py:34
  109.3 15.1 %collective-permute-start.29 = (bf16[4,40,1024]{2,1,0:T(8,128)(2,1)S(1)}, bf16[4,40,1024]{2,1,0:T(8,128)(2,1)S(1)}, u32[]{:S(2)}, u32[]{:S(2)}) collective-permute-start(bf16[4,40,1024]{2,1,0:T(8,128)(2,1)S(1)} %pad_maximum_fusion.9), channel_id=1, source_target_pairs={{0,64},{1,65},{2,66},{3,67},{4,68},{5,69},{6,70},{7,71},{64,0},{65... | collective-permute-start | bytes 983048 | tf_op jit(solution)/shard_map/ppermute | solution.py:34
  110.6 18.1 %collective-permute-start.34 = (bf16[4,32,1536]{2,1,0:T(8,128)(2,1)S(1)}, bf16[4,32,1536]{2,1,0:T(8,128)(2,1)S(1)}, u32[]{:S(2)}, u32[]{:S(2)}) collective-permute-start(bf16[4,32,1536]{2,1,0:T(8,128)(2,1)S(1)} %pad_maximum_fusion.7), channel_id=1, source_target_pairs={{0,1},{1,0},{2,3},{3,2},{4,5},{5,4},{6,7},{7,6},{8,9},{9,8},{10,11... | collective-permute-start | bytes 1179656 | tf_op jit(solution)/shard_map/ppermute | solution.py:23
  112.8 24.0 %collective-permute-start.36 = (bf16[2,4,32,1536]{3,2,1,0:T(8,128)(2,1)S(1)}, bf16[2,4,32,1536]{3,2,1,0:T(8,128)(2,1)S(1)}, u32[]{:S(2)}, u32[]{:S(2)}) collective-permute-start(bf16[2,4,32,1536]{3,2,1,0:T(8,128)(2,1)S(1)} %pad_maximum_fusion.4), channel_id=1, source_target_pairs={{0,6},{1,7},{2,0},{3,1},{4,2},{5,3},{6,4},{7,5},{8,14},{9,15},{10,... | collective-permute-start | bytes 2359304 | tf_op jit(solution)/shard_map/ppermute | solution.py:23
  113.1 23.9 %collective-permute-start.37 = (bf16[2,4,32,1536]{3,2,1,0:T(8,128)(2,1)S(1)}, bf16[2,4,32,1536]{3,2,1,0:T(8,128)(2,1)S(1)}, u32[]{:S(2)}, u32[]{:S(2)}) collective-permute-start(bf16[2,4,32,1536]{3,2,1,0:T(8,128)(2,1)S(1)} %pad_maximum_fusion.5), channel_id=1, source_target_pairs={{0,2},{1,3},{2,4},{3,5},{4,6},{5,7},{6,0},{7,1},{8,10},{9,11},{10,... | collective-permute-start | bytes 2359304 | tf_op jit(solution)/shard_map/ppermute | solution.py:23
  131.4 17.1 %collective-permute-start.35 = (bf16[4,32,1024]{2,1,0:T(8,128)(2,1)S(1)}, bf16[4,32,1024]{2,1,0:T(8,128)(2,1)S(1)}, u32[]{:S(2)}, u32[]{:S(2)}) collective-permute-start(bf16[4,32,1024]{2,1,0:T(8,128)(2,1)S(1)} %pad_maximum_fusion.19), channel_id=1, source_target_pairs={{0,1},{1,0},{2,3},{3,2},{4,5},{5,4},{6,7},{7,6},{64,65},{65,64},{6... | collective-permute-start | bytes 786440 | tf_op jit(solution)/shard_map/ppermute | solution.py:34
  132.7 10.5 %collective-permute-start.39 = (bf16[4,32,1536]{2,1,0:T(8,128)(2,1)S(1)}, bf16[4,32,1536]{2,1,0:T(8,128)(2,1)S(1)}, u32[]{:S(2)}, u32[]{:S(2)}) collective-permute-start(bf16[4,32,1536]{2,1,0:T(8,128)(2,1)S(1)} %add_convert_fusion.1), channel_id=1, source_target_pairs={{0,4},{1,5},{2,6},{3,7},{4,0},{5,1},{6,2},{7,3},{8,12},{9,13},{10,... | collective-permute-start | bytes 1179656 | tf_op jit(solution)/shard_map/ppermute | solution.py:23
  137.5 10.8 %collective-permute-start.40 = (bf16[4,32,1536]{2,1,0:T(8,128)(2,1)S(1)}, bf16[4,32,1536]{2,1,0:T(8,128)(2,1)S(1)}, u32[]{:S(2)}, u32[]{:S(2)}) collective-permute-start(bf16[4,32,1536]{2,1,0:T(8,128)(2,1)S(1)} %get-tuple-element.59), channel_id=1, source_target_pairs={{0,1},{1,0},{2,3},{3,2},{4,5},{5,4},{6,7},{7,6},{8,9},{9,8},{10,11... | collective-permute-start | bytes 1179656 | tf_op jit(solution)/shard_map/ppermute | solution.py:23
  (29 other events, 164.1 us)
